TPU v7x, 32 devices: a whole 2x2x4 slice. The times are simulated.
32 devices in a mesh: chaos: 8 (over y, x, core), slab: 4 (over z).
Axes of the slice: x: 2, y: 2, z: 4, core: 2. Of those that a mesh axis runs over, the one named last changes fastest.
Arguments:
- displacement: float32 [288, 3, 3072], P('chaos', None, 'slab'), may hold values from -1.5 to 1.5
- load: float32 [288, 3, 3072], P('chaos', None, 'slab'), may hold values from -12 to 12
- mean_modulus: float32 [3072], P('slab'), may hold values from 0.5 to 2
- modes: float32 [10, 3072], P(None, 'slab'), may hold values from -0.6 to 0.6
- owner: int32 [288], replicated, may hold values from 0 to 287, each once
Outputs:
- solution: float32 [288, 3, 3072], P('chaos', None, 'slab')
- residual: float32 [288, 3, 3072], P('chaos', None, 'slab')
Inputs may be any that keep to these rules, and one draw needn't show every extreme that they name: `owner`: each value appears exactly once. Slot s lies on device s // 36 of the chaos axis; values of 286 or more mark empty slots.
All inputs are finite; a program needn't handle non-finite values.
Results may differ from a plain program's by a relative error of at most 0.0003.
Values sent between devices are 32-bit elements; how exact they have to be, the bound alone decides.
No kernel may reach another device: no remote copies, remote signals or barrier semaphores. Data moves between devices by JAX's collectives and lax.ppermute only.
A program may use at most 128 MiB of HBM per device.

v0:
```python
import math

import jax
import jax.numpy as jnp
import numpy as np
from jax import lax
from jax.sharding import PartitionSpec as P

NX = 24
NY = 32
KL = 10
DEG = 3
SWEEPS = 4
ITERS = 2


bound_high = 50.0
bound_low = 2.5


def passed_along(value, axis, steps):
    count = lax.axis_size(axis)
    first, last = (max(0, -steps), min(count, count - steps))
    return lax.ppermute(value, axis, [(source, source + steps) for source in range(first, last)])


def extended_2(cells, sides, width):
    for axis, dim in sides:
        count = lax.axis_size(axis)
        ends = count - 1
        head = lax.slice_in_dim(cells, 0, width, axis=dim)
        tail = lax.slice_in_dim(cells, cells.shape[dim] - width, cells.shape[dim], axis=dim)
        cells = jnp.concatenate(
            [
                lax.ppermute(tail, axis, [(i, (i + 1) % count) for i in range(ends)]),
                cells,
                lax.ppermute(head, axis, [((i + 1) % count, i) for i in range(ends)]),
            ],
            axis=dim,
        )
    return cells


def multi_indices():
    listing = [[]]
    for variable in range(KL):
        extended_list = []
        for prefix in listing:
            for degree in range(DEG + 1 - sum(prefix)):
                extended_list.append(prefix + [degree])
        listing = extended_list
    return listing


def chaos_tables():
    listing = multi_indices()
    lookup = {tuple(multi_entry): number for number, multi_entry in enumerate(listing)}
    number_all = len(listing)
    up_index = np.full((number_all, KL), number_all, np.int32)
    up_weight = np.zeros((number_all, KL), np.float32)
    down_index = np.full((number_all, KL), number_all, np.int32)
    down_weight = np.zeros((number_all, KL), np.float32)
    for number, multi_entry in enumerate(listing):
        for variable in range(KL):
            raised = list(multi_entry)
            raised[variable] += 1
            if tuple(raised) in lookup:
                up_index[number, variable] = lookup[tuple(raised)]
                up_weight[number, variable] = math.sqrt(multi_entry[variable] + 1)
            if multi_entry[variable] > 0:
                lowered = list(multi_entry)
                lowered[variable] -= 1
                down_index[number, variable] = lookup[tuple(lowered)]
                down_weight[number, variable] = math.sqrt(multi_entry[variable])
    return (up_index, up_weight, down_index, down_weight)


def slot_neighbours(owner):
    up_index, up_weight, down_index, down_weight = chaos_tables()
    number_all = up_index.shape[0]
    live_slots = owner < number_all
    clipped = jnp.minimum(owner, number_all - 1)
    inverse = jnp.argsort(owner)

    def to_slots(index_table, weight_table):
        targets = jnp.asarray(index_table)[clipped]
        present = (targets < number_all) & live_slots[:, None]
        slots_of = inverse[jnp.minimum(targets, number_all - 1)]
        weights = jnp.where(present, jnp.asarray(weight_table)[clipped], 0.0)
        return (jnp.where(present, slots_of, 0), weights.astype(jnp.float32))

    return (to_slots(up_index, up_weight), to_slots(down_index, down_weight), live_slots)


def plane_masks(length):
    position = jnp.arange(length, dtype=jnp.int32)
    return (position // NY % NX, position % NY)


def forward_flat(values, step_size, keep):
    shifted = jnp.concatenate(
        [values[..., step_size:], jnp.zeros_like(values[..., :step_size])], axis=-1
    )
    return jnp.where(keep, shifted, 0.0) - values


def backward_flat(values, step_size, keep):
    shifted = jnp.concatenate(
        [jnp.zeros_like(values[..., :step_size]), values[..., :-step_size]], axis=-1
    )
    return values - jnp.where(keep, shifted, 0.0)


def stiffness_flat(fields, modulus):
    plane_size = NX * NY
    lowered = [field_one[..., :-plane_size] for field_one in fields]
    raised = [field_one[..., plane_size:] for field_one in fields]
    across_x, along_y = plane_masks(lowered[0].shape[-1])
    inner_x, inner_y = plane_masks(lowered[0].shape[-1] - plane_size)

    def slope_of(component, direction):
        if direction == 2:
            return raised[component] - lowered[component]
        if direction == 0:
            return forward_flat(lowered[component], NY, across_x != NX - 1)
        return forward_flat(lowered[component], 1, along_y != NY - 1)

    spread = slope_of(0, 0) + slope_of(1, 1) + slope_of(2, 2)
    results = []
    for component in range(3):
        summed = 0.0
        for direction in range(3):
            gradient = slope_of(component, direction)
            if direction == component:
                gradient = gradient + spread
            flux_term = modulus * gradient
            if direction == 2:
                summed = summed + (flux_term[..., plane_size:] - flux_term[..., :-plane_size])
            elif direction == 0:
                summed = summed + backward_flat(flux_term[..., plane_size:], NY, inner_x != 0)
            else:
                summed = summed + backward_flat(flux_term[..., plane_size:], 1, inner_y != 0)
        results.append(-summed)
    return results


def chebyshev(residual_in, apply_mean):
    center_value = 0.5 * (bound_high + bound_low)
    half_width = 0.5 * (bound_high - bound_low)
    ratio_value = center_value / half_width
    update = residual_in / center_value
    increment = update
    rho_prev = 1.0 / ratio_value
    for sweep_turn in range(SWEEPS):
        rho_next = 1.0 / (2.0 * ratio_value - rho_prev)
        increment = rho_next * rho_prev * increment + 2.0 * rho_next / half_width * (
            residual_in - apply_mean(update)
        )
        update = update + increment
        rho_prev = rho_next
    return update


def per_device(displacement, load, mean_modulus, modes, owner):
    plane_size = NX * NY
    slots_dev = displacement.shape[0]
    slots_all = owner.shape[0]
    (slot_up, weight_up), (slot_down, weight_down), live_slots = slot_neighbours(owner)
    own_start = lax.axis_index("chaos") * slots_dev
    live_own = lax.dynamic_slice_in_dim(live_slots, own_start, slots_dev, 0)
    keep_mask = live_own[:, None, None]
    solution = jnp.where(keep_mask, displacement, 0.0)
    target = jnp.where(keep_mask, load, 0.0)
    moduli = jnp.concatenate([mean_modulus[None], modes], axis=0)
    rim_below = passed_along(moduli, "slab", 1)
    moduli_ext = jnp.concatenate([rim_below, moduli], axis=1)
    mean_ext = moduli_ext[0]

    def operator_gathered(field_in):
        own_ids = own_start + jnp.arange(slots_dev, dtype=jnp.int32)
        up_own = lax.dynamic_slice_in_dim(slot_up, own_start, slots_dev, 0)
        down_own = lax.dynamic_slice_in_dim(slot_down, own_start, slots_dev, 0)
        up_weight_own = lax.dynamic_slice_in_dim(weight_up, own_start, slots_dev, 0)
        down_weight_own = lax.dynamic_slice_in_dim(weight_down, own_start, slots_dev, 0)
        columns = jnp.arange(slots_all, dtype=jnp.int32)
        identity_part = jnp.where(
            (own_ids[:, None] == columns[None, :]) & live_own[:, None], 1.0, 0.0
        )
        hits_up = jnp.where(
            up_own[:, :, None] == columns[None, None, :], up_weight_own[:, :, None], 0.0
        )
        hits_down = jnp.where(
            down_own[:, :, None] == columns[None, None, :], down_weight_own[:, :, None], 0.0
        )
        coupling = jnp.concatenate(
            [identity_part[None], jnp.transpose(hits_up + hits_down, (1, 0, 2))], axis=0
        )
        gathered = lax.all_gather(field_in, "chaos", axis=0, tiled=True)
        mixed_terms = jnp.einsum(
            "kij,jca->kcia", coupling, gathered, precision=lax.Precision.HIGHEST
        )
        extended = extended_2(mixed_terms, (("slab", 3),), plane_size)
        images = stiffness_flat(
            [extended[:, component] for component in range(3)], moduli_ext[:, None]
        )
        return jnp.stack([jnp.sum(image_one, axis=0) for image_one in images], axis=1)

    def apply_mean(field_in):
        extended = extended_2(field_in, (("slab", 2),), plane_size)
        return jnp.stack(
            stiffness_flat([extended[:, component] for component in range(3)], mean_ext), axis=1
        )

    residual = target
    for iteration in range(ITERS):
        image_now = operator_gathered(solution)
        residual = target - image_now
        solution = solution + chebyshev(residual, apply_mean)
    return (solution, residual)


def solution(mesh):
    in_specs = (P("chaos", None, "slab"), P("chaos", None, "slab"), P("slab"), P(None, "slab"), P())
    out_specs = (P("chaos", None, "slab"), P("chaos", None, "slab"))
    return jax.shard_map(
        per_device, mesh=mesh, in_specs=in_specs, out_specs=out_specs, check_vma=False
    )
```

profile of v0, /device:TPU:0, one launch (start us, length us, event | category | flops | bytes accessed | tf_op | source)
XLA Modules:
  0.0 548.0 jit_solution(756724415988174275)
XLA Ops:
  13.3 3.8 sort.17
  17.0 17.4 %gather_fusion.1 = s32[2880]{0:T(1024)S(1)} fusion(s32[288]{0:T(512)S(1)} %get-tuple-element.3, s32[3072]{0:T(1024)S(1)} %pad_clamp_fusion.1), kind=kCustom, calls=%fused_computation.1 | custom fusion | bytes 34560 | tf_op jit(solution)/shard_map/gather | solution.py:88
  34.8 17.4 %gather_fusion.4 = s32[2880]{0:T(1024)S(1)} fusion(s32[288]{0:T(512)S(1)} %get-tuple-element.3, s32[3072]{0:T(1024)S(1)} %pad_clamp_fusion), kind=kCustom, calls=%fused_computation.4 | custom fusion | bytes 34560 | tf_op jit(solution)/shard_map/gather | solution.py:88
  55.4 9.6 %fusion.8 = f32[11,3,36,768]{3,2,0,1:T(8,128)S(1)} fusion(f32[288,3,768,1]{2,1,0,3:T(4,128)} %bitcast.146, f32[10,36,288]{2,1,0:T(8,128)S(1)} %select_add_fusion, f32[1,36,288]{2,1,0:T(8,128)S(1)} %fusion.167), kind=kOutput, calls=%fused_computation.48 | convolution fusion | flops 3153313280 | bytes 6759936 | tf_op jit(solution)/shard_map/kij,jca->kcia/dot_general | solution.py:199
  65.0 5.2 collective-permute-start.1
  71.8 4.5 collective-permute-start
  76.4 81.4 %collective-permute-done = f32[11,768]{1,0:T(8,128)S(1)} collective-permute-done((f32[11,768]{1,0:T(8,128)S(1)}, f32[11,768]{1,0:T(8,128)S(1)}, u32[]{:S(2)}, u32[]{:S(2)}) %collective-permute-start) | collective-permute-done | bytes 33824 | tf_op jit(solution)/shard_map/ppermute | solution.py:24
  161.2 4.8 pad_maximum_fusion
  165.9 7.6 %slice_bitcast_fusion.5 = (f32[11,36,2304]{2,1,0:T(8,128)S(1)}, f32[11,36,2304]{2,1,0:T(8,128)S(1)}, f32[11,36,2304]{2,1,0:T(8,128)}) fusion(f32[11,3,36,2304]{3,2,0,1:T(8,128)} %pad_maximum_fusion), kind=kLoop, calls=%fused_computation.13 | loop fusion | bytes 21897216 | tf_op jit(solution)/shard_map/squeeze | solution.py:204
  188.2 14.8 %add_multiply_fusion.4 = (f32[11,36,1536]{2,1,0:T(8,128)}, f32[11,36,1536]{2,1,0:T(8,128)}, f32[11,36,1536]{2,1,0:T(8,128)}, f32[11,36,1536]{2,1,0:T(8,128)}, f3...) fusion(f32[11,1536]{1,0:T(8,128)S(1)} %maximum_maximum_fusion, ...), kind=kLoop, calls=%fused_computation.37 | loop fusion | flops 13989888 | bytes 43708272 | tf_op jit(solution)/shard_map/mul | solution.py:136
  211.9 4.5 fusion.30
  222.6 11.9 %collective-permute-start.4 = (f32[36,3,768]{2,0,1:T(8,128)S(1)}, f32[36,3,768]{2,0,1:T(8,128)S(1)}, u32[]{:S(2)}, u32[]{:S(2)}) collective-permute-start(f32[36,3,768]{2,0,1:T(8,128)S(1)} %get-tuple-element.30), channel_id=1, source_target_pairs={{1,0},{2,1},{3,2},{5,4},{6,5},{7,6},{9,8},{10,9},{11,10},{13,12},{... | collective-permute-start | bytes 995336 | tf_op jit(solution)/shard_map/ppermute | solution.py:37
  236.5 4.6 collective-permute-start.5
  242.4 4.8 collective-permute-done.5
  247.1 4.1 collective-permute-done.6
  261.7 4.4 collective-permute-done.8
  269.5 4.6 collective-permute-start.9
  283.4 34.3 %all-gather.5.cloned.1.call-done = f32[288,3,768]{2,1,0:T(4,128)} async-done(((f32[36,3,768]{2,1,0:T(4,128)}), f32[288,3,768]{2,1,0:T(4,128)}) %all-gather.5.cloned.1.call-update) | async-done | bytes 2654224 | tf_op jit(solution)/shard_map/all_gather | solution.py:198
  317.7 9.4 %fusion.11 = f32[11,3,36,768]{3,2,0,1:T(8,128)S(1)} fusion(f32[288,3,768,1]{2,1,0,3:T(4,128)} %bitcast.147, f32[10,36,288]{2,1,0:T(8,128)S(1)} %copy-done.25, f32[1,36,288]{2,1,0:T(8,128)S(1)} %fusion.167), kind=kOutput, calls=%fused_computation.49 | convolution fusion | flops 3153313280 | bytes 6759936 | tf_op jit(solution)/shard_map/kij,jca->kcia/dot_general | solution.py:199
  332.2 85.5 %collective-permute-done.11 = f32[11,3,36,768]{3,2,0,1:T(8,128)S(1)} collective-permute-done((f32[11,3,36,768]{3,2,0,1:T(8,128)S(1)}, f32[11,3,36,768]{3,2,0,1:T(8,128)S(1)}, u32[]{:S(2)}, u32[]{:S(2)}) %collective-permute-start.11) | collective-permute-done | bytes 3649568 | tf_op jit(solution)/shard_map/ppermute | solution.py:35
  417.7 4.4 collective-permute-done.12
  422.0 4.7 pad_maximum_fusion.1
  426.8 7.5 %slice_bitcast_fusion.2 = (f32[11,36,2304]{2,1,0:T(8,128)S(1)}, f32[11,36,2304]{2,1,0:T(8,128)S(1)}, f32[11,36,2304]{2,1,0:T(8,128)}) fusion(f32[11,3,36,2304]{3,2,0,1:T(8,128)} %pad_maximum_fusion.1), kind=kLoop, calls=%fused_computation.10 | loop fusion | bytes 21897216 | tf_op jit(solution)/shard_map/squeeze | solution.py:204
  448.8 15.0 %add_multiply_fusion.1 = (f32[11,36,1536]{2,1,0:T(8,128)}, f32[11,36,1536]{2,1,0:T(8,128)}, f32[11,36,1536]{2,1,0:T(8,128)}, f32[11,36,1536]{2,1,0:T(8,128)}, f3...) fusion(f32[11,1536]{1,0:T(8,128)S(1)} %maximum_maximum_fusion, ...), kind=kLoop, calls=%fused_computation.27 | loop fusion | flops 13989888 | bytes 43708272 | tf_op jit(solution)/shard_map/mul | solution.py:136
  472.7 4.5 fusion.21
  484.6 5.8 %collective-permute-done.13 = f32[36,3,768]{2,0,1:T(8,128)S(1)} collective-permute-done((f32[36,3,768]{2,0,1:T(8,128)S(1)}, f32[36,3,768]{2,0,1:T(8,128)S(1)}, u32[]{:S(2)}, u32[]{:S(2)}) %collective-permute-start.13) | collective-permute-done | bytes 331808 | tf_op jit(solution)/shard_map/ppermute | solution.py:35
  490.4 4.1 collective-permute-done.14
  501.4 4.3 collective-permute-done.15
  505.8 4.1 collective-permute-done.16
  519.4 4.4 collective-permute-done.18
  529.4 3.7 collective-permute-done.19
  533.1 4.4 collective-permute-done.20
  (311 shorter events, 130.4 us)
Async XLA Ops:
  7.2 4.8 copy-start.16
  7.2 6.1 %copy-start.27 = (s32[288]{0:T(512)S(1)}, s32[288]{0:T(512)}, u32[]{:S(2)}) copy-start(s32[288]{0:T(512)} %param.13) | copy-start | bytes 3460
  7.2 48.2 %all-gather.3.cloned.1.call-start = ((), (), s32[]{:S(2)}) async-start(), calls=%async_computation | async-start | bytes 3981312 | tf_op jit(solution)/shard_map/all_gather | solution.py:198
  10.2 307.5 %all-gather.5.cloned.1.call-start = ((), (), s32[]{:S(2)}) async-start(), calls=%async_computation.1 | async-start | bytes 3981312 | tf_op jit(solution)/shard_map/all_gather | solution.py:198
  34.8 17.9 %copy-start.15 = (f32[286,10]{1,0:T(8,128)S(1)}, f32[286,10]{1,0:T(8,128)}, u32[]{:S(2)}) copy-start(f32[286,10]{1,0:T(8,128)} %constant.269.clone) | copy-start | bytes 34324
  55.4 9.7 %copy-start.24 = (f32[10,36,288]{2,1,0:T(8,128)}, f32[10,36,288]{2,1,0:T(8,128)S(1)}, u32[]{:S(2)}) copy-start(f32[10,36,288]{2,1,0:T(8,128)S(1)} %select_add_fusion) | copy-start | bytes 1244164
  55.4 16.4 %copy-start.28 = (f32[768]{0:T(1024)S(1)}, f32[768]{0:T(1024)}, u32[]{:S(2)}) copy-start(f32[768]{0:T(1024)} %param.11) | copy-start | bytes 9220
  55.4 16.4 %copy-start.26 = (f32[10,768]{1,0:T(8,128)S(1)}, f32[10,768]{1,0:T(8,128)}, u32[]{:S(2)}) copy-start(f32[10,768]{1,0:T(8,128)} %param.12) | copy-start | bytes 92164
  65.0 92.8 %collective-permute-start.1 = (f32[11,3,36,768]{3,2,0,1:T(8,128)S(1)}, f32[11,3,36,768]{3,2,0,1:T(8,128)S(1)}, u32[]{:S(2)}, u32[]{:S(2)}) collective-permute-start(f32[11,3,36,768]{3,2,0,1:T(8,128)S(1)} %fusion.8), channel_id=1, source_target_pairs={{0,1},{1,2},{2,3},{4,5},{5,6},{6,7},{8,9},{9,10},{10,11},{12,13},{... | collective-permute-start | bytes 10948616 | tf_op jit(solution)/shard_map/ppermute | solution.py:35
  70.2 90.9 %collective-permute-start.2 = (f32[11,3,36,768]{3,2,0,1:T(8,128)S(1)}, f32[11,3,36,768]{3,2,0,1:T(8,128)S(1)}, u32[]{:S(2)}, u32[]{:S(2)}) collective-permute-start(f32[11,3,36,768]{3,2,0,1:T(8,128)S(1)} %fusion.8), channel_id=1, source_target_pairs={{1,0},{2,1},{3,2},{5,4},{6,5},{7,6},{9,8},{10,9},{11,10},{13,12},{... | collective-permute-start | bytes 10948616 | tf_op jit(solution)/shard_map/ppermute | solution.py:37
  71.8 86.0 %collective-permute-start = (f32[11,768]{1,0:T(8,128)S(1)}, f32[11,768]{1,0:T(8,128)S(1)}, u32[]{:S(2)}, u32[]{:S(2)}) collective-permute-start(f32[11,768]{1,0:T(8,128)S(1)} %pad_maximum_fusion.10), channel_id=1, source_target_pairs={{0,1},{1,2},{2,3},{4,5},{5,6},{6,7},{8,9},{9,10},{10,11},{12,13},{... | collective-permute-start | bytes 101384 | tf_op jit(solution)/shard_map/ppermute | solution.py:24
  219.3 15.2 %collective-permute-start.3 = (f32[36,3,768]{2,0,1:T(8,128)S(1)}, f32[36,3,768]{2,0,1:T(8,128)S(1)}, u32[]{:S(2)}, u32[]{:S(2)}) collective-permute-start(f32[36,3,768]{2,0,1:T(8,128)S(1)} %get-tuple-element.30), channel_id=1, source_target_pairs={{0,1},{1,2},{2,3},{4,5},{5,6},{6,7},{8,9},{9,10},{10,11},{12,13},{... | collective-permute-start | bytes 995336 | tf_op jit(solution)/shard_map/ppermute | solution.py:35
  222.6 12.0 %collective-permute-start.4 = (f32[36,3,768]{2,0,1:T(8,128)S(1)}, f32[36,3,768]{2,0,1:T(8,128)S(1)}, u32[]{:S(2)}, u32[]{:S(2)}) collective-permute-start(f32[36,3,768]{2,0,1:T(8,128)S(1)} %get-tuple-element.30), channel_id=1, source_target_pairs={{1,0},{2,1},{3,2},{5,4},{6,5},{7,6},{9,8},{10,9},{11,10},{13,12},{... | collective-permute-start | bytes 995336 | tf_op jit(solution)/shard_map/ppermute | solution.py:37
  236.5 10.6 %collective-permute-start.5 = (f32[36,3,768]{2,0,1:T(8,128)S(1)}, f32[36,3,768]{2,0,1:T(8,128)S(1)}, u32[]{:S(2)}, u32[]{:S(2)}) collective-permute-start(f32[36,3,768]{2,0,1:T(8,128)S(1)} %fusion.69), channel_id=1, source_target_pairs={{0,1},{1,2},{2,3},{4,5},{5,6},{6,7},{8,9},{9,10},{10,11},{12,13},{... | collective-permute-start | bytes 995336 | tf_op jit(solution)/shard_map/ppermute | solution.py:35
  241.1 10.2 %collective-permute-start.6 = (f32[36,3,768]{2,0,1:T(8,128)S(1)}, f32[36,3,768]{2,0,1:T(8,128)S(1)}, u32[]{:S(2)}, u32[]{:S(2)}) collective-permute-start(f32[36,3,768]{2,0,1:T(8,128)S(1)} %fusion.69), channel_id=1, source_target_pairs={{1,0},{2,1},{3,2},{5,4},{6,5},{7,6},{9,8},{10,9},{11,10},{13,12},{... | collective-permute-start | bytes 995336 | tf_op jit(solution)/shard_map/ppermute | solution.py:37
  253.3 8.5 %collective-permute-start.7 = (f32[36,3,768]{2,0,1:T(8,128)S(1)}, f32[36,3,768]{2,0,1:T(8,128)S(1)}, u32[]{:S(2)}, u32[]{:S(2)}) collective-permute-start(f32[36,3,768]{2,0,1:T(8,128)S(1)} %fusion.203), channel_id=1, source_target_pairs={{0,1},{1,2},{2,3},{4,5},{5,6},{6,7},{8,9},{9,10},{10,11},{12,13},{... | collective-permute-start | bytes 995336 | tf_op jit(solution)/shard_map/ppermute | solution.py:35
  256.7 9.4 %collective-permute-start.8 = (f32[36,3,768]{2,0,1:T(8,128)S(1)}, f32[36,3,768]{2,0,1:T(8,128)S(1)}, u32[]{:S(2)}, u32[]{:S(2)}) collective-permute-start(f32[36,3,768]{2,0,1:T(8,128)S(1)} %fusion.203), channel_id=1, source_target_pairs={{1,0},{2,1},{3,2},{5,4},{6,5},{7,6},{9,8},{10,9},{11,10},{13,12},{... | collective-permute-start | bytes 995336 | tf_op jit(solution)/shard_map/ppermute | solution.py:37
  268.2 9.4 %collective-permute-start.10 = (f32[36,3,768]{2,0,1:T(8,128)S(1)}, f32[36,3,768]{2,0,1:T(8,128)S(1)}, u32[]{:S(2)}, u32[]{:S(2)}) collective-permute-start(f32[36,3,768]{2,0,1:T(8,128)S(1)} %fusion.201), channel_id=1, source_target_pairs={{1,0},{2,1},{3,2},{5,4},{6,5},{7,6},{9,8},{10,9},{11,10},{13,12},{... | collective-permute-start | bytes 995336 | tf_op jit(solution)/shard_map/ppermute | solution.py:37
  269.5 9.6 %collective-permute-start.9 = (f32[36,3,768]{2,0,1:T(8,128)S(1)}, f32[36,3,768]{2,0,1:T(8,128)S(1)}, u32[]{:S(2)}, u32[]{:S(2)}) collective-permute-start(f32[36,3,768]{2,0,1:T(8,128)S(1)} %fusion.201), channel_id=1, source_target_pairs={{0,1},{1,2},{2,3},{4,5},{5,6},{6,7},{8,9},{9,10},{10,11},{12,13},{... | collective-permute-start | bytes 995336 | tf_op jit(solution)/shard_map/ppermute | solution.py:35
  280.7 36.9 %copy-start.25 = (f32[10,36,288]{2,1,0:T(8,128)S(1)}, f32[10,36,288]{2,1,0:T(8,128)}, u32[]{:S(2)}) copy-start(f32[10,36,288]{2,1,0:T(8,128)} %copy-done.24) | copy-start | bytes 1244164
  327.0 90.6 %collective-permute-start.11 = (f32[11,3,36,768]{3,2,0,1:T(8,128)S(1)}, f32[11,3,36,768]{3,2,0,1:T(8,128)S(1)}, u32[]{:S(2)}, u32[]{:S(2)}) collective-permute-start(f32[11,3,36,768]{3,2,0,1:T(8,128)S(1)} %fusion.11), channel_id=1, source_target_pairs={{0,1},{1,2},{2,3},{4,5},{5,6},{6,7},{8,9},{9,10},{10,11},{12,13},{... | collective-permute-start | bytes 10948616 | tf_op jit(solution)/shard_map/ppermute | solution.py:35
  330.7 91.4 %collective-permute-start.12 = (f32[11,3,36,768]{3,2,0,1:T(8,128)S(1)}, f32[11,3,36,768]{3,2,0,1:T(8,128)S(1)}, u32[]{:S(2)}, u32[]{:S(2)}) collective-permute-start(f32[11,3,36,768]{3,2,0,1:T(8,128)S(1)} %fusion.11), channel_id=1, source_target_pairs={{1,0},{2,1},{3,2},{5,4},{6,5},{7,6},{9,8},{10,9},{11,10},{13,12},{... | collective-permute-start | bytes 10948616 | tf_op jit(solution)/shard_map/ppermute | solution.py:37
  472.7 4.5 copy-start.6
  480.1 59.2 %copy-start.18 = (f32[36,3,768]{2,0,1:T(8,128)}, f32[36,3,768]{2,0,1:T(8,128)S(1)}, u32[]{:S(2)}) copy-start(f32[36,3,768]{2,0,1:T(8,128)S(1)} %get-tuple-element.19) | copy-start | bytes 995332
  480.2 10.3 %collective-permute-start.13 = (f32[36,3,768]{2,0,1:T(8,128)S(1)}, f32[36,3,768]{2,0,1:T(8,128)S(1)}, u32[]{:S(2)}, u32[]{:S(2)}) collective-permute-start(f32[36,3,768]{2,0,1:T(8,128)S(1)} %get-tuple-element.18), channel_id=1, source_target_pairs={{0,1},{1,2},{2,3},{4,5},{5,6},{6,7},{8,9},{9,10},{10,11},{12,13},{... | collective-permute-start | bytes 995336 | tf_op jit(solution)/shard_map/ppermute | solution.py:35
  483.3 11.2 %collective-permute-start.14 = (f32[36,3,768]{2,0,1:T(8,128)S(1)}, f32[36,3,768]{2,0,1:T(8,128)S(1)}, u32[]{:S(2)}, u32[]{:S(2)}) collective-permute-start(f32[36,3,768]{2,0,1:T(8,128)S(1)} %get-tuple-element.18), channel_id=1, source_target_pairs={{1,0},{2,1},{3,2},{5,4},{6,5},{7,6},{9,8},{10,9},{11,10},{13,12},{... | collective-permute-start | bytes 995336 | tf_op jit(solution)/shard_map/ppermute | solution.py:37
  496.5 9.3 %collective-permute-start.15 = (f32[36,3,768]{2,0,1:T(8,128)S(1)}, f32[36,3,768]{2,0,1:T(8,128)S(1)}, u32[]{:S(2)}, u32[]{:S(2)}) collective-permute-start(f32[36,3,768]{2,0,1:T(8,128)S(1)} %fusion.68), channel_id=1, source_target_pairs={{0,1},{1,2},{2,3},{4,5},{5,6},{6,7},{8,9},{9,10},{10,11},{12,13},{... | collective-permute-start | bytes 995336 | tf_op jit(solution)/shard_map/ppermute | solution.py:35
  499.9 10.0 %collective-permute-start.16 = (f32[36,3,768]{2,0,1:T(8,128)S(1)}, f32[36,3,768]{2,0,1:T(8,128)S(1)}, u32[]{:S(2)}, u32[]{:S(2)}) collective-permute-start(f32[36,3,768]{2,0,1:T(8,128)S(1)} %fusion.68), channel_id=1, source_target_pairs={{1,0},{2,1},{3,2},{5,4},{6,5},{7,6},{9,8},{10,9},{11,10},{13,12},{... | collective-permute-start | bytes 995336 | tf_op jit(solution)/shard_map/ppermute | solution.py:37
  511.9 7.5 %collective-permute-start.17 = (f32[36,3,768]{2,0,1:T(8,128)S(1)}, f32[36,3,768]{2,0,1:T(8,128)S(1)}, u32[]{:S(2)}, u32[]{:S(2)}) collective-permute-start(f32[36,3,768]{2,0,1:T(8,128)S(1)} %fusion.202), channel_id=1, source_target_pairs={{0,1},{1,2},{2,3},{4,5},{5,6},{6,7},{8,9},{9,10},{10,11},{12,13},{... | collective-permute-start | bytes 995336 | tf_op jit(solution)/shard_map/ppermute | solution.py:35
  514.4 9.4 %collective-permute-start.18 = (f32[36,3,768]{2,0,1:T(8,128)S(1)}, f32[36,3,768]{2,0,1:T(8,128)S(1)}, u32[]{:S(2)}, u32[]{:S(2)}) collective-permute-start(f32[36,3,768]{2,0,1:T(8,128)S(1)} %fusion.202), channel_id=1, source_target_pairs={{1,0},{2,1},{3,2},{5,4},{6,5},{7,6},{9,8},{10,9},{11,10},{13,12},{... | collective-permute-start | bytes 995336 | tf_op jit(solution)/shard_map/ppermute | solution.py:37
  525.9 7.2 %collective-permute-start.19 = (f32[36,3,768]{2,0,1:T(8,128)S(1)}, f32[36,3,768]{2,0,1:T(8,128)S(1)}, u32[]{:S(2)}, u32[]{:S(2)}) collective-permute-start(f32[36,3,768]{2,0,1:T(8,128)S(1)} %fusion.200), channel_id=1, source_target_pairs={{0,1},{1,2},{2,3},{4,5},{5,6},{6,7},{8,9},{9,10},{10,11},{12,13},{... | collective-permute-start | bytes 995336 | tf_op jit(solution)/shard_map/ppermute | solution.py:35
  528.1 9.4 %collective-permute-start.20 = (f32[36,3,768]{2,0,1:T(8,128)S(1)}, f32[36,3,768]{2,0,1:T(8,128)S(1)}, u32[]{:S(2)}, u32[]{:S(2)}) collective-permute-start(f32[36,3,768]{2,0,1:T(8,128)S(1)} %fusion.200), channel_id=1, source_target_pairs={{1,0},{2,1},{3,2},{5,4},{6,5},{7,6},{9,8},{10,9},{11,10},{13,12},{... | collective-permute-start | bytes 995336 | tf_op jit(solution)/shard_map/ppermute | solution.py:37
  (20 other events, 43.7 us)
Sparse Core Ops, SparseCore 0:
  10.3 36.6 all-gather.2
  283.5 34.0 all-gather.4
where the time goes:
time: 557 us; the launch traced here: 548 us
  waiting for transfers between devices  265 us (48%)
  local copies, waits for them, and re-layouts  110 us (20%)
  other arithmetic  72.9 us (13%)
  starting transfers between devices  64.8 us (12%)
  matrix products  19 us (3%)
  between operations  16.3 us (3%)
    ppermute x10, waiting for transfers between devices, extended_2(): lax.ppermute(tail, axis, [(i, (i + 1) % count) for i in range(ends)])  113 us
    ppermute x1, waiting for transfers between devices, passed_along(): lax.ppermute(value, axis, [(source, source + steps) for source in range(f...  81.4 us
    mul x20, other arithmetic, stiffness_flat(): flux_term = modulus * gradient  39.9 us
    ppermute x10, waiting for transfers between devices, extended_2(): lax.ppermute(head, axis, [((i + 1) % count, i) for i in range(ends)])  36.8 us
    ppermute x10, starting transfers between devices, extended_2(): lax.ppermute(tail, axis, [(i, (i + 1) % count) for i in range(ends)])  35.9 us
    gather x4, local copies, waits for them, and re-layouts, to_slots(): slots_of = inverse[jnp.minimum(targets, number_all - 1)]  35 us
    all_gather x2, waiting for transfers between devices, operator_gathered(): gathered = lax.all_gather(field_in, 'chaos', axis=0, tiled=True)  34.3 us
    slice x60, local copies, waits for them, and re-layouts, forward_flat(): values[..., step_size:]  33.5 us
  transfers between devices with their start and end apart: 23, of which 19 were waited for; matrix products, arithmetic and copies ran while one was open for 8% of the time, Pallas kernels for 0%

commit v1 on v0

v1 whole, which is shorter than its diff:
```python
import functools
import math

import jax
import jax.numpy as jnp
import numpy as np
from jax import lax
from jax.experimental import pallas as pl
from jax.experimental.pallas import tpu as pltpu
from jax.sharding import PartitionSpec as P

NX = 24
NY = 32
KL = 10
DEG = 3
SWEEPS = 4
PLANE = NX * NY
FIELDS = KL + 1

bound_high = 50.0
bound_low = 2.5
VMEM_LIMIT = 60 * 1024 * 1024
F32 = jnp.float32
BF16 = jnp.bfloat16


def up8(count):
    return -(-count // 8) * 8


def multi_indices():
    listing = [[]]
    for variable in range(KL):
        extended_list = []
        for prefix in listing:
            for degree in range(DEG + 1 - sum(prefix)):
                extended_list.append(prefix + [degree])
        listing = extended_list
    return listing


def edge_tables():
    listing = multi_indices()
    lookup = {tuple(entry): number for number, entry in enumerate(listing)}
    low, raised, level = [], [], []
    for number, entry in enumerate(listing):
        if sum(entry) == DEG:
            continue
        low.append(number)
        for variable in range(KL):
            other = list(entry)
            other[variable] += 1
            raised.append(lookup[tuple(other)])
            level.append(entry[variable])
    return len(listing), np.array(low, np.int32), np.array(raised, np.int32), np.array(level, np.int32)


class Plan:
    def __init__(self, chaos, slab, slots_dev):
        self.chaos, self.slab, self.slots_dev = chaos, slab, slots_dev
        self.n = chaos * slab
        self.nz = slab
        self.sp = -(-slots_dev // slab)
        self.hs = up8(self.sp)
        self.ls = self.nz * NY
        best = None
        for tx in range(1, 7):
            for ty in range(1, NY + 1):
                if NX % tx or NY % ty or (NX // tx) * (NY // ty) > self.n:
                    continue
                lanes = -(-3 * self.nz * (ty + 2) // 128) * 128
                rows = up8((self.sp - 1) * (tx + 2) + 8)
                key = (-(NX // tx) * (NY // ty), rows * lanes)
                if best is None or key < best[0]:
                    best = (key, tx, ty, lanes, rows)
        _, self.tx, self.ty, self.lanes, self.rows_in = best
        self.rx = self.tx + 2
        self.ry = self.ty + 2
        self.nxb, self.nyb = NX // self.tx, NY // self.ty
        self.rows_out = up8(self.sp * self.tx)
        self.rows_start = up8(6 * self.sp + 16)
        self.rows_end = up8(6 * self.sp)
        self.positions = self.n * self.sp

    def pack_table(self):
        table = np.zeros((3 * self.ls, self.nyb * self.lanes), np.float32)
        for c in range(3):
            for z in range(self.nz):
                for yb in range(self.nyb):
                    for k in range(self.ry):
                        y = yb * self.ty - 1 + k
                        if 0 <= y < NY:
                            table[
                                c * self.ls + z * NY + y,
                                yb * self.lanes + (c * self.nz + z) * self.ry + k,
                            ] = 1
        return table

    def unpack_table(self):
        table = np.zeros((self.nyb * self.lanes, 3 * self.ls), np.float32)
        for c in range(3):
            for z in range(self.nz):
                for y in range(NY):
                    yb, k = y // self.ty, y % self.ty + 1
                    table[
                        yb * self.lanes + (c * self.nz + z) * self.ry + k, c * self.ls + z * NY + y
                    ] = 1
        return table

    def modulus_table(self):
        table = np.zeros((self.nyb, self.ls, self.lanes), np.float32)
        for yb in range(self.nyb):
            for z in range(self.nz):
                for k in range(self.ry):
                    y = yb * self.ty - 1 + k
                    if 0 <= y < NY:
                        for c in range(3):
                            table[yb, z * NY + y, (c * self.nz + z) * self.ry + k] = 1
        return table


def picked(values, table):
    high = values.astype(BF16)
    rest = values - high.astype(F32)
    middle = rest.astype(BF16)
    low = (rest - middle.astype(F32)).astype(BF16)
    return (
        jnp.dot(high, table, preferred_element_type=F32)
        + jnp.dot(middle, table, preferred_element_type=F32)
        + jnp.dot(low, table, preferred_element_type=F32)
    )


def pick_into(out_ref, values_ref, table_ref):
    width = table_ref.shape[1]
    chunk = width if width <= 1024 else 512
    for first in range(0, width, chunk):
        out_ref[:, first : first + chunk] = picked(values_ref[...], table_ref[:, first : first + chunk])


def swap_quarters(parts):
    quarter = lax.broadcasted_iota(jnp.int32, parts[0].shape, 1) // NY
    swapped = []
    for j in range(4):
        total = parts[j]
        for i in range(4):
            if i != j:
                turned = pltpu.roll(parts[i], (i - j) % 4 * NY, 1)
                total = jnp.where(quarter == i, turned, total)
        swapped.append(total)
    return swapped


def strided(start, size, step):
    return pl.ds(start, size) if size == 1 or step == 1 else pl.ds(start, size, stride=step)


def store_message(plan, rows_ref, msg_ref):
    blank = jnp.zeros((8, plan.lanes), F32)
    for tile in range(plan.n):
        if tile >= plan.nxb * plan.nyb:
            msg_ref[tile] = jnp.zeros((plan.rows_in, plan.lanes), F32)
            continue
        xb, yb = divmod(tile, plan.nyb)
        msg_ref[tile, plan.rows_in - 8 :, :] = blank
        for k in range(plan.rx):
            x = xb * plan.tx - 1 + k
            if 0 <= x < NX:
                rows = rows_ref[
                    x * plan.hs : x * plan.hs + plan.sp, yb * plan.lanes : (yb + 1) * plan.lanes
                ]
            else:
                rows = jnp.zeros((plan.sp, plan.lanes), F32)
            msg_ref[tile, strided(k, plan.sp, plan.rx), :] = rows


def start_kernel(plan, tile_ref, in_ref, pack_ref, mtab_ref, msg_ref, load_ref, mean_ref, mods_ref, lhs, rows, fields):
    fields[0] = jnp.zeros((16, plan.ls), F32)
    fields[NX + 1] = jnp.zeros((16, plan.ls), F32)

    def slabs_of(first, count, a):
        out = [[] for _ in range(4)]
        for t in range(plan.nz // 4):
            parts = [in_ref[4 * t + i, first : first + count, a * 128 : (a + 1) * 128] for i in range(4)]
            for b, piece in enumerate(swap_quarters(parts)):
                out[b].append(piece)
        return [piece[0] if len(piece) == 1 else jnp.concatenate(piece, axis=1) for piece in out]

    for a in range(PLANE // 128):
        for c in range(3):
            for b, piece in enumerate(slabs_of(c * plan.sp, plan.hs, a)):
                x = 4 * a + b
                lhs[x * plan.hs : (x + 1) * plan.hs, c * plan.ls : (c + 1) * plan.ls] = piece
            for b, piece in enumerate(slabs_of((3 + c) * plan.sp, plan.hs, a)):
                load_ref[4 * a + b, c] = piece
        for b, piece in enumerate(slabs_of(6 * plan.sp, 16, a)):
            fields[4 * a + b + 1] = piece
            mean_ref[4 * a + b : 4 * a + b + 1, :] = piece[0:1]
    pick_into(rows, lhs, pack_ref)
    store_message(plan, rows, msg_ref)
    tile = jnp.minimum(tile_ref[0], plan.nxb * plan.nyb - 1)
    xb, yb = tile // plan.nyb, tile % plan.nyb
    table = mtab_ref[yb]
    mods_ref[...] = jnp.zeros(mods_ref.shape, F32)
    for k in range(plan.rx):
        here = picked(fields[xb * plan.tx + k], table)
        for v in range(FIELDS):
            mods_ref[v, k : k + 1, :] = here[v : v + 1]


def mix_kernel(plan, low_count, nodes_ref, level_ref, msg_ref, mods_ref, out_ref, grad, flux, scaled):
    sp, rx, ry, nz, lanes = plan.sp, plan.rx, plan.ry, plan.nz, plan.lanes
    segment = nz * ry
    lane = lax.broadcasted_iota(jnp.int32, (8, lanes), 1)
    part, height = lane // segment, lane % segment // ry
    not_top, not_bottom = height != nz - 1, height != 0
    is_x, is_y, is_z = part == 0, part == 1, part == 2
    for level in range(DEG):
        for v in range(KL):
            scaled[level * KL + v] = mods_ref[v + 1] * math.sqrt(level + 1)
    mean = mods_ref[0]

    def gradients(source, carry):
        for s in range(sp):
            own = msg_ref[source, s * rx : s * rx + 8, :]
            slope_x = pltpu.roll(own, 7, 0) - own
            slope_y = pltpu.roll(own, lanes - 1, 1) - own
            slope_z = jnp.where(not_top, pltpu.roll(own, lanes - ry, 1), 0.0) - own
            spread = slope_x + pltpu.roll(slope_y, lanes - segment, 1) + pltpu.roll(slope_z, lanes - 2 * segment, 1)
            full_x = slope_x + jnp.where(is_x, spread, 0.0)
            full_y = slope_y + jnp.where(is_y, pltpu.roll(spread, segment, 1), 0.0)
            full_z = slope_z + jnp.where(is_z, pltpu.roll(spread, 2 * segment, 1), 0.0)
            at = source * sp + s
            for d, full in enumerate((full_x, full_y, full_z)):
                grad[at, d] = full
                flux[at, d] = mean * full
        return carry

    lax.fori_loop(0, plan.n, gradients, 0)

    def edges(number, carry):
        base = nodes_ref[number]
        own = [grad[base, d] for d in range(3)]
        total = [flux[base, d] for d in range(3)]
        for group in range(0, KL, 5):
            at = [nodes_ref[low_count + number * KL + v] for v in range(group, group + 5)]
            field = [scaled[level_ref[number * KL + v] * KL + v] for v in range(group, group + 5)]
            fresh = [
                [flux[spot, d] + weight * own[d] for d in range(3)] for spot, weight in zip(at, field)
            ]
            for spot, weight in zip(at, field):
                total = [total[d] + weight * grad[spot, d] for d in range(3)]
            for spot, values in zip(at, fresh):
                for d in range(3):
                    flux[spot, d] = values[d]
        for d in range(3):
            flux[base, d] = total[d]
        return carry

    lax.fori_loop(0, low_count, edges, 0)

    def divergences(source, carry):
        for s in range(sp):
            at = source * sp + s
            flux_x, flux_y, flux_z = (flux[at, d] for d in range(3))
            total = flux_x - pltpu.roll(flux_x, 1, 0)
            total = total + (flux_y - pltpu.roll(flux_y, 1, 1))
            total = total + (flux_z - jnp.where(not_bottom, pltpu.roll(flux_z, ry, 1), 0.0))
            out_ref[source, s * plan.tx : (s + 1) * plan.tx, :] = total[1 : 1 + plan.tx]
        return carry

    lax.fori_loop(0, plan.n, divergences, 0)


def unpack_image(plan, image_ref, unpack_ref, lhs, rows):
    for xb in range(plan.nxb):
        for k in range(plan.tx):
            x = xb * plan.tx + k
            for yb in range(plan.nyb):
                lhs[x * plan.hs : x * plan.hs + plan.sp, yb * plan.lanes : (yb + 1) * plan.lanes] = image_ref[
                    xb * plan.nyb + yb, strided(k, plan.sp, plan.tx), :
                ]
    pick_into(rows, lhs, unpack_ref)


def smooth(plan, base_ref, live_ref, mean_ref, rows, residual_ref, update, step):
    hs, ls = plan.hs, plan.ls
    live = live_ref[...] != 0.0
    center_value = 0.5 * (bound_high + bound_low)
    half_width = 0.5 * (bound_high - bound_low)
    ratio_value = center_value / half_width
    lane = lax.broadcasted_iota(jnp.int32, (hs, ls), 1)
    at_y, at_z = lane % NY, lane // NY
    not_y_end, not_y_start = at_y != NY - 1, at_y != 0
    not_z_end, not_z_start = at_z != plan.nz - 1, at_z != 0

    def first(x, carry):
        for c in range(3):
            image = rows[pl.ds(pl.multiple_of(x * hs, hs), hs), c * ls : (c + 1) * ls]
            value = jnp.where(live, base_ref[x, c] + image, 0.0)
            residual_ref[x, c] = value
            scaled = value * (1.0 / center_value)
            update[x, c] = scaled
            step[x, c] = scaled
        return carry

    lax.fori_loop(0, NX, first, 0)
    for c in range(3):
        update[NX, c] = jnp.zeros((hs, ls), F32)

    rho_prev = 1.0 / ratio_value
    for sweep in range(SWEEPS):
        rho_next = 1.0 / (2.0 * ratio_value - rho_prev)
        keep, gain = rho_next * rho_prev, 2.0 * rho_next / half_width

        def slab_of(x, carry, keep=keep, gain=gain):
            behind, own = carry[:3], carry[3:]
            modulus = jnp.broadcast_to(mean_ref[pl.ds(x, 1), :], (hs, ls))
            ahead = [update[x + 1, c] for c in range(3)]
            slope_x = [ahead[c] - own[c] for c in range(3)]
            slope_y = [jnp.where(not_y_end, pltpu.roll(own[c], ls - 1, 1), 0.0) - own[c] for c in range(3)]
            slope_z = [jnp.where(not_z_end, pltpu.roll(own[c], ls - NY, 1), 0.0) - own[c] for c in range(3)]
            spread = slope_x[0] + slope_y[1] + slope_z[2]
            slope_x[0] = slope_x[0] + spread
            slope_y[1] = slope_y[1] + spread
            slope_z[2] = slope_z[2] + spread
            through = []
            for c in range(3):
                flux_x, flux_y, flux_z = (modulus * slope[c] for slope in (slope_x, slope_y, slope_z))
                through.append(flux_x)
                total = flux_x - behind[c]
                total = total + (flux_y - jnp.where(not_y_start, pltpu.roll(flux_y, 1, 1), 0.0))
                total = total + (flux_z - jnp.where(not_z_start, pltpu.roll(flux_z, NY, 1), 0.0))
                moved = keep * step[x, c] + gain * (residual_ref[x, c] + total)
                step[x, c] = moved
                update[x, c] = own[c] + moved
            return (*through, *ahead)

        zero = jnp.zeros((hs, ls), F32)
        lax.fori_loop(0, NX, slab_of, (zero, zero, zero, *(update[0, c] for c in range(3))), unroll=2)
        rho_prev = rho_next


def middle_kernel(plan, image_ref, base_ref, live_ref, mean_ref, unpack_ref, pack_ref, msg_ref, residual_ref, update_ref, wide, narrow, step):
    unpack_image(plan, image_ref, unpack_ref, wide, narrow)
    smooth(plan, base_ref, live_ref, mean_ref, narrow, residual_ref, update_ref, step)
    for x in range(NX):
        for c in range(3):
            narrow[x * plan.hs : (x + 1) * plan.hs, c * plan.ls : (c + 1) * plan.ls] = update_ref[x, c]
    pick_into(wide, narrow, pack_ref)
    store_message(plan, wide, msg_ref)


def end_kernel(plan, image_ref, base_ref, live_ref, mean_ref, unpack_ref, before_ref, out_ref, lhs_in, rows_in, residual, update, step):
    unpack_image(plan, image_ref, unpack_ref, lhs_in, rows_in)
    smooth(plan, base_ref, live_ref, mean_ref, rows_in, residual, update, step)
    sp = plan.sp

    def spread_out(values, first, a):
        for t in range(plan.nz // 4):
            parts = [value[:, t * 128 : (t + 1) * 128] for value in values]
            for i, piece in enumerate(swap_quarters(parts)):
                out_ref[4 * t + i, first : first + sp, a * 128 : (a + 1) * 128] = piece[:sp]

    for a in range(PLANE // 128):
        for c in range(3):
            spread_out([update[4 * a + b, c] + before_ref[4 * a + b, c] for b in range(4)], c * sp, a)
            spread_out([residual[4 * a + b, c] for b in range(4)], (3 + c) * sp, a)


def per_device(displacement, load, mean_modulus, modes, owner):
    chaos, slab = lax.axis_size("chaos"), lax.axis_size("slab")
    slots_dev, slots_all = displacement.shape[0], owner.shape[0]
    plan = Plan(chaos, slab, slots_dev)
    n, sp, hs, ls, lanes = plan.n, plan.sp, plan.hs, plan.ls, plan.lanes
    count, low, raised, level = edge_tables()
    at_chaos, at_slab = lax.axis_index("chaos"), lax.axis_index("slab")

    slots = np.arange(slots_all)
    places = (slots // slots_dev) * (slab * sp) + slots % slots_dev
    wanted = np.concatenate([low, raised])
    nodes = jnp.sum(
        jnp.where(wanted[:, None] == owner[None, :], jnp.asarray(places, jnp.int32)[None, :], 0), axis=1
    ).astype(jnp.int32)
    live_all = owner < count
    live_own = lax.dynamic_slice_in_dim(live_all, at_chaos * slots_dev, slots_dev, 0)
    live_here = jnp.pad(live_own.astype(F32), (0, slab * sp - slots_dev))
    live_here = lax.dynamic_slice_in_dim(live_here, at_slab * sp, sp, 0)
    live_here = jnp.broadcast_to(jnp.pad(live_here, (0, hs - sp))[:, None], (hs, ls))

    pack = jnp.asarray(plan.pack_table(), BF16)
    unpack = jnp.asarray(plan.unpack_table(), BF16)
    mtab = jnp.asarray(plan.modulus_table(), BF16)
    tile = (at_chaos * slab + at_slab).astype(jnp.int32).reshape(1)

    def by_slab(values):
        values = jnp.pad(values, ((0, slab * sp - slots_dev), (0, 0), (0, 0)))
        return jnp.transpose(values.reshape(slab, sp, 3, PLANE), (0, 2, 1, 3)).reshape(slab, 3 * sp, PLANE)

    moduli = jnp.concatenate([mean_modulus[None], modes], axis=0)
    outgoing = jnp.concatenate(
        [by_slab(displacement), by_slab(load), jnp.broadcast_to(moduli[None], (slab, FIELDS, PLANE))], axis=1
    )
    outgoing = jnp.pad(outgoing, ((0, 0), (0, plan.rows_start - outgoing.shape[1]), (0, 0)))
    incoming = lax.all_to_all(outgoing, "slab", 0, 0, tiled=True)

    smem = pl.BlockSpec(memory_space=pltpu.SMEM)
    vmem = pl.BlockSpec(memory_space=pltpu.VMEM)
    params = pltpu.CompilerParams(vmem_limit_bytes=VMEM_LIMIT)
    message = jax.ShapeDtypeStruct((n, plan.rows_in, lanes), F32)
    image = jax.ShapeDtypeStruct((n, plan.rows_out, lanes), F32)
    grid_field = jax.ShapeDtypeStruct((NX, 3, hs, ls), F32)
    grid_more = jax.ShapeDtypeStruct((NX + 1, 3, hs, ls), F32)
    wide = pltpu.VMEM((NX * hs, plan.nyb * lanes), F32)
    narrow = pltpu.VMEM((NX * hs, 3 * ls), F32)

    def everyone(values):
        return lax.all_to_all(values, ("chaos", "slab"), 0, 0, tiled=True)

    msg, load_s, mean_s, mods = pl.pallas_call(
        functools.partial(start_kernel, plan),
        out_shape=(
            message,
            grid_field,
            jax.ShapeDtypeStruct((NX, ls), F32),
            jax.ShapeDtypeStruct((FIELDS, 8, lanes), F32),
        ),
        in_specs=[smem, vmem, vmem, vmem],
        out_specs=(vmem,) * 4,
        scratch_shapes=[narrow, wide, pltpu.VMEM((NX + 2, 16, ls), F32)],
        compiler_params=params,
        name="start",
    )(tile, incoming, pack, mtab)

    def mixed(values):
        return pl.pallas_call(
            functools.partial(mix_kernel, plan, len(low)),
            out_shape=image,
            in_specs=[smem, smem, vmem, vmem],
            out_specs=vmem,
            scratch_shapes=[
                pltpu.VMEM((plan.positions, 3, 8, lanes), F32),
                pltpu.VMEM((plan.positions, 3, 8, lanes), F32),
                pltpu.VMEM((DEG * KL, 8, lanes), F32),
            ],
            compiler_params=params,
            name="mix",
        )(nodes, jnp.asarray(level, jnp.int32), values, mods)

    first_image = everyone(mixed(everyone(msg)))
    msg, residual_s, update_s = pl.pallas_call(
        functools.partial(middle_kernel, plan),
        out_shape=(message, grid_field, grid_more),
        in_specs=[vmem] * 6,
        out_specs=(vmem,) * 3,
        scratch_shapes=[wide, narrow, pltpu.VMEM((NX, 3, hs, ls), F32)],
        compiler_params=params,
        name="middle",
    )(first_image, load_s, live_here, mean_s, unpack, pack)

    second_image = everyone(mixed(everyone(msg)))
    ending = pl.pallas_call(
        functools.partial(end_kernel, plan),
        out_shape=jax.ShapeDtypeStruct((slab, plan.rows_end, PLANE), F32),
        in_specs=[vmem] * 6,
        out_specs=vmem,
        scratch_shapes=[
            wide,
            narrow,
            pltpu.VMEM((NX, 3, hs, ls), F32),
            pltpu.VMEM((NX + 1, 3, hs, ls), F32),
            pltpu.VMEM((NX, 3, hs, ls), F32),
        ],
        compiler_params=params,
        name="end",
    )(second_image, residual_s, live_here, mean_s, unpack, update_s)
    final = lax.all_to_all(ending, "slab", 0, 0, tiled=True)

    def by_slot(values):
        values = jnp.transpose(values.reshape(slab, 3, sp, PLANE), (0, 2, 1, 3))
        return values.reshape(slab * sp, 3, PLANE)[:slots_dev]

    start = jnp.where(live_own[:, None, None], displacement, 0.0)
    return (start + by_slot(final[:, : 3 * sp]), by_slot(final[:, 3 * sp : 6 * sp]))


def solution(mesh):
    in_specs = (P("chaos", None, "slab"), P("chaos", None, "slab"), P("slab"), P(None, "slab"), P())
    out_specs = (P("chaos", None, "slab"), P("chaos", None, "slab"))
    return jax.shard_map(
        per_device, mesh=mesh, in_specs=in_specs, out_specs=out_specs, check_vma=False
    )
```

time: 557 us -> 207 us (0.37); the launches traced: 548 us -> 206 us
  waiting for transfers between devices: 265 us -> 55.2 us
  local copies, waits for them, and re-layouts: 110 us -> 9.02 us
  other arithmetic: 72.9 us -> 2.16 us
  blocking collectives: 0 us -> 65.7 us
  Pallas kernels: 0 us -> 59 us
  starting transfers between devices: 64.8 us -> 14.4 us
  matrix products: 19 us -> 0 us
  between operations: 16.3 us -> 0.79 us
    ppermute x21 -> x0, waiting for transfers between devices: 231 us -> none  [the longest x10 113 us: extended_2(): lax.ppermute(tail, axis, [(i, (i + 1) % count) for i in range(ends)])]
    all_to_all x0 -> x3, blocking collectives: none -> 65.7 us  [the longest x2 42.7 us: everyone(): return lax.all_to_all(values, ('chaos', 'slab'), 0, 0, tiled=True)]
    ppermute x21 -> x0, starting transfers between devices: 64.8 us -> none  [the longest x10 35.9 us: extended_2(): lax.ppermute(tail, axis, [(i, (i + 1) % count) for i in range(ends)])]
    pallas_call x0 -> x5, Pallas kernels: none -> 59 us  [the longest x2 29.1 us: mixed(): pl.pallas_call(functools.partial(mix_kernel, plan, len(low)), out_shape=i...]
    all_to_all x0 -> x3, waiting for transfers between devices: none -> 55.2 us  [the longest x2 33 us: everyone(): return lax.all_to_all(values, ('chaos', 'slab'), 0, 0, tiled=True)]
    slice x121 -> x3, local copies, waits for them, and re-layouts: 41.7 us -> 0.49 us  [the longest x2 0.27 us: per_device(): final[:, 3 * sp:6 * sp]]
    mul x20 -> x0, other arithmetic: 39.9 us -> none  [stiffness_flat(): flux_term = modulus * gradient]
    gather x8 -> x0, local copies, waits for them, and re-layouts: 39.3 us -> none  [the longest x4 35 us: to_slots(): slots_of = inverse[jnp.minimum(targets, number_all - 1)]]
  transfers between devices with their start and end apart: 23 -> 3, of which waited for: 19 -> 3; matrix products, arithmetic and copies ran while one was open for 8% -> 0% of each run, Pallas kernels for 0% -> 0%
where the time goes in v1:
time: 207 us; the launch traced here: 206 us
  blocking collectives  65.7 us (32%)
  Pallas kernels  59 us (29%)
  waiting for transfers between devices  55.2 us (27%)
  starting transfers between devices  14.4 us (7%)
  local copies, waits for them, and re-layouts  9.02 us (4%)
  other arithmetic  2.16 us (1%)
    all_to_all x2, blocking collectives, everyone(): return lax.all_to_all(values, ('chaos', 'slab'), 0, 0, tiled=True)  42.7 us
    all_to_all x2, waiting for transfers between devices, everyone(): return lax.all_to_all(values, ('chaos', 'slab'), 0, 0, tiled=True)  33 us
    pallas_call x2, Pallas kernels, mixed(): pl.pallas_call(functools.partial(mix_kernel, plan, len(low)), out_shape=i...  29.1 us
    all_to_all x1, blocking collectives, per_device(): final = lax.all_to_all(ending, 'slab', 0, 0, tiled=True)  23.1 us
    all_to_all x1, waiting for transfers between devices, per_device(): incoming = lax.all_to_all(outgoing, 'slab', 0, 0, tiled=True)  22.2 us
    pallas_call x1, Pallas kernels, per_device(): pl.pallas_call(functools.partial(end_kernel, plan), out_shape=jax.ShapeDt...  13.2 us
    pallas_call x1, Pallas kernels, per_device(): pl.pallas_call(functools.partial(middle_kernel, plan), out_shape=(message...  13.1 us
    all_to_all x2, starting transfers between devices, everyone(): return lax.all_to_all(values, ('chaos', 'slab'), 0, 0, tiled=True)  8.07 us
  transfers between devices with their start and end apart: 3, of which 3 were waited for; matrix products, arithmetic and copies ran while one was open for 0% of the time, Pallas kernels for 0%

profile of v1, /device:TPU:0, one launch (start us, length us, event | category | flops | bytes accessed | tf_op | source)
XLA Modules:
  0.0 206.3 jit_solution(3755489645870345343)
XLA Ops:
  0.6 0.7 broadcast_in_dim.46
  1.3 1.2 copy.34
  2.5 0.1 copy.35
  2.7 0.9 copy-done.3
  3.6 0.2 copy.31
  3.9 0.7 copy-done.4
  4.7 1.0 select_maximum_fusion
  5.7 6.3 %all-to-all-start = ((f32[4,72,768]{2,1,0:T(8,128)}), f32[4,72,768]{2,1,0:T(8,128)S(1)}, u32[]{:S(2)}, u32[]{:S(2)}) async-start(f32[4,72,768]{2,1,0:T(8,128)} %select_maximum_fusion), calls=%async_computation | async-start | bytes 1769472 | tf_op jit(solution)/shard_map/all_to_all | solution.py:405
  12.0 22.2 %all-to-all-done.in_ref = f32[4,72,768]{2,1,0:T(8,128)S(1)} async-done(((f32[4,72,768]{2,1,0:T(8,128)}), f32[4,72,768]{2,1,0:T(8,128)S(1)}, u32[]{:S(2)}, u32[]{:S(2)}) %all-to-all-start) | async-done | bytes 884768 | tf_op jit(solution)/shard_map/all_to_all | solution.py:405
  34.2 0.9 copy-done
  35.1 3.7 %start.1 = (f32[32,48,128]{2,1,0:T(8,128)}, f32[24,3,16,128]{3,2,1,0:T(8,128)}, f32[24,128]{1,0:T(8,128)}, f32[11,8,128]{2,1,0:T(8,128)}) custom-call(s32[1]{0:T(128)} %bitcast.tile_ref, f32[4,72,768]{2,1,0:T(8,128)} %copy-done, bf16[384,512]{1,0:T(8,128)(2,1)} %constant.37.clone.pack_ref, bf16[4,128,128]{2,1,0:T(8,128)(2,1)} %constant.39.clone.mtab_ref), custom_call_target="tpu_custom_call" | custom-call | tf_op jit(solution)/shard_map/start/pallas_call | solution.py:420
  38.8 3.7 %all-to-all-start.1 = ((f32[32,48,128]{2,1,0:T(8,128)}), f32[32,48,128]{2,1,0:T(8,128)S(1)}, u32[]{:S(2)}, u32[]{:S(2)}) async-start(f32[32,48,128]{2,1,0:T(8,128)} %get-tuple-element.9), calls=%async_computation.1 | async-start | bytes 1572864 | tf_op jit(solution)/shard_map/all_to_all | solution.py:418
  42.5 0.8 fusion.nodes_ref
  43.3 18.8 %all-to-all-done.1.msg_ref = f32[32,48,128]{2,1,0:T(8,128)S(1)} async-done(((f32[32,48,128]{2,1,0:T(8,128)}), f32[32,48,128]{2,1,0:T(8,128)S(1)}, u32[]{:S(2)}, u32[]{:S(2)}) %all-to-all-start.1) | async-done | bytes 786464 | tf_op jit(solution)/shard_map/all_to_all | solution.py:418
  62.1 0.9 copy-done.1
  63.1 14.5 %mix.2 = f32[32,32,128]{2,1,0:T(8,128)} custom-call(s32[726]{0:T(1024)} %fusion.nodes_ref, s32[660]{0:T(1024)} %constant.40.clone.level_ref, f32[32,48,128]{2,1,0:T(8,128)} %copy-done.1, f32[11,8,128]{2,1,0:T(8,128)} %get-tuple-element.10.mods_ref), custom_call_target="tpu_custom_call" | custom-call | tf_op jit(solution)/shard_map/mix/pallas_call | solution.py:436
  77.6 4.4 %all-to-all-start.2 = ((f32[32,32,128]{2,1,0:T(8,128)}), f32[32,32,128]{2,1,0:T(8,128)S(1)}, u32[]{:S(2)}, u32[]{:S(2)}) async-start(f32[32,32,128]{2,1,0:T(8,128)} %mix.2), calls=%async_computation.2 | async-start | bytes 1048576 | tf_op jit(solution)/shard_map/all_to_all | solution.py:418
  82.1 14.2 %all-to-all-done.2.image_ref = f32[32,32,128]{2,1,0:T(8,128)S(1)} async-done(((f32[32,32,128]{2,1,0:T(8,128)}), f32[32,32,128]{2,1,0:T(8,128)S(1)}, u32[]{:S(2)}, u32[]{:S(2)}) %all-to-all-start.2) | async-done | bytes 524320 | tf_op jit(solution)/shard_map/all_to_all | solution.py:418
  96.3 0.8 broadcast_in_dim.48.live_ref
  97.1 13.1 %middle.1 = (f32[32,48,128]{2,1,0:T(8,128)}, f32[24,3,16,128]{3,2,1,0:T(8,128)}, f32[25,3,16,128]{3,2,1,0:T(8,128)}) custom-call(f32[32,32,128]{2,1,0:T(8,128)} %copy-done.2, f32[24,3,16,128]{3,2,1,0:T(8,128)} %get-tuple-element.11.base_ref, f32[16,128]{1,0:T(8,128)} %broadcast_in_dim.48.live_ref, f32[24,128]{1,0:T(8,128)} %get-tuple-element.12.mean_ref, ...), custom_call_target="tpu_custom_call" | custom-call | tf_op jit(solution)/shard_map/middle/pallas_call | solution.py:451
  110.2 23.8 %all_to_all.30.msg_ref = f32[32,48,128]{2,1,0:T(8,128)} all-to-all(f32[32,48,128]{2,1,0:T(8,128)} %get-tuple-element.13), channel_id=1, replica_groups=mesh['chaos'=8,'slab'=4] {'chaos','slab'}, dimensions={0} | all-to-all | bytes 1572864 | tf_op jit(solution)/shard_map/all_to_all | solution.py:418
  134.1 14.5 %mix.3 = f32[32,32,128]{2,1,0:T(8,128)} custom-call(s32[726]{0:T(1024)} %fusion.nodes_ref, s32[660]{0:T(1024)} %constant.40.clone.level_ref, f32[32,48,128]{2,1,0:T(8,128)} %all_to_all.30.msg_ref, f32[11,8,128]{2,1,0:T(8,128)} %get-tuple-element.10.mods_ref), custom_call_target="tpu_custom_call" | custom-call | tf_op jit(solution)/shard_map/mix/pallas_call | solution.py:436
  148.6 18.8 %all_to_all.31.image_ref = f32[32,32,128]{2,1,0:T(8,128)} all-to-all(f32[32,32,128]{2,1,0:T(8,128)} %mix.3), channel_id=1, replica_groups=mesh['chaos'=8,'slab'=4] {'chaos','slab'}, dimensions={0} | all-to-all | bytes 1048576 | tf_op jit(solution)/shard_map/all_to_all | solution.py:418
  167.4 13.2 %end.1 = f32[4,56,768]{2,1,0:T(8,128)} custom-call(f32[32,32,128]{2,1,0:T(8,128)} %all_to_all.31.image_ref, f32[24,3,16,128]{3,2,1,0:T(8,128)} %get-tuple-element.14.base_ref, f32[16,128]{1,0:T(8,128)} %broadcast_in_dim.48.live_ref, f32[24,128]{1,0:T(8,128)} %get-tuple-element.12.mean_ref, bf16[512,384]{1,0:T(8,128)(2,1)} %constant.38.clone.unpack_ref, ...), custom_call_target="tpu_custom_call" | custom-call | tf_op jit(solution)/shard_map/end/pallas_call | solution.py:462
  180.6 23.1 %all_to_all.32 = f32[4,56,768]{2,1,0:T(8,128)S(1)} all-to-all(f32[4,56,768]{2,1,0:T(8,128)} %end.1), channel_id=1, replica_groups=mesh['chaos'=8,'slab'=4] {'slab'}, dimensions={0} | all-to-all | bytes 1376256 | tf_op jit(solution)/shard_map/all_to_all | solution.py:477
  203.7 0.2 copy.40
  204.0 0.1 copy.41
  204.1 0.8 copy.43
  204.9 0.2 copy.38
  205.1 0.1 copy.39
  205.2 0.3 bitcast_add_fusion
  205.5 0.8 copy.42
  (20 shorter events, 0.5 us)
Async XLA Ops:
  2.6 1.0 copy-start.3
  3.8 0.8 copy-start.4
  5.7 28.5 %all-to-all-start = ((f32[4,72,768]{2,1,0:T(8,128)}), f32[4,72,768]{2,1,0:T(8,128)S(1)}, u32[]{:S(2)}, u32[]{:S(2)}) async-start(f32[4,72,768]{2,1,0:T(8,128)} %select_maximum_fusion), calls=%async_computation | async-start | bytes 1769472 | tf_op jit(solution)/shard_map/all_to_all | solution.py:405
  34.2 0.9 copy-start
  38.8 3.7 %copy-start.5 = (s32[288]{0:T(512)S(1)}, s32[288]{0:T(512)}, u32[]{:S(2)}) copy-start(s32[288]{0:T(512)} %param.16) | copy-start | bytes 3460
  38.8 3.7 %copy-start.6 = (s32[726]{0:T(1024)S(1)}, s32[726]{0:T(1024)}, u32[]{:S(2)}) copy-start(s32[726]{0:T(1024)} %constant.47) | copy-start | bytes 8716
  38.8 23.3 %all-to-all-start.1 = ((f32[32,48,128]{2,1,0:T(8,128)}), f32[32,48,128]{2,1,0:T(8,128)S(1)}, u32[]{:S(2)}, u32[]{:S(2)}) async-start(f32[32,48,128]{2,1,0:T(8,128)} %get-tuple-element.9), calls=%async_computation.1 | async-start | bytes 1572864 | tf_op jit(solution)/shard_map/all_to_all | solution.py:418
  62.1 0.9 copy-start.1
  77.6 18.7 %all-to-all-start.2 = ((f32[32,32,128]{2,1,0:T(8,128)}), f32[32,32,128]{2,1,0:T(8,128)S(1)}, u32[]{:S(2)}, u32[]{:S(2)}) async-start(f32[32,32,128]{2,1,0:T(8,128)} %mix.2), calls=%async_computation.2 | async-start | bytes 1048576 | tf_op jit(solution)/shard_map/all_to_all | solution.py:418
  96.3 0.8 copy-start.2

commit v2 on v1

--- a/solution.py
+++ b/solution.py
@@ -19,7 +19,7 @@
 
 bound_high = 50.0
 bound_low = 2.5
-VMEM_LIMIT = 60 * 1024 * 1024
+MIB = 1024 * 1024
 F32 = jnp.float32
 BF16 = jnp.bfloat16
 
@@ -78,8 +78,7 @@
         self.ry = self.ty + 2
         self.nxb, self.nyb = NX // self.tx, NY // self.ty
         self.rows_out = up8(self.sp * self.tx)
-        self.rows_start = up8(6 * self.sp + 16)
-        self.rows_end = up8(6 * self.sp)
+        self.rows_flat = up8(3 * self.sp)
         self.positions = self.n * self.sp
 
     def pack_table(self):
@@ -174,30 +173,79 @@
             msg_ref[tile, strided(k, plan.sp, plan.rx), :] = rows
 
 
-def start_kernel(plan, tile_ref, in_ref, pack_ref, mtab_ref, msg_ref, load_ref, mean_ref, mods_ref, lhs, rows, fields):
+def rows_at(piece_of):
+    return [jnp.concatenate(pieces, axis=1) if len(pieces) > 1 else pieces[0] for pieces in zip(*piece_of)]
+
+
+def start_kernel(plan, in_ref, pack_ref, msg_ref, lhs, rows):
+    for a in range(PLANE // 128):
+        for c in range(3):
+            pieces = rows_at(
+                swap_quarters(
+                    [
+                        in_ref[c, (4 * t + i) * plan.sp : (4 * t + i + 1) * plan.sp, a * 128 : (a + 1) * 128]
+                        for i in range(4)
+                    ]
+                )
+                for t in range(plan.slab // 4)
+            )
+            for b, piece in enumerate(pieces):
+                x = 4 * a + b
+                lhs[x * plan.hs : x * plan.hs + plan.sp, c * plan.ls : (c + 1) * plan.ls] = piece
+    pick_into(rows, lhs, pack_ref)
+    store_message(plan, rows, msg_ref)
+
+
+def split_kernel(plan, in_ref, out_ref):
+    for group in range(plan.slab):
+        for c in range(3):
+            out_ref[group, c * plan.sp : (c + 1) * plan.sp, :] = in_ref[
+                c, group * plan.sp : (group + 1) * plan.sp, :
+            ]
+
+
+def load_kernel(plan, in_ref, out_ref):
+    for a in range(PLANE // 128):
+        for c in range(3):
+            pieces = rows_at(
+                swap_quarters(
+                    [in_ref[4 * t + i, c * plan.sp : (c + 1) * plan.sp, a * 128 : (a + 1) * 128] for i in range(4)]
+                )
+                for t in range(plan.nz // 4)
+            )
+            for b, piece in enumerate(pieces):
+                out_ref[4 * a + b, c, 0 : plan.sp, :] = piece
+
+
+def join_kernel(plan, in_ref, out_ref):
+    for group in range(plan.slab):
+        for c in range(3):
+            out_ref[c, group * plan.sp : (group + 1) * plan.sp, :] = in_ref[
+                group, c * plan.sp : (c + 1) * plan.sp, :
+            ]
+
+
+def add_kernel(plan, in_ref, live_ref, start_ref, out_ref):
+    for group in range(plan.slab):
+        here = slice(group * plan.sp, (group + 1) * plan.sp)
+        live = jnp.broadcast_to(live_ref[here, :], (plan.sp, PLANE)) != 0.0
+        for c in range(3):
+            out_ref[c, here, :] = jnp.where(live, start_ref[c, here, :], 0.0) + in_ref[
+                group, c * plan.sp : (c + 1) * plan.sp, :
+            ]
+
+
+def moduli_kernel(plan, tile_ref, in_ref, mtab_ref, mean_ref, mods_ref, fields):
     fields[0] = jnp.zeros((16, plan.ls), F32)
     fields[NX + 1] = jnp.zeros((16, plan.ls), F32)
-
-    def slabs_of(first, count, a):
-        out = [[] for _ in range(4)]
-        for t in range(plan.nz // 4):
-            parts = [in_ref[4 * t + i, first : first + count, a * 128 : (a + 1) * 128] for i in range(4)]
-            for b, piece in enumerate(swap_quarters(parts)):
-                out[b].append(piece)
-        return [piece[0] if len(piece) == 1 else jnp.concatenate(piece, axis=1) for piece in out]
-
     for a in range(PLANE // 128):
-        for c in range(3):
-            for b, piece in enumerate(slabs_of(c * plan.sp, plan.hs, a)):
-                x = 4 * a + b
-                lhs[x * plan.hs : (x + 1) * plan.hs, c * plan.ls : (c + 1) * plan.ls] = piece
-            for b, piece in enumerate(slabs_of((3 + c) * plan.sp, plan.hs, a)):
-                load_ref[4 * a + b, c] = piece
-        for b, piece in enumerate(slabs_of(6 * plan.sp, 16, a)):
+        pieces = rows_at(
+            swap_quarters([in_ref[4 * t + i, :, a * 128 : (a + 1) * 128] for i in range(4)])
+            for t in range(plan.nz // 4)
+        )
+        for b, piece in enumerate(pieces):
             fields[4 * a + b + 1] = piece
             mean_ref[4 * a + b : 4 * a + b + 1, :] = piece[0:1]
-    pick_into(rows, lhs, pack_ref)
-    store_message(plan, rows, msg_ref)
     tile = jnp.minimum(tile_ref[0], plan.nxb * plan.nyb - 1)
     xb, yb = tile // plan.nyb, tile % plan.nyb
     table = mtab_ref[yb]
@@ -206,6 +254,29 @@
         here = picked(fields[xb * plan.tx + k], table)
         for v in range(FIELDS):
             mods_ref[v, k : k + 1, :] = here[v : v + 1]
+
+
+def regrouped(plan, msg_ref, out_ref):
+    lane = lax.broadcasted_iota(jnp.int32, (plan.rows_in, plan.lanes), 1)
+    height = lane % (plan.nz * plan.ry) // plan.ry
+
+    def one(row, carry):
+        parts = [msg_ref[row * plan.slab + z] for z in range(plan.nz)]
+        for group in range(plan.slab):
+            total = parts[group]
+            for z in range(plan.nz):
+                if z != group:
+                    turned = pltpu.roll(parts[z], (z - group) * plan.ry % plan.lanes, 1)
+                    total = jnp.where(height == z, turned, total)
+            out_ref[row * plan.slab + group] = total
+        return carry
+
+    lax.fori_loop(0, plan.chaos, one, 0)
+
+
+def first_mix_kernel(plan, low_count, nodes_ref, level_ref, msg_ref, mods_ref, out_ref, grad, flux, scaled, regroup):
+    regrouped(plan, msg_ref, regroup)
+    mix_kernel(plan, low_count, nodes_ref, level_ref, regroup, mods_ref, out_ref, grad, flux, scaled)
 
 
 def mix_kernel(plan, low_count, nodes_ref, level_ref, msg_ref, mods_ref, out_ref, grad, flux, scaled):
@@ -283,9 +354,20 @@
     pick_into(rows, lhs, unpack_ref)
 
 
-def smooth(plan, base_ref, live_ref, mean_ref, rows, residual_ref, update, step):
+def add_image(plan, base_ref, live_ref, rows, residual_ref):
+    live = live_ref[...] != 0.0
+
+    def one(x, carry):
+        for c in range(3):
+            image = rows[pl.ds(pl.multiple_of(x * plan.hs, plan.hs), plan.hs), c * plan.ls : (c + 1) * plan.ls]
+            residual_ref[x, c] = jnp.where(live, base_ref[x, c] + image, 0.0)
+        return carry
+
+    lax.fori_loop(0, NX, one, 0)
+
+
+def smooth(plan, mean_ref, residual_ref, update, step):
     hs, ls = plan.hs, plan.ls
-    live = live_ref[...] != 0.0
     center_value = 0.5 * (bound_high + bound_low)
     half_width = 0.5 * (bound_high - bound_low)
     ratio_value = center_value / half_width
@@ -296,10 +378,7 @@
 
     def first(x, carry):
         for c in range(3):
-            image = rows[pl.ds(pl.multiple_of(x * hs, hs), hs), c * ls : (c + 1) * ls]
-            value = jnp.where(live, base_ref[x, c] + image, 0.0)
-            residual_ref[x, c] = value
-            scaled = value * (1.0 / center_value)
+            scaled = residual_ref[x, c] * (1.0 / center_value)
             update[x, c] = scaled
             step[x, c] = scaled
         return carry
@@ -343,7 +422,8 @@
 
 def middle_kernel(plan, image_ref, base_ref, live_ref, mean_ref, unpack_ref, pack_ref, msg_ref, residual_ref, update_ref, wide, narrow, step):
     unpack_image(plan, image_ref, unpack_ref, wide, narrow)
-    smooth(plan, base_ref, live_ref, mean_ref, narrow, residual_ref, update_ref, step)
+    add_image(plan, base_ref, live_ref, narrow, residual_ref)
+    smooth(plan, mean_ref, residual_ref, update_ref, step)
     for x in range(NX):
         for c in range(3):
             narrow[x * plan.hs : (x + 1) * plan.hs, c * plan.ls : (c + 1) * plan.ls] = update_ref[x, c]
@@ -351,21 +431,26 @@
     store_message(plan, wide, msg_ref)
 
 
-def end_kernel(plan, image_ref, base_ref, live_ref, mean_ref, unpack_ref, before_ref, out_ref, lhs_in, rows_in, residual, update, step):
-    unpack_image(plan, image_ref, unpack_ref, lhs_in, rows_in)
-    smooth(plan, base_ref, live_ref, mean_ref, rows_in, residual, update, step)
-    sp = plan.sp
-
-    def spread_out(values, first, a):
-        for t in range(plan.nz // 4):
-            parts = [value[:, t * 128 : (t + 1) * 128] for value in values]
-            for i, piece in enumerate(swap_quarters(parts)):
-                out_ref[4 * t + i, first : first + sp, a * 128 : (a + 1) * 128] = piece[:sp]
-
+def flat_rows(plan, values, out_ref, c, a):
+    for t in range(plan.nz // 4):
+        parts = [value[:, t * 128 : (t + 1) * 128] for value in values]
+        for i, piece in enumerate(swap_quarters(parts)):
+            out_ref[4 * t + i, c * plan.sp : (c + 1) * plan.sp, a * 128 : (a + 1) * 128] = piece[: plan.sp]
+
+
+def residual_kernel(plan, image_ref, base_ref, live_ref, unpack_ref, residual_ref, out_ref, wide, narrow):
+    unpack_image(plan, image_ref, unpack_ref, wide, narrow)
+    add_image(plan, base_ref, live_ref, narrow, residual_ref)
     for a in range(PLANE // 128):
         for c in range(3):
-            spread_out([update[4 * a + b, c] + before_ref[4 * a + b, c] for b in range(4)], c * sp, a)
-            spread_out([residual[4 * a + b, c] for b in range(4)], (3 + c) * sp, a)
+            flat_rows(plan, [residual_ref[4 * a + b, c] for b in range(4)], out_ref, c, a)
+
+
+def end_kernel(plan, residual_ref, mean_ref, before_ref, out_ref, update, step):
+    smooth(plan, mean_ref, residual_ref, update, step)
+    for a in range(PLANE // 128):
+        for c in range(3):
+            flat_rows(plan, [update[4 * a + b, c] + before_ref[4 * a + b, c] for b in range(4)], out_ref, c, a)
 
 
 def per_device(displacement, load, mean_modulus, modes, owner):
@@ -393,95 +478,97 @@
     mtab = jnp.asarray(plan.modulus_table(), BF16)
     tile = (at_chaos * slab + at_slab).astype(jnp.int32).reshape(1)
 
-    def by_slab(values):
-        values = jnp.pad(values, ((0, slab * sp - slots_dev), (0, 0), (0, 0)))
-        return jnp.transpose(values.reshape(slab, sp, 3, PLANE), (0, 2, 1, 3)).reshape(slab, 3 * sp, PLANE)
-
-    moduli = jnp.concatenate([mean_modulus[None], modes], axis=0)
-    outgoing = jnp.concatenate(
-        [by_slab(displacement), by_slab(load), jnp.broadcast_to(moduli[None], (slab, FIELDS, PLANE))], axis=1
-    )
-    outgoing = jnp.pad(outgoing, ((0, 0), (0, plan.rows_start - outgoing.shape[1]), (0, 0)))
-    incoming = lax.all_to_all(outgoing, "slab", 0, 0, tiled=True)
+    slots_pad = slab * sp
+
+    def by_component(values):
+        return jnp.pad(jnp.transpose(values, (1, 0, 2)), ((0, 0), (0, slots_pad - slots_dev), (0, 0)))
+
+    def everyone(values):
+        return lax.all_to_all(values, ("chaos", "slab"), 0, 0, tiled=True)
+
+    def column(values):
+        return lax.all_to_all(values, "slab", 0, 0, tiled=True)
 
     smem = pl.BlockSpec(memory_space=pltpu.SMEM)
     vmem = pl.BlockSpec(memory_space=pltpu.VMEM)
-    params = pltpu.CompilerParams(vmem_limit_bytes=VMEM_LIMIT)
-    message = jax.ShapeDtypeStruct((n, plan.rows_in, lanes), F32)
-    image = jax.ShapeDtypeStruct((n, plan.rows_out, lanes), F32)
-    grid_field = jax.ShapeDtypeStruct((NX, 3, hs, ls), F32)
-    grid_more = jax.ShapeDtypeStruct((NX + 1, 3, hs, ls), F32)
+
+    def call(kernel, name, in_specs, out_shape, scratch_shapes):
+        return pl.pallas_call(
+            kernel,
+            out_shape=out_shape,
+            in_specs=in_specs,
+            out_specs=jax.tree.map(lambda _: vmem, out_shape),
+            scratch_shapes=scratch_shapes,
+            compiler_params=pltpu.CompilerParams(vmem_limit_bytes=(16 if plan.positions <= 512 and n <= 64 else 60) * MIB),
+            name=name,
+        )
+
+    def array(*shape):
+        return jax.ShapeDtypeStruct(shape, F32)
+
+    message, image = array(n, plan.rows_in, lanes), array(n, plan.rows_out, lanes)
+    grid_field, grid_more = array(NX, 3, hs, ls), array(NX + 1, 3, hs, ls)
     wide = pltpu.VMEM((NX * hs, plan.nyb * lanes), F32)
     narrow = pltpu.VMEM((NX * hs, 3 * ls), F32)
-
-    def everyone(values):
-        return lax.all_to_all(values, ("chaos", "slab"), 0, 0, tiled=True)
-
-    msg, load_s, mean_s, mods = pl.pallas_call(
-        functools.partial(start_kernel, plan),
-        out_shape=(
-            message,
-            grid_field,
-            jax.ShapeDtypeStruct((NX, ls), F32),
-            jax.ShapeDtypeStruct((FIELDS, 8, lanes), F32),
-        ),
-        in_specs=[smem, vmem, vmem, vmem],
-        out_specs=(vmem,) * 4,
-        scratch_shapes=[narrow, wide, pltpu.VMEM((NX + 2, 16, ls), F32)],
-        compiler_params=params,
-        name="start",
-    )(tile, incoming, pack, mtab)
-
-    def mixed(values):
-        return pl.pallas_call(
-            functools.partial(mix_kernel, plan, len(low)),
-            out_shape=image,
-            in_specs=[smem, smem, vmem, vmem],
-            out_specs=vmem,
-            scratch_shapes=[
-                pltpu.VMEM((plan.positions, 3, 8, lanes), F32),
-                pltpu.VMEM((plan.positions, 3, 8, lanes), F32),
-                pltpu.VMEM((DEG * KL, 8, lanes), F32),
-            ],
-            compiler_params=params,
-            name="mix",
+    field_scratch, more_scratch = pltpu.VMEM(grid_field.shape, F32), pltpu.VMEM(grid_more.shape, F32)
+
+    moduli = jnp.concatenate([mean_modulus[None], modes], axis=0)
+    moduli = lax.all_gather(jnp.pad(moduli, ((0, 16 - FIELDS), (0, 0))), "slab", axis=0)
+    mean_s, mods = call(
+        functools.partial(moduli_kernel, plan),
+        "moduli",
+        [smem, vmem, vmem],
+        (array(NX, ls), array(FIELDS, 8, lanes)),
+        [pltpu.VMEM((NX + 2, 16, ls), F32)],
+    )(tile, moduli, mtab)
+
+    msg = call(functools.partial(start_kernel, plan), "start", [vmem, vmem], message, [narrow, wide])(
+        by_component(displacement), pack
+    )
+
+    def mixed(values, first):
+        scratch = [
+            pltpu.VMEM((plan.positions, 3, 8, lanes), F32),
+            pltpu.VMEM((plan.positions, 3, 8, lanes), F32),
+            pltpu.VMEM((DEG * KL, 8, lanes), F32),
+        ]
+        kernel = mix_kernel
+        if first:
+            kernel = first_mix_kernel
+            scratch.append(pltpu.VMEM((n, plan.rows_in, lanes), F32))
+        return call(
+            functools.partial(kernel, plan, len(low)), "mix", [smem, smem, vmem, vmem], image, scratch
         )(nodes, jnp.asarray(level, jnp.int32), values, mods)
 
-    first_image = everyone(mixed(everyone(msg)))
-    msg, residual_s, update_s = pl.pallas_call(
+    arrived = everyone(msg)
+    flat, parts = array(slab, plan.rows_flat, PLANE), array(3, slots_pad, PLANE)
+    load_flat = call(functools.partial(split_kernel, plan), "split", [vmem], flat, [])(by_component(load))
+    load_flat, nodes, mean_s, mods = lax.optimization_barrier((load_flat, nodes, mean_s, mods))
+    load_flat, arrived = lax.optimization_barrier((load_flat, arrived))
+    load_s = call(functools.partial(load_kernel, plan), "load", [vmem], grid_field, [])(column(load_flat))
+    first_image = everyone(mixed(arrived, True))
+    msg, residual_s, update_s = call(
         functools.partial(middle_kernel, plan),
-        out_shape=(message, grid_field, grid_more),
-        in_specs=[vmem] * 6,
-        out_specs=(vmem,) * 3,
-        scratch_shapes=[wide, narrow, pltpu.VMEM((NX, 3, hs, ls), F32)],
-        compiler_params=params,
-        name="middle",
+        "middle",
+        [vmem] * 6,
+        (message, grid_field, grid_more),
+        [wide, narrow, field_scratch],
     )(first_image, load_s, live_here, mean_s, unpack, pack)
 
-    second_image = everyone(mixed(everyone(msg)))
-    ending = pl.pallas_call(
-        functools.partial(end_kernel, plan),
-        out_shape=jax.ShapeDtypeStruct((slab, plan.rows_end, PLANE), F32),
-        in_specs=[vmem] * 6,
-        out_specs=vmem,
-        scratch_shapes=[
-            wide,
-            narrow,
-            pltpu.VMEM((NX, 3, hs, ls), F32),
-            pltpu.VMEM((NX + 1, 3, hs, ls), F32),
-            pltpu.VMEM((NX, 3, hs, ls), F32),
-        ],
-        compiler_params=params,
-        name="end",
-    )(second_image, residual_s, live_here, mean_s, unpack, update_s)
-    final = lax.all_to_all(ending, "slab", 0, 0, tiled=True)
-
-    def by_slot(values):
-        values = jnp.transpose(values.reshape(slab, 3, sp, PLANE), (0, 2, 1, 3))
-        return values.reshape(slab * sp, 3, PLANE)[:slots_dev]
-
-    start = jnp.where(live_own[:, None, None], displacement, 0.0)
-    return (start + by_slot(final[:, : 3 * sp]), by_slot(final[:, 3 * sp : 6 * sp]))
+    second_image = everyone(mixed(everyone(msg), False))
+    residual_s, residual_flat = call(
+        functools.partial(residual_kernel, plan), "residual", [vmem] * 4, (grid_field, flat), [wide, narrow]
+    )(second_image, residual_s, live_here, unpack)
+    residual = column(residual_flat)
+    update_flat = call(
+        functools.partial(end_kernel, plan), "end", [vmem] * 3, flat, [more_scratch, field_scratch]
+    )(residual_s, mean_s, update_s)
+    residual = call(functools.partial(join_kernel, plan), "join", [vmem], parts, [])(residual)
+    live_pad = jnp.pad(live_own.astype(F32), (0, slots_pad - slots_dev))
+    total = call(functools.partial(add_kernel, plan), "add", [vmem] * 3, parts, [])(
+        column(update_flat), jnp.broadcast_to(live_pad[:, None], (slots_pad, 128))[:, :1], by_component(displacement)
+    )
+    return tuple(jnp.transpose(values, (1, 0, 2))[:slots_dev] for values in (total, residual))
 
 
 def solution(mesh):

time: 207 us -> 182 us (0.88)
  waiting for transfers between devices: 55.2 us -> 26.9 us
  starting transfers between devices: 14.4 us -> 24.8 us
  local copies, waits for them, and re-layouts: 9.02 us -> 3.21 us
  blocking collectives: 65.7 us -> 67.9 us
    all_gather x0 -> x1, blocking collectives: none -> 25.8 us  [per_device(): lax.all_gather(jnp.pad(moduli, ((0, 16 - FIELDS), (0, 0))), 'slab', axis=0)]
    all_to_all x1 -> x0, blocking collectives: 23.1 us -> none  [per_device(): final = lax.all_to_all(ending, 'slab', 0, 0, tiled=True)]
    all_to_all x2, waiting for transfers between devices: 33 us -> 13.7 us  [everyone(): return lax.all_to_all(values, ('chaos', 'slab'), 0, 0, tiled=True)]
    all_to_all x1 -> x3, waiting for transfers between devices: 22.2 us -> 13.3 us  [column(): return lax.all_to_all(values, 'slab', 0, 0, tiled=True)]
    all_to_all x2, starting transfers between devices: 8.07 us -> 13.3 us  [everyone(): return lax.all_to_all(values, ('chaos', 'slab'), 0, 0, tiled=True)]
    all_to_all x1 -> x3, starting transfers between devices: 6.32 us -> 11.5 us  [column(): return lax.all_to_all(values, 'slab', 0, 0, tiled=True)]
    unnamed x18 -> x24, local copies, waits for them, and re-layouts: 6.42 us -> 2.95 us
    pallas_call x5 -> x11, Pallas kernels: 59 us -> 57.1 us  [the longest x2 28.4 us: mixed(): call(functools.partial(kernel, plan, len(low)), 'mix', [smem, smem, vmem,...]
  transfers between devices with their start and end apart: 3 -> 5, of which waited for: 3 -> 3; matrix products, arithmetic and copies ran while one was open for 0% -> 0% of each run, Pallas kernels for 0% -> 15%
where the time goes in v2:
time: 182 us; the launch traced here: 181 us
  blocking collectives  67.9 us (37%)
  Pallas kernels  57.1 us (31%)
  waiting for transfers between devices  26.9 us (15%)
  starting transfers between devices  24.8 us (14%)
  local copies, waits for them, and re-layouts  3.21 us (2%)
    all_to_all x2, blocking collectives, everyone(): return lax.all_to_all(values, ('chaos', 'slab'), 0, 0, tiled=True)  42.1 us
    pallas_call x2, Pallas kernels, mixed(): call(functools.partial(kernel, plan, len(low)), 'mix', [smem, smem, vmem,...  28.4 us
    all_gather x1, blocking collectives, per_device(): lax.all_gather(jnp.pad(moduli, ((0, 16 - FIELDS), (0, 0))), 'slab', axis=0)  25.8 us
    all_to_all x2, waiting for transfers between devices, everyone(): return lax.all_to_all(values, ('chaos', 'slab'), 0, 0, tiled=True)  13.7 us
    all_to_all x2, starting transfers between devices, everyone(): return lax.all_to_all(values, ('chaos', 'slab'), 0, 0, tiled=True)  13.3 us
    all_to_all x3, waiting for transfers between devices, column(): return lax.all_to_all(values, 'slab', 0, 0, tiled=True)  13.3 us
    all_to_all x3, starting transfers between devices, column(): return lax.all_to_all(values, 'slab', 0, 0, tiled=True)  11.5 us
    pallas_call x1, Pallas kernels, per_device(): call(functools.partial(middle_kernel, plan), 'middle', [vmem] * 6, (messa...  10.7 us
  transfers between devices with their start and end apart: 5, of which 3 were waited for; matrix products, arithmetic and copies ran while one was open for 0% of the time, Pallas kernels for 15%

profile of v2, /device:TPU:0, one launch (start us, length us, event | category | flops | bytes accessed | tf_op | source)
XLA Modules:
  0.0 181.1 jit_solution(1379825751059143408)
XLA Ops:
  0.6 1.0 copy-done
  1.6 1.0 copy-done.3
  2.6 2.1 %start.1 = f32[32,48,128]{2,1,0:T(8,128)} custom-call(f32[3,36,768]{2,1,0:T(8,128)S(1)} %bitcast.8, bf16[384,512]{1,0:T(8,128)(2,1)S(1)} %copy-done), custom_call_target="tpu_custom_call" | custom-call | tf_op jit(solution)/shard_map/start/pallas_call | solution.py:525
  4.7 7.3 %all-to-all-start = ((f32[32,48,128]{2,1,0:T(8,128)}), f32[32,48,128]{2,1,0:T(8,128)S(1)}, u32[]{:S(2)}, u32[]{:S(2)}) async-start(f32[32,48,128]{2,1,0:T(8,128)} %start.1), calls=%async_computation | async-start | bytes 1572864 | tf_op jit(solution)/shard_map/all_to_all | solution.py:487
  12.0 0.7 copy-done.10
  12.7 0.8 split.1
  13.6 25.8 %all-gather = f32[64,768]{1,0:T(8,128)S(1)} all-gather(f32[16,768]{1,0:T(8,128)S(1)} %select_maximum_fusion), channel_id=2, replica_groups=mesh['chaos'=8,'slab'=4] {'slab'}, dimensions={0}, use_global_device_ids=true | all-gather | bytes 245760 | tf_op jit(solution)/shard_map/all_gather | solution.py:516
  39.4 0.4 moduli.1
  39.8 0.2 copy-done.9
  40.1 0.2 fusion.nodes_ref
  40.3 4.0 %all-to-all-start.2 = ((f32[4,32,768]{2,1,0:T(8,128)}), f32[4,32,768]{2,1,0:T(8,128)S(1)}, u32[]{:S(2)}, u32[]{:S(2)}) async-start(f32[4,32,768]{2,1,0:T(8,128)} %split.1), calls=%async_computation.2 | async-start | bytes 786432 | tf_op jit(solution)/shard_map/all_to_all | solution.py:490
  44.2 15.2 %mix.2 = f32[32,32,128]{2,1,0:T(8,128)} custom-call(s32[726]{0:T(1024)S(1)} %fusion.nodes_ref, s32[660]{0:T(1024)S(1)} %copy-done.7, f32[32,48,128]{2,1,0:T(8,128)S(1)} %all-to-all-done.msg_ref, f32[11,8,128]{2,1,0:T(8,128)S(1)} %get-tuple-element.20.mods_ref), custom_call_target="tpu_custom_call" | custom-call | tf_op jit(solution)/shard_map/mix/pallas_call | solution.py:539
  59.4 6.0 %all-to-all-start.1 = ((f32[32,32,128]{2,1,0:T(8,128)}), f32[32,32,128]{2,1,0:T(8,128)S(1)}, u32[]{:S(2)}, u32[]{:S(2)}) async-start(f32[32,32,128]{2,1,0:T(8,128)} %mix.2), calls=%async_computation.1 | async-start | bytes 1048576 | tf_op jit(solution)/shard_map/all_to_all | solution.py:487
  65.5 0.1 dynamic-slice_convert_fusion
  65.6 0.1 dynamic_slice.7
  65.6 0.5 load.1.base_ref
  66.2 13.7 %all-to-all-done.1.image_ref = f32[32,32,128]{2,1,0:T(8,128)S(1)} async-done(((f32[32,32,128]{2,1,0:T(8,128)}), f32[32,32,128]{2,1,0:T(8,128)S(1)}, u32[]{:S(2)}, u32[]{:S(2)}) %all-to-all-start.1) | async-done | bytes 524320 | tf_op jit(solution)/shard_map/all_to_all | solution.py:487
  79.8 0.1 broadcast_in_dim.30.live_ref
  79.9 10.7 %middle.1 = (f32[32,48,128]{2,1,0:T(8,128)S(1)}, f32[24,3,16,128]{3,2,1,0:T(8,128)S(1)}, f32[25,3,16,128]{3,2,1,0:T(8,128)S(1)}) custom-call(f32[32,32,128]{2,1,0:T(8,128)S(1)} %all-to-all-done.1.image_ref, f32[24,3,16,128]{3,2,1,0:T(8,128)S(1)} %load.1.base_ref, f32[16,128]{1,0:T(8,128)S(1)} %broadcast_in_dim.30.live_ref, ...), custom_call_target="tpu_custom_call" | custom-call | tf_op jit(solution)/shard_map/middle/pallas_call | solution.py:550
  90.6 23.5 %all_to_all.35.msg_ref = f32[32,48,128]{2,1,0:T(8,128)S(1)} all-to-all(f32[32,48,128]{2,1,0:T(8,128)S(1)} %get-tuple-element.23), channel_id=1, replica_groups=mesh['chaos'=8,'slab'=4] {'chaos','slab'}, dimensions={0} | all-to-all | bytes 1572864 | tf_op jit(solution)/shard_map/all_to_all | solution.py:487
  114.1 13.2 %mix.3 = f32[32,32,128]{2,1,0:T(8,128)S(1)} custom-call(s32[726]{0:T(1024)S(1)} %fusion.nodes_ref, s32[660]{0:T(1024)S(1)} %copy-done.7, f32[32,48,128]{2,1,0:T(8,128)S(1)} %all_to_all.35.msg_ref, f32[11,8,128]{2,1,0:T(8,128)S(1)} %get-tuple-element.20.mods_ref), custom_call_target="tpu_custom_call" | custom-call | tf_op jit(solution)/shard_map/mix/pallas_call | solution.py:539
  127.3 18.5 %all_to_all.36.image_ref = f32[32,32,128]{2,1,0:T(8,128)S(1)} all-to-all(f32[32,32,128]{2,1,0:T(8,128)S(1)} %mix.3), channel_id=1, replica_groups=mesh['chaos'=8,'slab'=4] {'chaos','slab'}, dimensions={0} | all-to-all | bytes 1048576 | tf_op jit(solution)/shard_map/all_to_all | solution.py:487
  145.9 2.2 %residual.1 = (f32[24,3,16,128]{3,2,1,0:T(8,128)S(1)}, f32[4,32,768]{2,1,0:T(8,128)}) custom-call(f32[32,32,128]{2,1,0:T(8,128)S(1)} %all_to_all.36.image_ref, f32[24,3,16,128]{3,2,1,0:T(8,128)S(1)} %get-tuple-element.24.base_ref, f32[16,128]{1,0:T(8,128)S(1)} %broadcast_in_dim.30.live_ref, bf16[512,384]{1,0:T(8,128)(2,1)S(1)} %copy-done.2), custom_call_target="tpu_custom_call" | custom-call | tf_op jit(solution)/shard_map/residual/pallas_call | solution.py:559
  148.1 4.1 %all-to-all-start.6 = ((f32[4,32,768]{2,1,0:T(8,128)}), f32[4,32,768]{2,1,0:T(8,128)S(1)}, u32[]{:S(2)}, u32[]{:S(2)}) async-start(f32[4,32,768]{2,1,0:T(8,128)} %get-tuple-element.27), calls=%async_computation.6 | async-start | bytes 786432 | tf_op jit(solution)/shard_map/all_to_all | solution.py:490
  152.2 10.2 %end.1 = f32[4,32,768]{2,1,0:T(8,128)} custom-call(f32[24,3,16,128]{3,2,1,0:T(8,128)S(1)} %get-tuple-element.25.residual_ref, f32[24,128]{1,0:T(8,128)S(1)} %get-tuple-element.22.mean_ref, f32[25,3,16,128]{3,2,1,0:T(8,128)S(1)} %get-tuple-element.26.before_ref), custom_call_target="tpu_custom_call" | custom-call | tf_op jit(solution)/shard_map/end/pallas_call | solution.py:563
  162.4 2.4 %all-to-all-done.6.in_ref = f32[4,32,768]{2,1,0:T(8,128)S(1)} async-done(((f32[4,32,768]{2,1,0:T(8,128)}), f32[4,32,768]{2,1,0:T(8,128)S(1)}, u32[]{:S(2)}, u32[]{:S(2)}) %all-to-all-start.6) | async-done | bytes 393248 | tf_op jit(solution)/shard_map/all_to_all | solution.py:490
  164.8 3.5 %all-to-all-start.5 = ((f32[4,32,768]{2,1,0:T(8,128)}), f32[4,32,768]{2,1,0:T(8,128)S(1)}, u32[]{:S(2)}, u32[]{:S(2)}) async-start(f32[4,32,768]{2,1,0:T(8,128)} %end.1), calls=%async_computation.5 | async-start | bytes 786432 | tf_op jit(solution)/shard_map/all_to_all | solution.py:490
  168.3 0.1 fusion.1
  168.4 0.1 copy.15.live_ref
  168.5 0.8 join.1
  169.3 10.9 %all-to-all-done.5.in_ref = f32[4,32,768]{2,1,0:T(8,128)S(1)} async-done(((f32[4,32,768]{2,1,0:T(8,128)}), f32[4,32,768]{2,1,0:T(8,128)S(1)}, u32[]{:S(2)}, u32[]{:S(2)}) %all-to-all-start.5) | async-done | bytes 393248 | tf_op jit(solution)/shard_map/all_to_all | solution.py:490
  180.2 0.9 add.17
  (26 shorter events, 0.1 us)
Async XLA Ops:
  0.6 1.0 copy-start
  1.6 1.0 copy-start.3
  4.7 8.0 %copy-start.5 = (f32[36,3,768]{2,0,1:T(8,128)S(1)}, f32[36,3,768]{2,0,1:T(8,128)}, u32[]{:S(2)}) copy-start(f32[36,3,768]{2,0,1:T(8,128)} %param.13) | copy-start | bytes 995332
  4.7 35.6 %all-to-all-start = ((f32[32,48,128]{2,1,0:T(8,128)}), f32[32,48,128]{2,1,0:T(8,128)S(1)}, u32[]{:S(2)}, u32[]{:S(2)}) async-start(f32[32,48,128]{2,1,0:T(8,128)} %start.1), calls=%async_computation | async-start | bytes 1572864 | tf_op jit(solution)/shard_map/all_to_all | solution.py:487
  12.0 0.7 copy-start.10
  12.7 0.8 copy-start.8
  13.5 25.8 %copy-start.6 = (bf16[4,128,128]{2,1,0:T(8,128)(2,1)S(1)}, bf16[4,128,128]{2,1,0:T(8,128)(2,1)}, u32[]{:S(2)}) copy-start(bf16[4,128,128]{2,1,0:T(8,128)(2,1)} %constant.38.clone.mtab_ref) | copy-start | bytes 393220
  39.4 0.7 copy-start.9
  39.4 0.7 copy-start.11
  40.2 4.0 %copy-start.7 = (s32[660]{0:T(1024)S(1)}, s32[660]{0:T(1024)}, u32[]{:S(2)}) copy-start(s32[660]{0:T(1024)} %constant.39.clone.level_ref) | copy-start | bytes 7924
  40.3 19.1 %all-to-all-start.2 = ((f32[4,32,768]{2,1,0:T(8,128)}), f32[4,32,768]{2,1,0:T(8,128)S(1)}, u32[]{:S(2)}, u32[]{:S(2)}) async-start(f32[4,32,768]{2,1,0:T(8,128)} %split.1), calls=%async_computation.2 | async-start | bytes 786432 | tf_op jit(solution)/shard_map/all_to_all | solution.py:490
  59.4 20.4 %all-to-all-start.1 = ((f32[32,32,128]{2,1,0:T(8,128)}), f32[32,32,128]{2,1,0:T(8,128)S(1)}, u32[]{:S(2)}, u32[]{:S(2)}) async-start(f32[32,32,128]{2,1,0:T(8,128)} %mix.2), calls=%async_computation.1 | async-start | bytes 1048576 | tf_op jit(solution)/shard_map/all_to_all | solution.py:487
  65.6 14.3 %copy-start.1 = (bf16[384,512]{1,0:T(8,128)(2,1)S(1)}, bf16[384,512]{1,0:T(8,128)(2,1)}, u32[]{:S(2)}) copy-start(bf16[384,512]{1,0:T(8,128)(2,1)} %constant.36.clone.pack_ref) | copy-start | bytes 1179652
  65.6 14.3 %copy-start.2 = (bf16[512,384]{1,0:T(8,128)(2,1)S(1)}, bf16[512,384]{1,0:T(8,128)(2,1)}, u32[]{:S(2)}) copy-start(bf16[512,384]{1,0:T(8,128)(2,1)} %constant.37.clone.unpack_ref) | copy-start | bytes 1179652
  148.1 16.7 %all-to-all-start.6 = ((f32[4,32,768]{2,1,0:T(8,128)}), f32[4,32,768]{2,1,0:T(8,128)S(1)}, u32[]{:S(2)}, u32[]{:S(2)}) async-start(f32[4,32,768]{2,1,0:T(8,128)} %get-tuple-element.27), calls=%async_computation.6 | async-start | bytes 786432 | tf_op jit(solution)/shard_map/all_to_all | solution.py:490
  164.8 15.3 %all-to-all-start.5 = ((f32[4,32,768]{2,1,0:T(8,128)}), f32[4,32,768]{2,1,0:T(8,128)S(1)}, u32[]{:S(2)}, u32[]{:S(2)}) async-start(f32[4,32,768]{2,1,0:T(8,128)} %end.1), calls=%async_computation.5 | async-start | bytes 786432 | tf_op jit(solution)/shard_map/all_to_all | solution.py:490
  168.5 11.7 %copy-start.4 = (f32[36,3,768]{2,0,1:T(8,128)S(1)}, f32[36,3,768]{2,0,1:T(8,128)}, u32[]{:S(2)}) copy-start(f32[36,3,768]{2,0,1:T(8,128)} %param.12) | copy-start | bytes 995332

commit v3 on v2

--- a/solution.py
+++ b/solution.py
@@ -236,11 +236,12 @@
 
 
 def moduli_kernel(plan, tile_ref, in_ref, mtab_ref, mean_ref, mods_ref, fields):
+    from_plane = [lax.rem(tile_ref[1] + (plan.nz - z), plan.nz) for z in range(plan.nz)]
     fields[0] = jnp.zeros((16, plan.ls), F32)
     fields[NX + 1] = jnp.zeros((16, plan.ls), F32)
     for a in range(PLANE // 128):
         pieces = rows_at(
-            swap_quarters([in_ref[4 * t + i, :, a * 128 : (a + 1) * 128] for i in range(4)])
+            swap_quarters([in_ref[from_plane[4 * t + i], :, a * 128 : (a + 1) * 128] for i in range(4)])
             for t in range(plan.nz // 4)
         )
         for b, piece in enumerate(pieces):
@@ -271,7 +272,7 @@
             out_ref[row * plan.slab + group] = total
         return carry
 
-    lax.fori_loop(0, plan.chaos, one, 0)
+    lax.fori_loop(0, plan.chaos, one, 0, unroll=4)
 
 
 def first_mix_kernel(plan, low_count, nodes_ref, level_ref, msg_ref, mods_ref, out_ref, grad, flux, scaled, regroup):
@@ -292,22 +293,21 @@
     mean = mods_ref[0]
 
     def gradients(source, carry):
-        for s in range(sp):
-            own = msg_ref[source, s * rx : s * rx + 8, :]
-            slope_x = pltpu.roll(own, 7, 0) - own
-            slope_y = pltpu.roll(own, lanes - 1, 1) - own
-            slope_z = jnp.where(not_top, pltpu.roll(own, lanes - ry, 1), 0.0) - own
-            spread = slope_x + pltpu.roll(slope_y, lanes - segment, 1) + pltpu.roll(slope_z, lanes - 2 * segment, 1)
-            full_x = slope_x + jnp.where(is_x, spread, 0.0)
-            full_y = slope_y + jnp.where(is_y, pltpu.roll(spread, segment, 1), 0.0)
-            full_z = slope_z + jnp.where(is_z, pltpu.roll(spread, 2 * segment, 1), 0.0)
-            at = source * sp + s
-            for d, full in enumerate((full_x, full_y, full_z)):
-                grad[at, d] = full
-                flux[at, d] = mean * full
+        own = jnp.stack([msg_ref[source, s * rx : s * rx + 8, :] for s in range(sp)])
+        slope_x = pltpu.roll(own, 7, 1) - own
+        slope_y = pltpu.roll(own, lanes - 1, 2) - own
+        slope_z = jnp.where(not_top, pltpu.roll(own, lanes - ry, 2), 0.0) - own
+        spread = slope_x + pltpu.roll(slope_y, lanes - segment, 2) + pltpu.roll(slope_z, lanes - 2 * segment, 2)
+        full_x = slope_x + jnp.where(is_x, spread, 0.0)
+        full_y = slope_y + jnp.where(is_y, pltpu.roll(spread, segment, 2), 0.0)
+        full_z = slope_z + jnp.where(is_z, pltpu.roll(spread, 2 * segment, 2), 0.0)
+        here = pl.ds(source * sp, sp)
+        for d, full in enumerate((full_x, full_y, full_z)):
+            grad[here, d] = full
+            flux[here, d] = mean * full
         return carry
 
-    lax.fori_loop(0, plan.n, gradients, 0)
+    lax.fori_loop(0, plan.n, gradients, 0, unroll=4)
 
     def edges(number, carry):
         base = nodes_ref[number]
@@ -328,19 +328,19 @@
             flux[base, d] = total[d]
         return carry
 
-    lax.fori_loop(0, low_count, edges, 0)
+    lax.fori_loop(0, low_count, edges, 0, unroll=2)
 
     def divergences(source, carry):
+        here = pl.ds(source * sp, sp)
+        flux_x, flux_y, flux_z = (flux[here, d] for d in range(3))
+        total = flux_x - pltpu.roll(flux_x, 1, 1)
+        total = total + (flux_y - pltpu.roll(flux_y, 1, 2))
+        total = total + (flux_z - jnp.where(not_bottom, pltpu.roll(flux_z, ry, 2), 0.0))
         for s in range(sp):
-            at = source * sp + s
-            flux_x, flux_y, flux_z = (flux[at, d] for d in range(3))
-            total = flux_x - pltpu.roll(flux_x, 1, 0)
-            total = total + (flux_y - pltpu.roll(flux_y, 1, 1))
-            total = total + (flux_z - jnp.where(not_bottom, pltpu.roll(flux_z, ry, 1), 0.0))
-            out_ref[source, s * plan.tx : (s + 1) * plan.tx, :] = total[1 : 1 + plan.tx]
+            out_ref[source, s * plan.tx : (s + 1) * plan.tx, :] = total[s, 1 : 1 + plan.tx]
         return carry
 
-    lax.fori_loop(0, plan.n, divergences, 0)
+    lax.fori_loop(0, plan.n, divergences, 0, unroll=2)
 
 
 def unpack_image(plan, image_ref, unpack_ref, lhs, rows):
@@ -363,7 +363,7 @@
             residual_ref[x, c] = jnp.where(live, base_ref[x, c] + image, 0.0)
         return carry
 
-    lax.fori_loop(0, NX, one, 0)
+    lax.fori_loop(0, NX, one, 0, unroll=6)
 
 
 def smooth(plan, mean_ref, residual_ref, update, step):
@@ -383,7 +383,7 @@
             step[x, c] = scaled
         return carry
 
-    lax.fori_loop(0, NX, first, 0)
+    lax.fori_loop(0, NX, first, 0, unroll=6)
     for c in range(3):
         update[NX, c] = jnp.zeros((hs, ls), F32)
 
@@ -416,7 +416,7 @@
             return (*through, *ahead)
 
         zero = jnp.zeros((hs, ls), F32)
-        lax.fori_loop(0, NX, slab_of, (zero, zero, zero, *(update[0, c] for c in range(3))), unroll=2)
+        lax.fori_loop(0, NX, slab_of, (zero, zero, zero, *(update[0, c] for c in range(3))), unroll=6)
         rho_prev = rho_next
 
 
@@ -476,7 +476,7 @@
     pack = jnp.asarray(plan.pack_table(), BF16)
     unpack = jnp.asarray(plan.unpack_table(), BF16)
     mtab = jnp.asarray(plan.modulus_table(), BF16)
-    tile = (at_chaos * slab + at_slab).astype(jnp.int32).reshape(1)
+    tile = jnp.stack([at_chaos * slab + at_slab, at_slab]).astype(jnp.int32)
 
     slots_pad = slab * sp
 
@@ -513,7 +513,10 @@
     field_scratch, more_scratch = pltpu.VMEM(grid_field.shape, F32), pltpu.VMEM(grid_more.shape, F32)
 
     moduli = jnp.concatenate([mean_modulus[None], modes], axis=0)
-    moduli = lax.all_gather(jnp.pad(moduli, ((0, 16 - FIELDS), (0, 0))), "slab", axis=0)
+    moduli = jnp.pad(moduli, ((0, 16 - FIELDS), (0, 0)))
+    moduli = jnp.stack(
+        [moduli] + [lax.ppermute(moduli, "slab", [(z, (z + step) % slab) for z in range(slab)]) for step in range(1, slab)]
+    )
     mean_s, mods = call(
         functools.partial(moduli_kernel, plan),
         "moduli",

time: 182 us -> 164 us (0.901)
  blocking collectives: 67.9 us -> 42 us
  waiting for transfers between devices: 26.9 us -> 49.9 us
  Pallas kernels: 57.1 us -> 38.2 us
  starting transfers between devices: 24.8 us -> 27.8 us
    all_gather x1 -> x0, blocking collectives: 25.8 us -> none  [per_device(): lax.all_gather(jnp.pad(moduli, ((0, 16 - FIELDS), (0, 0))), 'slab', axis=0)]
    ppermute x0 -> x3, waiting for transfers between devices: none -> 16.8 us  [per_device(): lax.ppermute(moduli, 'slab', [(z, (z + step) % slab) for z in range(slab)])]
    pallas_call x2, Pallas kernels: 28.4 us -> 17 us  [mixed(): call(functools.partial(kernel, plan, len(low)), 'mix', [smem, smem, vmem,...]
    all_to_all x3, waiting for transfers between devices: 13.3 us -> 19.5 us  [column(): return lax.all_to_all(values, 'slab', 0, 0, tiled=True)]
    ppermute x0 -> x3, starting transfers between devices: none -> 5.65 us  [per_device(): lax.ppermute(moduli, 'slab', [(z, (z + step) % slab) for z in range(slab)])]
    pallas_call x1, Pallas kernels: 10.2 us -> 6.24 us  [per_device(): call(functools.partial(end_kernel, plan), 'end', [vmem] * 3, flat, [more_...]
    pallas_call x1, Pallas kernels: 10.7 us -> 6.75 us  [per_device(): call(functools.partial(middle_kernel, plan), 'middle', [vmem] * 6, (messa...]
    all_to_all x2, starting transfers between devices: 13.3 us -> 11 us  [everyone(): return lax.all_to_all(values, ('chaos', 'slab'), 0, 0, tiled=True)]
  transfers between devices with their start and end apart: 5 -> 8, of which waited for: 3 -> 6; matrix products, arithmetic and copies ran while one was open for 0% -> 0% of each run, Pallas kernels for 15% -> 11%
where the time goes in v3:
time: 164 us; the launch traced here: 163 us
  waiting for transfers between devices  49.9 us (30%)
  blocking collectives  42 us (26%)
  Pallas kernels  38.2 us (23%)
  starting transfers between devices  27.8 us (17%)
  local copies, waits for them, and re-layouts  3.84 us (2%)
    all_to_all x2, blocking collectives, everyone(): return lax.all_to_all(values, ('chaos', 'slab'), 0, 0, tiled=True)  42 us
    all_to_all x3, waiting for transfers between devices, column(): return lax.all_to_all(values, 'slab', 0, 0, tiled=True)  19.5 us
    pallas_call x2, Pallas kernels, mixed(): call(functools.partial(kernel, plan, len(low)), 'mix', [smem, smem, vmem,...  17 us
    ppermute x3, waiting for transfers between devices, per_device(): lax.ppermute(moduli, 'slab', [(z, (z + step) % slab) for z in range(slab)])  16.8 us
    all_to_all x2, waiting for transfers between devices, everyone(): return lax.all_to_all(values, ('chaos', 'slab'), 0, 0, tiled=True)  13.7 us
    all_to_all x3, starting transfers between devices, column(): return lax.all_to_all(values, 'slab', 0, 0, tiled=True)  11.1 us
    all_to_all x2, starting transfers between devices, everyone(): return lax.all_to_all(values, ('chaos', 'slab'), 0, 0, tiled=True)  11 us
    pallas_call x1, Pallas kernels, per_device(): call(functools.partial(middle_kernel, plan), 'middle', [vmem] * 6, (messa...  6.75 us
  transfers between devices with their start and end apart: 8, of which 6 were waited for; matrix products, arithmetic and copies ran while one was open for 0% of the time, Pallas kernels for 11%

profile of v3, /device:TPU:0, one launch (start us, length us, event | category | flops | bytes accessed | tf_op | source)
XLA Modules:
  0.0 163.0 jit_solution(4924797201158557569)
XLA Ops:
  0.6 1.0 copy-done
  1.6 1.0 copy-done.3
  2.6 2.1 %start.1 = f32[32,48,128]{2,1,0:T(8,128)} custom-call(f32[3,36,768]{2,1,0:T(8,128)S(1)} %bitcast.13, bf16[384,512]{1,0:T(8,128)(2,1)S(1)} %copy-done), custom_call_target="tpu_custom_call" | custom-call | tf_op jit(solution)/shard_map/start/pallas_call | solution.py:528
  4.7 7.3 %all-to-all-start = ((f32[32,48,128]{2,1,0:T(8,128)}), f32[32,48,128]{2,1,0:T(8,128)S(1)}, u32[]{:S(2)}, u32[]{:S(2)}) async-start(f32[32,48,128]{2,1,0:T(8,128)} %start.1), calls=%async_computation | async-start | bytes 1572864 | tf_op jit(solution)/shard_map/all_to_all | solution.py:487
  12.0 1.8 %collective-permute-start = (f32[16,768]{1,0:T(8,128)S(1)}, f32[16,768]{1,0:T(8,128)S(1)}, u32[]{:S(2)}, u32[]{:S(2)}) collective-permute-start(f32[16,768]{1,0:T(8,128)S(1)} %select_maximum_fusion), channel_id=1, source_target_pairs={{0,1},{1,2},{2,3},{3,0},{4,5},{5,6},{6,7},{7,4},{8,9},{9,10},{10,1... | collective-permute-start | bytes 147464 | tf_op jit(solution)/shard_map/ppermute | solution.py:518
  13.9 2.4 %collective-permute-start.1 = (f32[16,768]{1,0:T(8,128)S(1)}, f32[16,768]{1,0:T(8,128)S(1)}, u32[]{:S(2)}, u32[]{:S(2)}) collective-permute-start(f32[16,768]{1,0:T(8,128)S(1)} %select_maximum_fusion), channel_id=1, source_target_pairs={{0,2},{1,3},{2,0},{3,1},{4,6},{5,7},{6,4},{7,5},{8,10},{9,11},{10,... | collective-permute-start | bytes 147464 | tf_op jit(solution)/shard_map/ppermute | solution.py:518
  16.3 1.4 collective-permute-start.2
  17.7 0.7 copy-done.9
  18.4 0.2 fusion.nodes_ref
  18.6 0.8 split.1
  19.5 11.4 %collective-permute-done = f32[16,768]{1,0:T(8,128)S(1)} collective-permute-done((f32[16,768]{1,0:T(8,128)S(1)}, f32[16,768]{1,0:T(8,128)S(1)}, u32[]{:S(2)}, u32[]{:S(2)}) %collective-permute-start) | collective-permute-done | bytes 49184 | tf_op jit(solution)/shard_map/ppermute | solution.py:518
  30.9 5.4 %collective-permute-done.1 = f32[16,768]{1,0:T(8,128)S(1)} collective-permute-done((f32[16,768]{1,0:T(8,128)S(1)}, f32[16,768]{1,0:T(8,128)S(1)}, u32[]{:S(2)}, u32[]{:S(2)}) %collective-permute-start.1) | collective-permute-done | bytes 49184 | tf_op jit(solution)/shard_map/ppermute | solution.py:518
  36.3 0.9 copy-done.6
  37.1 1.0 moduli.1
  38.2 3.6 %all-to-all-start.2 = ((f32[4,32,768]{2,1,0:T(8,128)}), f32[4,32,768]{2,1,0:T(8,128)S(1)}, u32[]{:S(2)}, u32[]{:S(2)}) async-start(f32[4,32,768]{2,1,0:T(8,128)} %split.1), calls=%async_computation.2 | async-start | bytes 786432 | tf_op jit(solution)/shard_map/all_to_all | solution.py:490
  41.8 9.3 %mix.2 = f32[32,32,128]{2,1,0:T(8,128)} custom-call(s32[726]{0:T(1024)S(1)} %fusion.nodes_ref, s32[660]{0:T(1024)S(1)} %copy-done.7, f32[32,48,128]{2,1,0:T(8,128)S(1)} %all-to-all-done.msg_ref, f32[11,8,128]{2,1,0:T(8,128)S(1)} %get-tuple-element.20.mods_ref), custom_call_target="tpu_custom_call" | custom-call | tf_op jit(solution)/shard_map/mix/pallas_call | solution.py:542
  51.0 2.3 %all-to-all-done.2.in_ref = f32[4,32,768]{2,1,0:T(8,128)S(1)} async-done(((f32[4,32,768]{2,1,0:T(8,128)}), f32[4,32,768]{2,1,0:T(8,128)S(1)}, u32[]{:S(2)}, u32[]{:S(2)}) %all-to-all-start.2) | async-done | bytes 393248 | tf_op jit(solution)/shard_map/all_to_all | solution.py:490
  53.3 3.7 %all-to-all-start.1 = ((f32[32,32,128]{2,1,0:T(8,128)}), f32[32,32,128]{2,1,0:T(8,128)S(1)}, u32[]{:S(2)}, u32[]{:S(2)}) async-start(f32[32,32,128]{2,1,0:T(8,128)} %mix.2), calls=%async_computation.1 | async-start | bytes 1048576 | tf_op jit(solution)/shard_map/all_to_all | solution.py:487
  57.2 0.5 load.1.base_ref
  57.7 13.7 %all-to-all-done.1.image_ref = f32[32,32,128]{2,1,0:T(8,128)S(1)} async-done(((f32[32,32,128]{2,1,0:T(8,128)}), f32[32,32,128]{2,1,0:T(8,128)S(1)}, u32[]{:S(2)}, u32[]{:S(2)}) %all-to-all-start.1) | async-done | bytes 524320 | tf_op jit(solution)/shard_map/all_to_all | solution.py:487
  71.5 6.7 %middle.1 = (f32[32,48,128]{2,1,0:T(8,128)S(1)}, f32[24,3,16,128]{3,2,1,0:T(8,128)S(1)}, f32[25,3,16,128]{3,2,1,0:T(8,128)S(1)}) custom-call(f32[32,32,128]{2,1,0:T(8,128)S(1)} %all-to-all-done.1.image_ref, f32[24,3,16,128]{3,2,1,0:T(8,128)S(1)} %load.1.base_ref, f32[16,128]{1,0:T(8,128)S(1)} %broadcast_in_dim.30.live_ref, ...), custom_call_target="tpu_custom_call" | custom-call | tf_op jit(solution)/shard_map/middle/pallas_call | solution.py:553
  78.2 23.5 %all_to_all.35.msg_ref = f32[32,48,128]{2,1,0:T(8,128)S(1)} all-to-all(f32[32,48,128]{2,1,0:T(8,128)S(1)} %get-tuple-element.23), channel_id=1, replica_groups=mesh['chaos'=8,'slab'=4] {'chaos','slab'}, dimensions={0} | all-to-all | bytes 1572864 | tf_op jit(solution)/shard_map/all_to_all | solution.py:487
  101.7 7.7 %mix.3 = f32[32,32,128]{2,1,0:T(8,128)S(1)} custom-call(s32[726]{0:T(1024)S(1)} %fusion.nodes_ref, s32[660]{0:T(1024)S(1)} %copy-done.7, f32[32,48,128]{2,1,0:T(8,128)S(1)} %all_to_all.35.msg_ref, f32[11,8,128]{2,1,0:T(8,128)S(1)} %get-tuple-element.20.mods_ref), custom_call_target="tpu_custom_call" | custom-call | tf_op jit(solution)/shard_map/mix/pallas_call | solution.py:542
  109.4 18.5 %all_to_all.36.image_ref = f32[32,32,128]{2,1,0:T(8,128)S(1)} all-to-all(f32[32,32,128]{2,1,0:T(8,128)S(1)} %mix.3), channel_id=1, replica_groups=mesh['chaos'=8,'slab'=4] {'chaos','slab'}, dimensions={0} | all-to-all | bytes 1048576 | tf_op jit(solution)/shard_map/all_to_all | solution.py:487
  128.0 2.1 %residual.1 = (f32[24,3,16,128]{3,2,1,0:T(8,128)S(1)}, f32[4,32,768]{2,1,0:T(8,128)}) custom-call(f32[32,32,128]{2,1,0:T(8,128)S(1)} %all_to_all.36.image_ref, f32[24,3,16,128]{3,2,1,0:T(8,128)S(1)} %get-tuple-element.24.base_ref, f32[16,128]{1,0:T(8,128)S(1)} %broadcast_in_dim.30.live_ref, bf16[512,384]{1,0:T(8,128)(2,1)S(1)} %copy-done.2), custom_call_target="tpu_custom_call" | custom-call | tf_op jit(solution)/shard_map/residual/pallas_call | solution.py:562
  130.1 4.1 %all-to-all-start.6 = ((f32[4,32,768]{2,1,0:T(8,128)}), f32[4,32,768]{2,1,0:T(8,128)S(1)}, u32[]{:S(2)}, u32[]{:S(2)}) async-start(f32[4,32,768]{2,1,0:T(8,128)} %get-tuple-element.27), calls=%async_computation.6 | async-start | bytes 786432 | tf_op jit(solution)/shard_map/all_to_all | solution.py:490
  134.2 6.2 %end.1 = f32[4,32,768]{2,1,0:T(8,128)} custom-call(f32[24,3,16,128]{3,2,1,0:T(8,128)S(1)} %get-tuple-element.25.residual_ref, f32[24,128]{1,0:T(8,128)S(1)} %get-tuple-element.22.mean_ref, f32[25,3,16,128]{3,2,1,0:T(8,128)S(1)} %get-tuple-element.26.before_ref), custom_call_target="tpu_custom_call" | custom-call | tf_op jit(solution)/shard_map/end/pallas_call | solution.py:566
  140.4 6.4 %all-to-all-done.6.in_ref = f32[4,32,768]{2,1,0:T(8,128)S(1)} async-done(((f32[4,32,768]{2,1,0:T(8,128)}), f32[4,32,768]{2,1,0:T(8,128)S(1)}, u32[]{:S(2)}, u32[]{:S(2)}) %all-to-all-start.6) | async-done | bytes 393248 | tf_op jit(solution)/shard_map/all_to_all | solution.py:490
  146.8 3.5 %all-to-all-start.5 = ((f32[4,32,768]{2,1,0:T(8,128)}), f32[4,32,768]{2,1,0:T(8,128)S(1)}, u32[]{:S(2)}, u32[]{:S(2)}) async-start(f32[4,32,768]{2,1,0:T(8,128)} %end.1), calls=%async_computation.5 | async-start | bytes 786432 | tf_op jit(solution)/shard_map/all_to_all | solution.py:490
  150.5 0.8 join.1
  151.3 10.8 %all-to-all-done.5.in_ref = f32[4,32,768]{2,1,0:T(8,128)S(1)} async-done(((f32[4,32,768]{2,1,0:T(8,128)}), f32[4,32,768]{2,1,0:T(8,128)S(1)}, u32[]{:S(2)}, u32[]{:S(2)}) %all-to-all-start.5) | async-done | bytes 393248 | tf_op jit(solution)/shard_map/all_to_all | solution.py:490
  162.1 0.9 add.19
  (34 shorter events, 0.6 us)
Async XLA Ops:
  0.6 1.0 copy-start
  1.6 1.0 copy-start.3
  4.7 7.3 %copy-start.10 = (f32[768]{0:T(1024)S(1)}, f32[768]{0:T(1024)}, u32[]{:S(2)}) copy-start(f32[768]{0:T(1024)} %param.14) | copy-start | bytes 9220
  4.7 7.3 %copy-start.8 = (f32[10,768]{1,0:T(8,128)S(1)}, f32[10,768]{1,0:T(8,128)}, u32[]{:S(2)}) copy-start(f32[10,768]{1,0:T(8,128)} %param.15) | copy-start | bytes 92164
  4.7 14.0 %copy-start.5 = (f32[36,3,768]{2,0,1:T(8,128)S(1)}, f32[36,3,768]{2,0,1:T(8,128)}, u32[]{:S(2)}) copy-start(f32[36,3,768]{2,0,1:T(8,128)} %param.13) | copy-start | bytes 995332
  4.7 33.5 %all-to-all-start = ((f32[32,48,128]{2,1,0:T(8,128)}), f32[32,48,128]{2,1,0:T(8,128)S(1)}, u32[]{:S(2)}, u32[]{:S(2)}) async-start(f32[32,48,128]{2,1,0:T(8,128)} %start.1), calls=%async_computation | async-start | bytes 1572864 | tf_op jit(solution)/shard_map/all_to_all | solution.py:487
  12.0 18.8 %collective-permute-start = (f32[16,768]{1,0:T(8,128)S(1)}, f32[16,768]{1,0:T(8,128)S(1)}, u32[]{:S(2)}, u32[]{:S(2)}) collective-permute-start(f32[16,768]{1,0:T(8,128)S(1)} %select_maximum_fusion), channel_id=1, source_target_pairs={{0,1},{1,2},{2,3},{3,0},{4,5},{5,6},{6,7},{7,4},{8,9},{9,10},{10,1... | collective-permute-start | bytes 147464 | tf_op jit(solution)/shard_map/ppermute | solution.py:518
  13.9 22.4 %collective-permute-start.1 = (f32[16,768]{1,0:T(8,128)S(1)}, f32[16,768]{1,0:T(8,128)S(1)}, u32[]{:S(2)}, u32[]{:S(2)}) collective-permute-start(f32[16,768]{1,0:T(8,128)S(1)} %select_maximum_fusion), channel_id=1, source_target_pairs={{0,2},{1,3},{2,0},{3,1},{4,6},{5,7},{6,4},{7,5},{8,10},{9,11},{10,... | collective-permute-start | bytes 147464 | tf_op jit(solution)/shard_map/ppermute | solution.py:518
  16.3 20.0 %collective-permute-start.2 = (f32[16,768]{1,0:T(8,128)S(1)}, f32[16,768]{1,0:T(8,128)S(1)}, u32[]{:S(2)}, u32[]{:S(2)}) collective-permute-start(f32[16,768]{1,0:T(8,128)S(1)} %select_maximum_fusion), channel_id=1, source_target_pairs={{0,3},{1,0},{2,1},{3,2},{4,7},{5,4},{6,5},{7,6},{8,11},{9,8},{10,9... | collective-permute-start | bytes 147464 | tf_op jit(solution)/shard_map/ppermute | solution.py:518
  17.7 0.7 copy-start.9
  17.7 0.7 copy-start.11
  36.2 0.9 copy-start.6
  38.1 3.6 %copy-start.7 = (s32[660]{0:T(1024)S(1)}, s32[660]{0:T(1024)}, u32[]{:S(2)}) copy-start(s32[660]{0:T(1024)} %constant.39.clone.level_ref) | copy-start | bytes 7924
  38.2 15.1 %all-to-all-start.2 = ((f32[4,32,768]{2,1,0:T(8,128)}), f32[4,32,768]{2,1,0:T(8,128)S(1)}, u32[]{:S(2)}, u32[]{:S(2)}) async-start(f32[4,32,768]{2,1,0:T(8,128)} %split.1), calls=%async_computation.2 | async-start | bytes 786432 | tf_op jit(solution)/shard_map/all_to_all | solution.py:490
  53.3 18.1 %all-to-all-start.1 = ((f32[32,32,128]{2,1,0:T(8,128)}), f32[32,32,128]{2,1,0:T(8,128)S(1)}, u32[]{:S(2)}, u32[]{:S(2)}) async-start(f32[32,32,128]{2,1,0:T(8,128)} %mix.2), calls=%async_computation.1 | async-start | bytes 1048576 | tf_op jit(solution)/shard_map/all_to_all | solution.py:487
  57.2 14.3 %copy-start.1 = (bf16[384,512]{1,0:T(8,128)(2,1)S(1)}, bf16[384,512]{1,0:T(8,128)(2,1)}, u32[]{:S(2)}) copy-start(bf16[384,512]{1,0:T(8,128)(2,1)} %constant.36.clone.pack_ref) | copy-start | bytes 1179652
  57.2 14.3 %copy-start.2 = (bf16[512,384]{1,0:T(8,128)(2,1)S(1)}, bf16[512,384]{1,0:T(8,128)(2,1)}, u32[]{:S(2)}) copy-start(bf16[512,384]{1,0:T(8,128)(2,1)} %constant.37.clone.unpack_ref) | copy-start | bytes 1179652
  130.1 16.7 %all-to-all-start.6 = ((f32[4,32,768]{2,1,0:T(8,128)}), f32[4,32,768]{2,1,0:T(8,128)S(1)}, u32[]{:S(2)}, u32[]{:S(2)}) async-start(f32[4,32,768]{2,1,0:T(8,128)} %get-tuple-element.27), calls=%async_computation.6 | async-start | bytes 786432 | tf_op jit(solution)/shard_map/all_to_all | solution.py:490
  146.8 15.3 %all-to-all-start.5 = ((f32[4,32,768]{2,1,0:T(8,128)}), f32[4,32,768]{2,1,0:T(8,128)S(1)}, u32[]{:S(2)}, u32[]{:S(2)}) async-start(f32[4,32,768]{2,1,0:T(8,128)} %end.1), calls=%async_computation.5 | async-start | bytes 786432 | tf_op jit(solution)/shard_map/all_to_all | solution.py:490
  150.5 11.6 %copy-start.4 = (f32[36,3,768]{2,0,1:T(8,128)S(1)}, f32[36,3,768]{2,0,1:T(8,128)}, u32[]{:S(2)}) copy-start(f32[36,3,768]{2,0,1:T(8,128)} %param.12) | copy-start | bytes 995332

commit v4 on v3

--- a/solution.py
+++ b/solution.py
@@ -78,7 +78,10 @@
         self.ry = self.ty + 2
         self.nxb, self.nyb = NX // self.tx, NY // self.ty
         self.rows_out = up8(self.sp * self.tx)
-        self.rows_flat = up8(3 * self.sp)
+        self.rows_flat = up8(3 * self.sp + 1)
+        self.rows_end = up8(6 * self.sp)
+        self.shares = -(-FIELDS // min(chaos, 16))
+        self.per_share = 16 // self.shares
         self.positions = self.n * self.sp
 
     def pack_table(self):
@@ -152,6 +155,56 @@
 
 def strided(start, size, step):
     return pl.ds(start, size) if size == 1 or step == 1 else pl.ds(start, size, stride=step)
+
+
+def store_moduli(plan, chaos_at, moduli_ref, msg_ref):
+    quarter = lax.broadcasted_iota(jnp.int32, (1, 128), 1) // NY
+    own = [moduli_ref[pl.ds(share * plan.per_share + chaos_at, 1), :] for share in range(plan.shares)]
+    count, first = plan.shares * plan.rx, plan.sp * plan.rx
+    for xb in range(plan.nxb):
+        for start in range(0, count, 4):
+            line = jnp.zeros((1, 128), F32)
+            for number in range(start, min(count, start + 4)):
+                share, k = divmod(number, plan.rx)
+                x = xb * plan.tx - 1 + k
+                if 0 <= x < NX:
+                    piece = own[share][:, x // 4 * 128 : (x // 4 + 1) * 128]
+                    turned = pltpu.roll(piece, (number - x) % 4 * NY, 1)
+                    line = jnp.where(quarter == number % 4, turned, line)
+            row, column = divmod(start // 4, plan.lanes // 128)
+            for yb in range(plan.nyb):
+                tile = xb * plan.nyb + yb
+                msg_ref[tile, first + row : first + row + 1, column * 128 : (column + 1) * 128] = line
+
+
+def gather_moduli(plan, tile_at, msg_ref, mtab_ref, mods_ref):
+    quarter = lax.broadcasted_iota(jnp.int32, (plan.per_share, 128), 1) // NY
+    first, rows = plan.sp * plan.rx, plan.rows_in
+    table = mtab_ref[lax.rem(tile_at, plan.nyb)]
+    mods_ref[...] = jnp.zeros(mods_ref.shape, F32)
+    for share in range(plan.shares):
+        lines = []
+        for k in range(plan.rx):
+            number = share * plan.rx + k
+            row, column = divmod(number // 4, plan.lanes // 128)
+            parts = []
+            for t in range(plan.nz // 4):
+                total = jnp.zeros((plan.per_share, 128), F32)
+                for i in range(4):
+                    at, columns = (4 * t + i) * rows + first + row, slice(column * 128, (column + 1) * 128)
+                    if plan.lanes == 128:
+                        piece = msg_ref[pl.ds(at, plan.per_share, stride=plan.slab * rows), columns]
+                    else:
+                        lone = [at + j * plan.slab * rows for j in range(plan.per_share)]
+                        piece = jnp.concatenate([msg_ref[j : j + 1, columns] for j in lone], axis=0)
+                    total = jnp.where(quarter == i, pltpu.roll(piece, (i - number) % 4 * NY, 1), total)
+                parts.append(total)
+            lines.append(parts[0] if len(parts) == 1 else jnp.concatenate(parts, axis=1))
+        here = picked(jnp.concatenate(lines, axis=0), table)
+        for k in range(plan.rx):
+            for v in range(min(plan.per_share, FIELDS - share * plan.per_share)):
+                at = k * plan.per_share + v
+                mods_ref[share * plan.per_share + v, k : k + 1, :] = here[at : at + 1]
 
 
 def store_message(plan, rows_ref, msg_ref):
@@ -177,7 +230,10 @@
     return [jnp.concatenate(pieces, axis=1) if len(pieces) > 1 else pieces[0] for pieces in zip(*piece_of)]
 
 
-def start_kernel(plan, in_ref, pack_ref, msg_ref, lhs, rows):
+def start_kernel(plan, place_ref, in_ref, mean_ref, modes_ref, pack_ref, msg_ref, lhs, rows, moduli):
+    moduli[...] = jnp.zeros(moduli.shape, F32)
+    moduli[0:1] = mean_ref[...]
+    moduli[1:FIELDS] = modes_ref[...]
     for a in range(PLANE // 128):
         for c in range(3):
             pieces = rows_at(
@@ -194,18 +250,28 @@
                 lhs[x * plan.hs : x * plan.hs + plan.sp, c * plan.ls : (c + 1) * plan.ls] = piece
     pick_into(rows, lhs, pack_ref)
     store_message(plan, rows, msg_ref)
-
-
-def split_kernel(plan, in_ref, out_ref):
+    store_moduli(plan, jnp.minimum(place_ref[0], plan.per_share - 1), moduli, msg_ref)
+
+
+def split_kernel(plan, in_ref, mean_ref, out_ref):
     for group in range(plan.slab):
+        out_ref[group, 3 * plan.sp : 3 * plan.sp + 1, :] = mean_ref[...]
         for c in range(3):
             out_ref[group, c * plan.sp : (c + 1) * plan.sp, :] = in_ref[
                 c, group * plan.sp : (group + 1) * plan.sp, :
             ]
 
 
-def load_kernel(plan, in_ref, out_ref):
+def load_kernel(plan, in_ref, out_ref, mean_ref):
     for a in range(PLANE // 128):
+        pieces = rows_at(
+            swap_quarters(
+                [in_ref[4 * t + i, 3 * plan.sp : 3 * plan.sp + 1, a * 128 : (a + 1) * 128] for i in range(4)]
+            )
+            for t in range(plan.nz // 4)
+        )
+        for b, piece in enumerate(pieces):
+            mean_ref[4 * a + b : 4 * a + b + 1, :] = piece
         for c in range(3):
             pieces = rows_at(
                 swap_quarters(
@@ -217,44 +283,15 @@
                 out_ref[4 * a + b, c, 0 : plan.sp, :] = piece
 
 
-def join_kernel(plan, in_ref, out_ref):
-    for group in range(plan.slab):
-        for c in range(3):
-            out_ref[c, group * plan.sp : (group + 1) * plan.sp, :] = in_ref[
-                group, c * plan.sp : (c + 1) * plan.sp, :
-            ]
-
-
-def add_kernel(plan, in_ref, live_ref, start_ref, out_ref):
+def finish_kernel(plan, in_ref, live_ref, start_ref, total_ref, residual_ref):
     for group in range(plan.slab):
         here = slice(group * plan.sp, (group + 1) * plan.sp)
         live = jnp.broadcast_to(live_ref[here, :], (plan.sp, PLANE)) != 0.0
         for c in range(3):
-            out_ref[c, here, :] = jnp.where(live, start_ref[c, here, :], 0.0) + in_ref[
+            total_ref[c, here, :] = jnp.where(live, start_ref[c, here, :], 0.0) + in_ref[
                 group, c * plan.sp : (c + 1) * plan.sp, :
             ]
-
-
-def moduli_kernel(plan, tile_ref, in_ref, mtab_ref, mean_ref, mods_ref, fields):
-    from_plane = [lax.rem(tile_ref[1] + (plan.nz - z), plan.nz) for z in range(plan.nz)]
-    fields[0] = jnp.zeros((16, plan.ls), F32)
-    fields[NX + 1] = jnp.zeros((16, plan.ls), F32)
-    for a in range(PLANE // 128):
-        pieces = rows_at(
-            swap_quarters([in_ref[from_plane[4 * t + i], :, a * 128 : (a + 1) * 128] for i in range(4)])
-            for t in range(plan.nz // 4)
-        )
-        for b, piece in enumerate(pieces):
-            fields[4 * a + b + 1] = piece
-            mean_ref[4 * a + b : 4 * a + b + 1, :] = piece[0:1]
-    tile = jnp.minimum(tile_ref[0], plan.nxb * plan.nyb - 1)
-    xb, yb = tile // plan.nyb, tile % plan.nyb
-    table = mtab_ref[yb]
-    mods_ref[...] = jnp.zeros(mods_ref.shape, F32)
-    for k in range(plan.rx):
-        here = picked(fields[xb * plan.tx + k], table)
-        for v in range(FIELDS):
-            mods_ref[v, k : k + 1, :] = here[v : v + 1]
+            residual_ref[c, here, :] = in_ref[group, (3 + c) * plan.sp : (4 + c) * plan.sp, :]
 
 
 def regrouped(plan, msg_ref, out_ref):
@@ -262,7 +299,9 @@
     height = lane % (plan.nz * plan.ry) // plan.ry
 
     def one(row, carry):
-        parts = [msg_ref[row * plan.slab + z] for z in range(plan.nz)]
+        parts = [
+            msg_ref[pl.ds(pl.multiple_of((row * plan.slab + z) * plan.rows_in, 8), plan.rows_in), :] for z in range(plan.nz)
+        ]
         for group in range(plan.slab):
             total = parts[group]
             for z in range(plan.nz):
@@ -275,7 +314,8 @@
     lax.fori_loop(0, plan.chaos, one, 0, unroll=4)
 
 
-def first_mix_kernel(plan, low_count, nodes_ref, level_ref, msg_ref, mods_ref, out_ref, grad, flux, scaled, regroup):
+def first_mix_kernel(plan, low_count, place_ref, nodes_ref, level_ref, msg_ref, mtab_ref, out_ref, mods_ref, grad, flux, scaled, regroup):
+    gather_moduli(plan, place_ref[0] * plan.slab + place_ref[1], msg_ref, mtab_ref, mods_ref)
     regrouped(plan, msg_ref, regroup)
     mix_kernel(plan, low_count, nodes_ref, level_ref, regroup, mods_ref, out_ref, grad, flux, scaled)
 
@@ -431,26 +471,21 @@
     store_message(plan, wide, msg_ref)
 
 
-def flat_rows(plan, values, out_ref, c, a):
+def flat_rows(plan, values, out_ref, first, a):
     for t in range(plan.nz // 4):
         parts = [value[:, t * 128 : (t + 1) * 128] for value in values]
         for i, piece in enumerate(swap_quarters(parts)):
-            out_ref[4 * t + i, c * plan.sp : (c + 1) * plan.sp, a * 128 : (a + 1) * 128] = piece[: plan.sp]
-
-
-def residual_kernel(plan, image_ref, base_ref, live_ref, unpack_ref, residual_ref, out_ref, wide, narrow):
+            out_ref[4 * t + i, first : first + plan.sp, a * 128 : (a + 1) * 128] = piece[: plan.sp]
+
+
+def end_kernel(plan, image_ref, base_ref, live_ref, mean_ref, unpack_ref, before_ref, out_ref, wide, narrow, residual, update, step):
     unpack_image(plan, image_ref, unpack_ref, wide, narrow)
-    add_image(plan, base_ref, live_ref, narrow, residual_ref)
+    add_image(plan, base_ref, live_ref, narrow, residual)
+    smooth(plan, mean_ref, residual, update, step)
     for a in range(PLANE // 128):
         for c in range(3):
-            flat_rows(plan, [residual_ref[4 * a + b, c] for b in range(4)], out_ref, c, a)
-
-
-def end_kernel(plan, residual_ref, mean_ref, before_ref, out_ref, update, step):
-    smooth(plan, mean_ref, residual_ref, update, step)
-    for a in range(PLANE // 128):
-        for c in range(3):
-            flat_rows(plan, [update[4 * a + b, c] + before_ref[4 * a + b, c] for b in range(4)], out_ref, c, a)
+            flat_rows(plan, [update[4 * a + b, c] + before_ref[4 * a + b, c] for b in range(4)], out_ref, c * plan.sp, a)
+            flat_rows(plan, [residual[4 * a + b, c] for b in range(4)], out_ref, (3 + c) * plan.sp, a)
 
 
 def per_device(displacement, load, mean_modulus, modes, owner):
@@ -476,7 +511,7 @@
     pack = jnp.asarray(plan.pack_table(), BF16)
     unpack = jnp.asarray(plan.unpack_table(), BF16)
     mtab = jnp.asarray(plan.modulus_table(), BF16)
-    tile = jnp.stack([at_chaos * slab + at_slab, at_slab]).astype(jnp.int32)
+    place = jnp.stack([at_chaos, at_slab]).astype(jnp.int32)
 
     slots_pad = slab * sp
 
@@ -512,66 +547,61 @@
     narrow = pltpu.VMEM((NX * hs, 3 * ls), F32)
     field_scratch, more_scratch = pltpu.VMEM(grid_field.shape, F32), pltpu.VMEM(grid_more.shape, F32)
 
-    moduli = jnp.concatenate([mean_modulus[None], modes], axis=0)
-    moduli = jnp.pad(moduli, ((0, 16 - FIELDS), (0, 0)))
-    moduli = jnp.stack(
-        [moduli] + [lax.ppermute(moduli, "slab", [(z, (z + step) % slab) for z in range(slab)]) for step in range(1, slab)]
-    )
-    mean_s, mods = call(
-        functools.partial(moduli_kernel, plan),
-        "moduli",
-        [smem, vmem, vmem],
-        (array(NX, ls), array(FIELDS, 8, lanes)),
-        [pltpu.VMEM((NX + 2, 16, ls), F32)],
-    )(tile, moduli, mtab)
-
-    msg = call(functools.partial(start_kernel, plan), "start", [vmem, vmem], message, [narrow, wide])(
-        by_component(displacement), pack
-    )
-
-    def mixed(values, first):
-        scratch = [
-            pltpu.VMEM((plan.positions, 3, 8, lanes), F32),
-            pltpu.VMEM((plan.positions, 3, 8, lanes), F32),
-            pltpu.VMEM((DEG * KL, 8, lanes), F32),
-        ]
-        kernel = mix_kernel
-        if first:
-            kernel = first_mix_kernel
-            scratch.append(pltpu.VMEM((n, plan.rows_in, lanes), F32))
-        return call(
-            functools.partial(kernel, plan, len(low)), "mix", [smem, smem, vmem, vmem], image, scratch
-        )(nodes, jnp.asarray(level, jnp.int32), values, mods)
+    mean_row = mean_modulus.reshape(1, PLANE)
+    msg = call(
+        functools.partial(start_kernel, plan),
+        "start",
+        [smem, vmem, vmem, vmem, vmem],
+        message,
+        [narrow, wide, pltpu.VMEM((16, PLANE), F32)],
+    )(place, by_component(displacement), mean_row, modes, pack)
+    levels = jnp.asarray(level, jnp.int32)
+    mix_scratch = [
+        pltpu.VMEM((plan.positions, 3, 8, lanes), F32),
+        pltpu.VMEM((plan.positions, 3, 8, lanes), F32),
+        pltpu.VMEM((DEG * KL, 8, lanes), F32),
+    ]
 
     arrived = everyone(msg)
     flat, parts = array(slab, plan.rows_flat, PLANE), array(3, slots_pad, PLANE)
-    load_flat = call(functools.partial(split_kernel, plan), "split", [vmem], flat, [])(by_component(load))
-    load_flat, nodes, mean_s, mods = lax.optimization_barrier((load_flat, nodes, mean_s, mods))
+    load_flat = call(functools.partial(split_kernel, plan), "split", [vmem, vmem], flat, [])(
+        by_component(load), mean_row
+    )
+    load_flat, nodes, place = lax.optimization_barrier((load_flat, nodes, place))
     load_flat, arrived = lax.optimization_barrier((load_flat, arrived))
-    load_s = call(functools.partial(load_kernel, plan), "load", [vmem], grid_field, [])(column(load_flat))
-    first_image = everyone(mixed(arrived, True))
+    load_s, mean_s = call(functools.partial(load_kernel, plan), "load", [vmem], (grid_field, array(NX, ls)), [])(
+        column(load_flat)
+    )
+    first_image, mods = call(
+        functools.partial(first_mix_kernel, plan, len(low)),
+        "mix",
+        [smem, smem, smem, vmem, vmem],
+        (image, array(FIELDS, 8, lanes)),
+        mix_scratch + [pltpu.VMEM((n, plan.rows_in, lanes), F32)],
+    )(place, nodes, levels, arrived.reshape(n * plan.rows_in, lanes), mtab)
     msg, residual_s, update_s = call(
         functools.partial(middle_kernel, plan),
         "middle",
         [vmem] * 6,
         (message, grid_field, grid_more),
         [wide, narrow, field_scratch],
-    )(first_image, load_s, live_here, mean_s, unpack, pack)
-
-    second_image = everyone(mixed(everyone(msg), False))
-    residual_s, residual_flat = call(
-        functools.partial(residual_kernel, plan), "residual", [vmem] * 4, (grid_field, flat), [wide, narrow]
-    )(second_image, residual_s, live_here, unpack)
-    residual = column(residual_flat)
-    update_flat = call(
-        functools.partial(end_kernel, plan), "end", [vmem] * 3, flat, [more_scratch, field_scratch]
-    )(residual_s, mean_s, update_s)
-    residual = call(functools.partial(join_kernel, plan), "join", [vmem], parts, [])(residual)
+    )(everyone(first_image), load_s, live_here, mean_s, unpack, pack)
+
+    second_image = call(
+        functools.partial(mix_kernel, plan, len(low)), "mix", [smem, smem, vmem, vmem], image, mix_scratch
+    )(nodes, levels, everyone(msg), mods)
+    ending = call(
+        functools.partial(end_kernel, plan),
+        "end",
+        [vmem] * 6,
+        array(slab, plan.rows_end, PLANE),
+        [wide, narrow, field_scratch, more_scratch, field_scratch],
+    )(everyone(second_image), residual_s, live_here, mean_s, unpack, update_s)
     live_pad = jnp.pad(live_own.astype(F32), (0, slots_pad - slots_dev))
-    total = call(functools.partial(add_kernel, plan), "add", [vmem] * 3, parts, [])(
-        column(update_flat), jnp.broadcast_to(live_pad[:, None], (slots_pad, 128))[:, :1], by_component(displacement)
+    outs = call(functools.partial(finish_kernel, plan), "finish", [vmem] * 3, (parts, parts), [])(
+        column(ending), live_pad[:, None], by_component(displacement)
     )
-    return tuple(jnp.transpose(values, (1, 0, 2))[:slots_dev] for values in (total, residual))
+    return tuple(jnp.transpose(values, (1, 0, 2))[:slots_dev] for values in outs)
 
 
 def solution(mesh):

time: 164 us -> 157 us (0.957)
  starting transfers between devices: 27.8 us -> 18.8 us
  waiting for transfers between devices: 49.9 us -> 54.1 us
    all_to_all x2, waiting for transfers between devices: 13.7 us -> 32.1 us  [everyone(): return lax.all_to_all(values, ('chaos', 'slab'), 0, 0, tiled=True)]
    ppermute x3 -> x0, waiting for transfers between devices: 16.8 us -> none  [per_device(): lax.ppermute(moduli, 'slab', [(z, (z + step) % slab) for z in range(slab)])]
    ppermute x3 -> x0, starting transfers between devices: 5.65 us -> none  [per_device(): lax.ppermute(moduli, 'slab', [(z, (z + step) % slab) for z in range(slab)])]
    all_to_all x3 -> x2, waiting for transfers between devices: 19.5 us -> 21.9 us  [column(): return lax.all_to_all(values, 'slab', 0, 0, tiled=True)]
    all_to_all x3 -> x2, starting transfers between devices: 11.1 us -> 8.71 us  [column(): return lax.all_to_all(values, 'slab', 0, 0, tiled=True)]
    pallas_call x10 -> x7, Pallas kernels: 31.4 us -> 30.1 us  [the longest x1 9.52 us: per_device(): call(functools.partial(first_mix_kernel, plan, len(low)), 'mix', [smem, s...]
  transfers between devices with their start and end apart: 8 -> 4, of which waited for: 6 -> 4; matrix products, arithmetic and copies ran while one was open for 0% -> 0% of each run, Pallas kernels for 11% -> 7%
where the time goes in v4:
time: 157 us
  waiting for transfers between devices  54.1 us (34%)
  blocking collectives  42 us (27%)
  Pallas kernels  36.8 us (23%)
  starting transfers between devices  18.8 us (12%)
  local copies, waits for them, and re-layouts  3.76 us (2%)
    all_to_all x2, blocking collectives, everyone(): return lax.all_to_all(values, ('chaos', 'slab'), 0, 0, tiled=True)  42 us
    all_to_all x2, waiting for transfers between devices, everyone(): return lax.all_to_all(values, ('chaos', 'slab'), 0, 0, tiled=True)  32.1 us
    all_to_all x2, waiting for transfers between devices, column(): return lax.all_to_all(values, 'slab', 0, 0, tiled=True)  21.9 us
    all_to_all x2, starting transfers between devices, everyone(): return lax.all_to_all(values, ('chaos', 'slab'), 0, 0, tiled=True)  10.1 us
    pallas_call x1, Pallas kernels, per_device(): call(functools.partial(first_mix_kernel, plan, len(low)), 'mix', [smem, s...  9.52 us
    all_to_all x2, starting transfers between devices, column(): return lax.all_to_all(values, 'slab', 0, 0, tiled=True)  8.71 us
    pallas_call x1, Pallas kernels, per_device(): call(functools.partial(end_kernel, plan), 'end', [vmem] * 6, array(slab,...  7.72 us
    pallas_call x1, Pallas kernels, per_device(): call(functools.partial(mix_kernel, plan, len(low)), 'mix', [smem, smem, v...  7.71 us
  transfers between devices with their start and end apart: 4, of which 4 were waited for; matrix products, arithmetic and copies ran while one was open for 0% of the time, Pallas kernels for 7%

profile of v4, /device:TPU:0, one launch (start us, length us, event | category | flops | bytes accessed | tf_op | source)
XLA Modules:
  0.0 156.6 jit_solution(14276762354193946206)
XLA Ops:
  0.6 0.7 copy-done.10
  1.3 0.1 pad_add_fusion.place_ref
  1.4 1.0 copy-done
  2.4 1.0 copy-done.3
  3.4 0.8 copy-done.7
  4.2 2.6 %start.1 = f32[32,48,128]{2,1,0:T(8,128)} custom-call(s32[2]{0:T(128)S(1)} %pad_add_fusion.place_ref, f32[3,36,768]{2,1,0:T(8,128)S(1)} %bitcast.10, f32[1,768]{1,0:T(1,128)S(1)} %reshape.13.mean_ref, f32[10,768]{1,0:T(8,128)S(1)} %copy-done.7, bf16[384,512]{1,0:T(8,128)(2,1)S(1)} %copy-done), custom_call_target="tpu_custom_call" | custom-call | tf_op jit(solution)/shard_map/start/pallas_call | solution.py:551
  6.8 7.3 %all-to-all-start = ((f32[32,48,128]{2,1,0:T(8,128)}), f32[32,48,128]{2,1,0:T(8,128)S(1)}, u32[]{:S(2)}, u32[]{:S(2)}) async-start(f32[32,48,128]{2,1,0:T(8,128)} %start.1), calls=%async_computation | async-start | bytes 1572864 | tf_op jit(solution)/shard_map/all_to_all | solution.py:522
  14.1 0.0 copy-start.11
  14.2 0.8 split.1
  15.0 0.2 fusion.nodes_ref
  15.2 0.0 copy-start.6
  15.2 18.6 %all-to-all-done = f32[32,48,128]{2,1,0:T(8,128)S(1)} async-done(((f32[32,48,128]{2,1,0:T(8,128)}), f32[32,48,128]{2,1,0:T(8,128)S(1)}, u32[]{:S(2)}, u32[]{:S(2)}) %all-to-all-start) | async-done | bytes 786464 | tf_op jit(solution)/shard_map/all_to_all | solution.py:522
  33.7 4.5 %all-to-all-start.2 = ((f32[4,32,768]{2,1,0:T(8,128)}), f32[4,32,768]{2,1,0:T(8,128)S(1)}, u32[]{:S(2)}, u32[]{:S(2)}) async-start(f32[4,32,768]{2,1,0:T(8,128)} %split.1), calls=%async_computation.2 | async-start | bytes 786432 | tf_op jit(solution)/shard_map/all_to_all | solution.py:525
  38.2 9.5 %mix.2 = (f32[32,32,128]{2,1,0:T(8,128)}, f32[11,8,128]{2,1,0:T(8,128)S(1)}) custom-call(s32[2]{0:T(128)S(1)} %pad_add_fusion.place_ref, s32[726]{0:T(1024)S(1)} %fusion.nodes_ref, s32[660]{0:T(1024)S(1)} %copy-done.8, f32[1536,128]{1,0:T(8,128)S(1)} %bitcast.9, bf16[4,128,128]{2,1,0:T(8,128)(2,1)S(1)} %copy-done.6), custom_call_target="tpu_custom_call" | custom-call | tf_op jit(solution)/shard_map/mix/pallas_call | solution.py:575
  47.8 3.1 %all-to-all-done.2.in_ref = f32[4,32,768]{2,1,0:T(8,128)S(1)} async-done(((f32[4,32,768]{2,1,0:T(8,128)}), f32[4,32,768]{2,1,0:T(8,128)S(1)}, u32[]{:S(2)}, u32[]{:S(2)}) %all-to-all-start.2) | async-done | bytes 393248 | tf_op jit(solution)/shard_map/all_to_all | solution.py:525
  50.9 2.8 %all-to-all-start.1 = ((f32[32,32,128]{2,1,0:T(8,128)}), f32[32,32,128]{2,1,0:T(8,128)S(1)}, u32[]{:S(2)}, u32[]{:S(2)}) async-start(f32[32,32,128]{2,1,0:T(8,128)} %get-tuple-element.20), calls=%async_computation.1 | async-start | bytes 1048576 | tf_op jit(solution)/shard_map/all_to_all | solution.py:522
  53.6 0.0 copy-start.1
  53.7 0.1 dynamic-slice_convert_fusion
  53.8 0.1 dynamic_slice.7
  53.8 0.6 load.1
  54.4 13.6 %all-to-all-done.1.image_ref = f32[32,32,128]{2,1,0:T(8,128)S(1)} async-done(((f32[32,32,128]{2,1,0:T(8,128)}), f32[32,32,128]{2,1,0:T(8,128)S(1)}, u32[]{:S(2)}, u32[]{:S(2)}) %all-to-all-start.1) | async-done | bytes 524320 | tf_op jit(solution)/shard_map/all_to_all | solution.py:522
  68.0 0.1 broadcast_in_dim.25.live_ref
  68.1 6.7 %middle.1 = (f32[32,48,128]{2,1,0:T(8,128)S(1)}, f32[24,3,16,128]{3,2,1,0:T(8,128)S(1)}, f32[25,3,16,128]{3,2,1,0:T(8,128)S(1)}) custom-call(f32[32,32,128]{2,1,0:T(8,128)S(1)} %all-to-all-done.1.image_ref, f32[24,3,16,128]{3,2,1,0:T(8,128)S(1)} %get-tuple-element.22.base_ref, f32[16,128]{1,0:T(8,128)S(1)} %broadcast_in_dim.25.live_ref, ...), custom_call_target="tpu_custom_call" | custom-call | tf_op jit(solution)/shard_map/middle/pallas_call | solution.py:582
  74.8 23.5 %all_to_all.30.msg_ref = f32[32,48,128]{2,1,0:T(8,128)S(1)} all-to-all(f32[32,48,128]{2,1,0:T(8,128)S(1)} %get-tuple-element.24), channel_id=1, replica_groups=mesh['chaos'=8,'slab'=4] {'chaos','slab'}, dimensions={0} | all-to-all | bytes 1572864 | tf_op jit(solution)/shard_map/all_to_all | solution.py:522
  98.3 7.7 %mix.3 = f32[32,32,128]{2,1,0:T(8,128)S(1)} custom-call(s32[726]{0:T(1024)S(1)} %fusion.nodes_ref, s32[660]{0:T(1024)S(1)} %copy-done.8, f32[32,48,128]{2,1,0:T(8,128)S(1)} %all_to_all.30.msg_ref, f32[11,8,128]{2,1,0:T(8,128)S(1)} %get-tuple-element.25.mods_ref), custom_call_target="tpu_custom_call" | custom-call | tf_op jit(solution)/shard_map/mix/pallas_call | solution.py:590
  106.0 18.5 %all_to_all.31.image_ref = f32[32,32,128]{2,1,0:T(8,128)S(1)} all-to-all(f32[32,32,128]{2,1,0:T(8,128)S(1)} %mix.3), channel_id=1, replica_groups=mesh['chaos'=8,'slab'=4] {'chaos','slab'}, dimensions={0} | all-to-all | bytes 1048576 | tf_op jit(solution)/shard_map/all_to_all | solution.py:522
  124.6 7.7 %end.1 = f32[4,56,768]{2,1,0:T(8,128)} custom-call(f32[32,32,128]{2,1,0:T(8,128)S(1)} %all_to_all.31.image_ref, f32[24,3,16,128]{3,2,1,0:T(8,128)S(1)} %get-tuple-element.26.base_ref, f32[16,128]{1,0:T(8,128)S(1)} %broadcast_in_dim.25.live_ref, f32[24,128]{1,0:T(8,128)S(1)} %get-tuple-element.23.mean_ref, bf16[512,384]{1,0:T(8,128)(2,1)S(1)} %copy-done.2, ...), custom_call_target="tpu_custom_call" | custom-call | tf_op jit(solution)/shard_map/end/pallas_call | solution.py:593
  132.3 4.2 %all-to-all-start.5 = ((f32[4,56,768]{2,1,0:T(8,128)}), f32[4,56,768]{2,1,0:T(8,128)S(1)}, u32[]{:S(2)}, u32[]{:S(2)}) async-start(f32[4,56,768]{2,1,0:T(8,128)} %end.1), calls=%async_computation.5 | async-start | bytes 1376256 | tf_op jit(solution)/shard_map/all_to_all | solution.py:525
  136.5 0.1 fusion.1
  136.6 0.1 copy.14.live_ref
  136.7 18.8 %all-to-all-done.5.in_ref = f32[4,56,768]{2,1,0:T(8,128)S(1)} async-done(((f32[4,56,768]{2,1,0:T(8,128)}), f32[4,56,768]{2,1,0:T(8,128)S(1)}, u32[]{:S(2)}, u32[]{:S(2)}) %all-to-all-start.5) | async-done | bytes 688160 | tf_op jit(solution)/shard_map/all_to_all | solution.py:525
  155.5 1.1 finish.1
  (20 shorter events, 0.0 us)
Async XLA Ops:
  0.6 0.7 copy-start.10
  1.4 1.0 copy-start
  2.4 1.0 copy-start.3
  3.4 0.8 copy-start.7
  6.8 7.3 %copy-start.5 = (f32[36,3,768]{2,0,1:T(8,128)S(1)}, f32[36,3,768]{2,0,1:T(8,128)}, u32[]{:S(2)}) copy-start(f32[36,3,768]{2,0,1:T(8,128)} %param.12) | copy-start | bytes 995332
  6.8 26.9 %all-to-all-start = ((f32[32,48,128]{2,1,0:T(8,128)}), f32[32,48,128]{2,1,0:T(8,128)S(1)}, u32[]{:S(2)}, u32[]{:S(2)}) async-start(f32[32,48,128]{2,1,0:T(8,128)} %start.1), calls=%async_computation | async-start | bytes 1572864 | tf_op jit(solution)/shard_map/all_to_all | solution.py:522
  14.1 0.9 copy-start.9
  14.1 0.8 copy-start.11
  15.2 23.1 %copy-start.6 = (bf16[4,128,128]{2,1,0:T(8,128)(2,1)S(1)}, bf16[4,128,128]{2,1,0:T(8,128)(2,1)}, u32[]{:S(2)}) copy-start(bf16[4,128,128]{2,1,0:T(8,128)(2,1)} %constant.36.clone.mtab_ref) | copy-start | bytes 393220
  33.7 4.5 %copy-start.8 = (s32[660]{0:T(1024)S(1)}, s32[660]{0:T(1024)}, u32[]{:S(2)}) copy-start(s32[660]{0:T(1024)} %constant.37.clone.level_ref) | copy-start | bytes 7924
  33.7 17.1 %all-to-all-start.2 = ((f32[4,32,768]{2,1,0:T(8,128)}), f32[4,32,768]{2,1,0:T(8,128)S(1)}, u32[]{:S(2)}, u32[]{:S(2)}) async-start(f32[4,32,768]{2,1,0:T(8,128)} %split.1), calls=%async_computation.2 | async-start | bytes 786432 | tf_op jit(solution)/shard_map/all_to_all | solution.py:525
  50.9 17.2 %copy-start.2 = (bf16[512,384]{1,0:T(8,128)(2,1)S(1)}, bf16[512,384]{1,0:T(8,128)(2,1)}, u32[]{:S(2)}) copy-start(bf16[512,384]{1,0:T(8,128)(2,1)} %constant.35.clone.unpack_ref) | copy-start | bytes 1179652
  50.9 17.1 %all-to-all-start.1 = ((f32[32,32,128]{2,1,0:T(8,128)}), f32[32,32,128]{2,1,0:T(8,128)S(1)}, u32[]{:S(2)}, u32[]{:S(2)}) async-start(f32[32,32,128]{2,1,0:T(8,128)} %get-tuple-element.20), calls=%async_computation.1 | async-start | bytes 1048576 | tf_op jit(solution)/shard_map/all_to_all | solution.py:522
  53.6 14.4 %copy-start.1 = (bf16[384,512]{1,0:T(8,128)(2,1)S(1)}, bf16[384,512]{1,0:T(8,128)(2,1)}, u32[]{:S(2)}) copy-start(bf16[384,512]{1,0:T(8,128)(2,1)} %constant.34.clone.pack_ref) | copy-start | bytes 1179652
  132.3 23.2 %copy-start.4 = (f32[36,3,768]{2,0,1:T(8,128)S(1)}, f32[36,3,768]{2,0,1:T(8,128)}, u32[]{:S(2)}) copy-start(f32[36,3,768]{2,0,1:T(8,128)} %param.11) | copy-start | bytes 995332
  132.3 23.2 %all-to-all-start.5 = ((f32[4,56,768]{2,1,0:T(8,128)}), f32[4,56,768]{2,1,0:T(8,128)S(1)}, u32[]{:S(2)}, u32[]{:S(2)}) async-start(f32[4,56,768]{2,1,0:T(8,128)} %end.1), calls=%async_computation.5 | async-start | bytes 1376256 | tf_op jit(solution)/shard_map/all_to_all | solution.py:525

commit v5 on v4

--- a/solution.py
+++ b/solution.py
@@ -77,7 +77,12 @@
         self.rx = self.tx + 2
         self.ry = self.ty + 2
         self.nxb, self.nyb = NX // self.tx, NY // self.ty
-        self.rows_out = up8(self.sp * self.tx)
+        self.lanes_out = -(-3 * self.nz * self.ty // 128) * 128
+        self.segment = self.nz * self.ty
+        self.moved = self.sp // 4 if self.lanes_out >= 4 * self.segment else 0
+        self.kept = self.sp - self.moved
+        self.rows_out = up8(self.kept * self.tx)
+        self.image_width = (4 if self.moved else 3) * self.ls
         self.rows_flat = up8(3 * self.sp + 1)
         self.rows_end = up8(6 * self.sp)
         self.shares = -(-FIELDS // min(chaos, 16))
@@ -99,14 +104,66 @@
         return table
 
     def unpack_table(self):
-        table = np.zeros((self.nyb * self.lanes, 3 * self.ls), np.float32)
-        for c in range(3):
+        table = np.zeros((self.nyb * self.lanes_out, self.image_width), np.float32)
+        for c in range(self.image_width // self.ls):
             for z in range(self.nz):
                 for y in range(NY):
-                    yb, k = y // self.ty, y % self.ty + 1
+                    yb, k = divmod(y, self.ty)
                     table[
-                        yb * self.lanes + (c * self.nz + z) * self.ry + k, c * self.ls + z * NY + y
+                        yb * self.lanes_out + (c * self.nz + z) * self.ty + k, c * self.ls + z * NY + y
                     ] = 1
+        return table
+
+    def tile_lane(self, c, z, y):
+        return (c * self.nz + z) * self.ry + y
+
+    def gradient_table(self):
+        table = np.zeros((2 * self.lanes, 3 * self.lanes), np.float32)
+        at, wide = self.tile_lane, self.lanes
+
+        def add(column, c, d, z, y, sign=1):
+            if d == 0:
+                table[wide + at(c, z, y), column] += 1
+                return
+            table[at(c, z, y), column] -= 1
+            if d == 1 and y + 1 < self.ry:
+                table[at(c, z, y + 1), column] += 1
+            if d == 2 and z + 1 < self.nz:
+                table[at(c, z + 1, y), column] += 1
+
+        for z in range(self.nz):
+            for y in range(self.ry):
+                for c in range(3):
+                    for d in range(3):
+                        add(d * wide + at(c, z, y), c, d, z, y)
+                        add(c * wide + at(c, z, y), d, d, z, y)
+        return table
+
+    def divergence_table(self):
+        table = np.zeros((3 * self.lanes, self.lanes_out), np.float32)
+        at, wide = self.tile_lane, self.lanes
+        for c in range(3):
+            for z in range(self.nz):
+                for y in range(self.ty):
+                    column = (c * self.nz + z) * self.ty + y
+                    table[at(c, z, y + 1), column] = 1
+                    table[wide + at(c, z, y + 1), column] = 1
+                    table[wide + at(c, z, y), column] = -1
+                    table[2 * wide + at(c, z, y + 1), column] = 1
+                    if z:
+                        table[2 * wide + at(c, z - 1, y + 1), column] = -1
+        return table
+
+    def slope_table(self):
+        table = np.zeros((self.ls, 2 * self.ls), np.float32)
+        for z in range(self.nz):
+            for y in range(NY):
+                j = z * NY + y
+                table[j, j] = table[j, self.ls + j] = -1
+                if y + 1 < NY:
+                    table[j + 1, j] = 1
+                if z + 1 < self.nz:
+                    table[j + NY, self.ls + j] = 1
         return table
 
     def modulus_table(self):
@@ -121,23 +178,24 @@
         return table
 
 
-def picked(values, table):
-    high = values.astype(BF16)
-    rest = values - high.astype(F32)
-    middle = rest.astype(BF16)
-    low = (rest - middle.astype(F32)).astype(BF16)
-    return (
-        jnp.dot(high, table, preferred_element_type=F32)
-        + jnp.dot(middle, table, preferred_element_type=F32)
-        + jnp.dot(low, table, preferred_element_type=F32)
-    )
+def picked(values, table, parts=3):
+    total, rest = None, values
+    for part in range(parts):
+        head = rest.astype(BF16)
+        product = jnp.dot(head, table, preferred_element_type=F32)
+        total = product if total is None else total + product
+        if part + 1 < parts:
+            rest = rest - head.astype(F32)
+    return total
 
 
 def pick_into(out_ref, values_ref, table_ref):
     width = table_ref.shape[1]
     chunk = width if width <= 1024 else 512
     for first in range(0, width, chunk):
-        out_ref[:, first : first + chunk] = picked(values_ref[...], table_ref[:, first : first + chunk])
+        out_ref[:, first : first + chunk] = picked(
+            values_ref[:, : table_ref.shape[0]], table_ref[:, first : first + chunk]
+        )
 
 
 def swap_quarters(parts):
@@ -271,7 +329,7 @@
             for t in range(plan.nz // 4)
         )
         for b, piece in enumerate(pieces):
-            mean_ref[4 * a + b : 4 * a + b + 1, :] = piece
+            mean_ref[4 * a + b] = jnp.broadcast_to(piece, (plan.hs, plan.ls))
         for c in range(3):
             pieces = rows_at(
                 swap_quarters(
@@ -314,40 +372,40 @@
     lax.fori_loop(0, plan.chaos, one, 0, unroll=4)
 
 
-def first_mix_kernel(plan, low_count, place_ref, nodes_ref, level_ref, msg_ref, mtab_ref, out_ref, mods_ref, grad, flux, scaled, regroup):
+def first_mix_kernel(plan, low_count, parts, place_ref, nodes_ref, level_ref, msg_ref, mtab_ref, grad_ref, div_ref, out_ref, mods_ref, grad, flux, scaled, regroup):
     gather_moduli(plan, place_ref[0] * plan.slab + place_ref[1], msg_ref, mtab_ref, mods_ref)
     regrouped(plan, msg_ref, regroup)
-    mix_kernel(plan, low_count, nodes_ref, level_ref, regroup, mods_ref, out_ref, grad, flux, scaled)
-
-
-def mix_kernel(plan, low_count, nodes_ref, level_ref, msg_ref, mods_ref, out_ref, grad, flux, scaled):
-    sp, rx, ry, nz, lanes = plan.sp, plan.rx, plan.ry, plan.nz, plan.lanes
-    segment = nz * ry
-    lane = lax.broadcasted_iota(jnp.int32, (8, lanes), 1)
-    part, height = lane // segment, lane % segment // ry
-    not_top, not_bottom = height != nz - 1, height != 0
-    is_x, is_y, is_z = part == 0, part == 1, part == 2
+    mix_kernel(plan, low_count, parts, nodes_ref, level_ref, regroup, mods_ref, grad_ref, div_ref, out_ref, grad, flux, scaled)
+
+
+def mix_kernel(plan, low_count, parts, nodes_ref, level_ref, msg_ref, mods_ref, grad_ref, div_ref, out_ref, grad, flux, scaled):
+    sp, rx, tx, lanes = plan.sp, plan.rx, plan.tx, plan.lanes
     for level in range(DEG):
         for v in range(KL):
             scaled[level * KL + v] = mods_ref[v + 1] * math.sqrt(level + 1)
     mean = mods_ref[0]
 
-    def gradients(source, carry):
-        own = jnp.stack([msg_ref[source, s * rx : s * rx + 8, :] for s in range(sp)])
-        slope_x = pltpu.roll(own, 7, 1) - own
-        slope_y = pltpu.roll(own, lanes - 1, 2) - own
-        slope_z = jnp.where(not_top, pltpu.roll(own, lanes - ry, 2), 0.0) - own
-        spread = slope_x + pltpu.roll(slope_y, lanes - segment, 2) + pltpu.roll(slope_z, lanes - 2 * segment, 2)
-        full_x = slope_x + jnp.where(is_x, spread, 0.0)
-        full_y = slope_y + jnp.where(is_y, pltpu.roll(spread, segment, 2), 0.0)
-        full_z = slope_z + jnp.where(is_z, pltpu.roll(spread, 2 * segment, 2), 0.0)
-        here = pl.ds(source * sp, sp)
-        for d, full in enumerate((full_x, full_y, full_z)):
-            grad[here, d] = full
-            flux[here, d] = mean * full
+    def gradients(chunk, carry):
+        windows, behind = [], []
+        for i in range(4):
+            source = chunk * 4 + i
+            for s in range(sp):
+                windows.append(msg_ref[source, s * rx : s * rx + 8, :])
+                if s * rx + 9 <= plan.rows_in:
+                    behind.append(msg_ref[source, s * rx + 1 : s * rx + 9, :])
+                else:
+                    behind.append(pltpu.roll(windows[-1], 7, 0))
+        own = jnp.concatenate(windows, axis=0)
+        slope_x = jnp.concatenate(behind, axis=0) - own
+        full = picked(jnp.concatenate([own, slope_x], axis=1), grad_ref[...], parts)
+        here = pl.ds(chunk * 4 * sp, 4 * sp)
+        for d in range(3):
+            part = full[:, d * lanes : (d + 1) * lanes].reshape(4 * sp, 8, lanes)
+            grad[here, d] = part
+            flux[here, d] = mean * part
         return carry
 
-    lax.fori_loop(0, plan.n, gradients, 0, unroll=4)
+    lax.fori_loop(0, plan.n // 4, gradients, 0, unroll=8)
 
     def edges(number, carry):
         base = nodes_ref[number]
@@ -370,17 +428,24 @@
 
     lax.fori_loop(0, low_count, edges, 0, unroll=2)
 
-    def divergences(source, carry):
-        here = pl.ds(source * sp, sp)
+    def divergences(chunk, carry):
+        here = pl.ds(chunk * 4 * sp, 4 * sp)
         flux_x, flux_y, flux_z = (flux[here, d] for d in range(3))
-        total = flux_x - pltpu.roll(flux_x, 1, 1)
-        total = total + (flux_y - pltpu.roll(flux_y, 1, 2))
-        total = total + (flux_z - jnp.where(not_bottom, pltpu.roll(flux_z, ry, 2), 0.0))
-        for s in range(sp):
-            out_ref[source, s * plan.tx : (s + 1) * plan.tx, :] = total[s, 1 : 1 + plan.tx]
+        flux_x = flux_x - pltpu.roll(flux_x, 1, 1)
+        values = jnp.concatenate([flux_x, flux_y, flux_z], axis=2).reshape(4 * sp * 8, 3 * lanes)
+        total = picked(values, div_ref[...], parts).reshape(4, sp, 8, plan.lanes_out)
+        for i in range(4):
+            for s in range(plan.kept):
+                out_ref[chunk * 4 + i, s * tx : (s + 1) * tx, :] = total[i, s, 1 : 1 + tx]
+            for number in range(3 * plan.moved):
+                slot, c = plan.kept + number // 3, number % 3
+                turned = pltpu.roll(total[i, slot], (3 - c) * plan.segment, 1)
+                out_ref[chunk * 4 + i, number * tx : (number + 1) * tx, 3 * plan.segment : 4 * plan.segment] = turned[
+                    1 : 1 + tx, 3 * plan.segment : 4 * plan.segment
+                ]
         return carry
 
-    lax.fori_loop(0, plan.n, divergences, 0, unroll=2)
+    lax.fori_loop(0, plan.n // 4, divergences, 0, unroll=8)
 
 
 def unpack_image(plan, image_ref, unpack_ref, lhs, rows):
@@ -388,33 +453,34 @@
         for k in range(plan.tx):
             x = xb * plan.tx + k
             for yb in range(plan.nyb):
-                lhs[x * plan.hs : x * plan.hs + plan.sp, yb * plan.lanes : (yb + 1) * plan.lanes] = image_ref[
-                    xb * plan.nyb + yb, strided(k, plan.sp, plan.tx), :
+                lhs[x * plan.hs : x * plan.hs + plan.kept, yb * plan.lanes_out : (yb + 1) * plan.lanes_out] = image_ref[
+                    xb * plan.nyb + yb, strided(k, plan.kept, plan.tx), :
                 ]
     pick_into(rows, lhs, unpack_ref)
 
 
 def add_image(plan, base_ref, live_ref, rows, residual_ref):
     live = live_ref[...] != 0.0
+    slot = lax.broadcasted_iota(jnp.int32, (plan.hs, plan.ls), 0)
 
     def one(x, carry):
-        for c in range(3):
-            image = rows[pl.ds(pl.multiple_of(x * plan.hs, plan.hs), plan.hs), c * plan.ls : (c + 1) * plan.ls]
+        block = rows.at[pl.ds(pl.multiple_of(x * plan.hs, plan.hs), plan.hs)]
+        for c in range(3):
+            image = block[:, c * plan.ls : (c + 1) * plan.ls]
+            for q in range(plan.moved):
+                line = block[3 * q + c : 3 * q + c + 1, 3 * plan.ls : 4 * plan.ls]
+                image = jnp.where(slot == plan.kept + q, line, image)
             residual_ref[x, c] = jnp.where(live, base_ref[x, c] + image, 0.0)
         return carry
 
     lax.fori_loop(0, NX, one, 0, unroll=6)
 
 
-def smooth(plan, mean_ref, residual_ref, update, step):
-    hs, ls = plan.hs, plan.ls
+def smooth(plan, mean_ref, slope_ref, back_ref, residual_ref, update, step):
+    hs, ls, many = plan.hs, plan.ls, 6
     center_value = 0.5 * (bound_high + bound_low)
     half_width = 0.5 * (bound_high - bound_low)
     ratio_value = center_value / half_width
-    lane = lax.broadcasted_iota(jnp.int32, (hs, ls), 1)
-    at_y, at_z = lane % NY, lane // NY
-    not_y_end, not_y_start = at_y != NY - 1, at_y != 0
-    not_z_end, not_z_start = at_z != plan.nz - 1, at_z != 0
 
     def first(x, carry):
         for c in range(3):
@@ -424,46 +490,46 @@
         return carry
 
     lax.fori_loop(0, NX, first, 0, unroll=6)
-    for c in range(3):
-        update[NX, c] = jnp.zeros((hs, ls), F32)
+    update[NX] = jnp.zeros((3, hs, ls), F32)
 
     rho_prev = 1.0 / ratio_value
     for sweep in range(SWEEPS):
         rho_next = 1.0 / (2.0 * ratio_value - rho_prev)
         keep, gain = rho_next * rho_prev, 2.0 * rho_next / half_width
 
-        def slab_of(x, carry, keep=keep, gain=gain):
-            behind, own = carry[:3], carry[3:]
-            modulus = jnp.broadcast_to(mean_ref[pl.ds(x, 1), :], (hs, ls))
-            ahead = [update[x + 1, c] for c in range(3)]
-            slope_x = [ahead[c] - own[c] for c in range(3)]
-            slope_y = [jnp.where(not_y_end, pltpu.roll(own[c], ls - 1, 1), 0.0) - own[c] for c in range(3)]
-            slope_z = [jnp.where(not_z_end, pltpu.roll(own[c], ls - NY, 1), 0.0) - own[c] for c in range(3)]
-            spread = slope_x[0] + slope_y[1] + slope_z[2]
-            slope_x[0] = slope_x[0] + spread
-            slope_y[1] = slope_y[1] + spread
-            slope_z[2] = slope_z[2] + spread
-            through = []
+        def slabs_of(chunk, behind, keep=keep, gain=gain):
+            here = pl.ds(chunk * many, many)
+            own = update[here]
+            slope_x = update[pl.ds(chunk * many + 1, many)] - own
+            slopes = picked(own.reshape(many * 3 * hs, ls), slope_ref[...], 2)
+            slopes = slopes.reshape(many, 3, hs, 2 * ls)
+            modulus = mean_ref[here]
+            spread = slope_x[:, 0] + slopes[:, 1, :, :ls] + slopes[:, 2, :, ls:]
+            flux_x, flux_yz = [], []
             for c in range(3):
-                flux_x, flux_y, flux_z = (modulus * slope[c] for slope in (slope_x, slope_y, slope_z))
-                through.append(flux_x)
-                total = flux_x - behind[c]
-                total = total + (flux_y - jnp.where(not_y_start, pltpu.roll(flux_y, 1, 1), 0.0))
-                total = total + (flux_z - jnp.where(not_z_start, pltpu.roll(flux_z, NY, 1), 0.0))
-                moved = keep * step[x, c] + gain * (residual_ref[x, c] + total)
-                step[x, c] = moved
-                update[x, c] = own[c] + moved
-            return (*through, *ahead)
+                parts = [slope_x[:, c], slopes[:, c, :, :ls], slopes[:, c, :, ls:]]
+                parts[c] = parts[c] + spread
+                flux_x.append(modulus * parts[0])
+                flux_yz.append(jnp.concatenate([modulus * parts[1], modulus * parts[2]], axis=-1))
+            flux_yz = jnp.stack(flux_yz, axis=1).reshape(many * 3 * hs, 2 * ls)
+            back = picked(flux_yz, back_ref[...], 2).reshape(many, 3, hs, ls)
+            for c in range(3):
+                earlier = jnp.concatenate([behind[c][None], flux_x[c][:-1]], axis=0)
+                total = flux_x[c] - earlier - back[:, c]
+                moved = keep * step[here, c] + gain * (residual_ref[here, c] + total)
+                step[here, c] = moved
+                update[here, c] = own[:, c] + moved
+            return tuple(flux[-1] for flux in flux_x)
 
         zero = jnp.zeros((hs, ls), F32)
-        lax.fori_loop(0, NX, slab_of, (zero, zero, zero, *(update[0, c] for c in range(3))), unroll=6)
+        lax.fori_loop(0, NX // many, slabs_of, (zero, zero, zero), unroll=4)
         rho_prev = rho_next
 
 
-def middle_kernel(plan, image_ref, base_ref, live_ref, mean_ref, unpack_ref, pack_ref, msg_ref, residual_ref, update_ref, wide, narrow, step):
+def middle_kernel(plan, image_ref, base_ref, live_ref, mean_ref, slope_ref, back_ref, unpack_ref, pack_ref, msg_ref, residual_ref, update_ref, wide, narrow, step):
     unpack_image(plan, image_ref, unpack_ref, wide, narrow)
     add_image(plan, base_ref, live_ref, narrow, residual_ref)
-    smooth(plan, mean_ref, residual_ref, update_ref, step)
+    smooth(plan, mean_ref, slope_ref, back_ref, residual_ref, update_ref, step)
     for x in range(NX):
         for c in range(3):
             narrow[x * plan.hs : (x + 1) * plan.hs, c * plan.ls : (c + 1) * plan.ls] = update_ref[x, c]
@@ -478,10 +544,10 @@
             out_ref[4 * t + i, first : first + plan.sp, a * 128 : (a + 1) * 128] = piece[: plan.sp]
 
 
-def end_kernel(plan, image_ref, base_ref, live_ref, mean_ref, unpack_ref, before_ref, out_ref, wide, narrow, residual, update, step):
+def end_kernel(plan, image_ref, base_ref, live_ref, mean_ref, slope_ref, back_ref, unpack_ref, before_ref, out_ref, wide, narrow, residual, update, step):
     unpack_image(plan, image_ref, unpack_ref, wide, narrow)
     add_image(plan, base_ref, live_ref, narrow, residual)
-    smooth(plan, mean_ref, residual, update, step)
+    smooth(plan, mean_ref, slope_ref, back_ref, residual, update, step)
     for a in range(PLANE // 128):
         for c in range(3):
             flat_rows(plan, [update[4 * a + b, c] + before_ref[4 * a + b, c] for b in range(4)], out_ref, c * plan.sp, a)
@@ -511,6 +577,8 @@
     pack = jnp.asarray(plan.pack_table(), BF16)
     unpack = jnp.asarray(plan.unpack_table(), BF16)
     mtab = jnp.asarray(plan.modulus_table(), BF16)
+    slopes, backs = (jnp.asarray(values, BF16) for values in (plan.slope_table(), plan.slope_table().T))
+    grads, divs = (jnp.asarray(values, BF16) for values in (plan.gradient_table(), plan.divergence_table()))
     place = jnp.stack([at_chaos, at_slab]).astype(jnp.int32)
 
     slots_pad = slab * sp
@@ -541,10 +609,10 @@
     def array(*shape):
         return jax.ShapeDtypeStruct(shape, F32)
 
-    message, image = array(n, plan.rows_in, lanes), array(n, plan.rows_out, lanes)
+    message, image = array(n, plan.rows_in, lanes), array(n, plan.rows_out, plan.lanes_out)
     grid_field, grid_more = array(NX, 3, hs, ls), array(NX + 1, 3, hs, ls)
     wide = pltpu.VMEM((NX * hs, plan.nyb * lanes), F32)
-    narrow = pltpu.VMEM((NX * hs, 3 * ls), F32)
+    narrow = pltpu.VMEM((NX * hs, plan.image_width), F32)
     field_scratch, more_scratch = pltpu.VMEM(grid_field.shape, F32), pltpu.VMEM(grid_more.shape, F32)
 
     mean_row = mean_modulus.reshape(1, PLANE)
@@ -569,34 +637,34 @@
     )
     load_flat, nodes, place = lax.optimization_barrier((load_flat, nodes, place))
     load_flat, arrived = lax.optimization_barrier((load_flat, arrived))
-    load_s, mean_s = call(functools.partial(load_kernel, plan), "load", [vmem], (grid_field, array(NX, ls)), [])(
+    load_s, mean_s = call(functools.partial(load_kernel, plan), "load", [vmem], (grid_field, array(NX, hs, ls)), [])(
         column(load_flat)
     )
     first_image, mods = call(
-        functools.partial(first_mix_kernel, plan, len(low)),
+        functools.partial(first_mix_kernel, plan, len(low), 3),
         "mix",
-        [smem, smem, smem, vmem, vmem],
+        [smem, smem, smem, vmem, vmem, vmem, vmem],
         (image, array(FIELDS, 8, lanes)),
         mix_scratch + [pltpu.VMEM((n, plan.rows_in, lanes), F32)],
-    )(place, nodes, levels, arrived.reshape(n * plan.rows_in, lanes), mtab)
+    )(place, nodes, levels, arrived.reshape(n * plan.rows_in, lanes), mtab, grads, divs)
     msg, residual_s, update_s = call(
         functools.partial(middle_kernel, plan),
         "middle",
-        [vmem] * 6,
+        [vmem] * 8,
         (message, grid_field, grid_more),
         [wide, narrow, field_scratch],
-    )(everyone(first_image), load_s, live_here, mean_s, unpack, pack)
+    )(everyone(first_image), load_s, live_here, mean_s, slopes, backs, unpack, pack)
 
     second_image = call(
-        functools.partial(mix_kernel, plan, len(low)), "mix", [smem, smem, vmem, vmem], image, mix_scratch
-    )(nodes, levels, everyone(msg), mods)
+        functools.partial(mix_kernel, plan, len(low), 2), "mix", [smem, smem, vmem, vmem, vmem, vmem], image, mix_scratch
+    )(nodes, levels, everyone(msg), mods, grads, divs)
     ending = call(
         functools.partial(end_kernel, plan),
         "end",
-        [vmem] * 6,
+        [vmem] * 8,
         array(slab, plan.rows_end, PLANE),
         [wide, narrow, field_scratch, more_scratch, field_scratch],
-    )(everyone(second_image), residual_s, live_here, mean_s, unpack, update_s)
+    )(everyone(second_image), residual_s, live_here, mean_s, slopes, backs, unpack, update_s)
     live_pad = jnp.pad(live_own.astype(F32), (0, slots_pad - slots_dev))
     outs = call(functools.partial(finish_kernel, plan), "finish", [vmem] * 3, (parts, parts), [])(
         column(ending), live_pad[:, None], by_component(displacement)

time: 157 us -> 144 us (0.917)
  Pallas kernels: 36.8 us -> 27.8 us
  blocking collectives: 42 us -> 39.3 us
    pallas_call x4, Pallas kernels: 31.7 us -> 22.7 us  [the longest x1 7.96 us: per_device(): call(functools.partial(first_mix_kernel, plan, len(low), 3), 'mix', [smem...]
    all_to_all x2, blocking collectives: 42 us -> 39.3 us  [everyone(): return lax.all_to_all(values, ('chaos', 'slab'), 0, 0, tiled=True)]
    all_to_all x2, waiting for transfers between devices: 32.1 us -> 29.6 us  [everyone(): return lax.all_to_all(values, ('chaos', 'slab'), 0, 0, tiled=True)]
    all_to_all x2, waiting for transfers between devices: 21.9 us -> 23.7 us  [column(): return lax.all_to_all(values, 'slab', 0, 0, tiled=True)]
    unnamed x24 -> x32, local copies, waits for them, and re-layouts: 3.5 us -> 3.52 us
where the time goes in v5:
time: 144 us
  waiting for transfers between devices  53.3 us (37%)
  blocking collectives  39.3 us (27%)
  Pallas kernels  27.8 us (19%)
  starting transfers between devices  18.5 us (13%)
  local copies, waits for them, and re-layouts  3.78 us (3%)
    all_to_all x2, blocking collectives, everyone(): return lax.all_to_all(values, ('chaos', 'slab'), 0, 0, tiled=True)  39.3 us
    all_to_all x2, waiting for transfers between devices, everyone(): return lax.all_to_all(values, ('chaos', 'slab'), 0, 0, tiled=True)  29.6 us
    all_to_all x2, waiting for transfers between devices, column(): return lax.all_to_all(values, 'slab', 0, 0, tiled=True)  23.7 us
    all_to_all x2, starting transfers between devices, everyone(): return lax.all_to_all(values, ('chaos', 'slab'), 0, 0, tiled=True)  10.1 us
    all_to_all x2, starting transfers between devices, column(): return lax.all_to_all(values, 'slab', 0, 0, tiled=True)  8.49 us
    pallas_call x1, Pallas kernels, per_device(): call(functools.partial(first_mix_kernel, plan, len(low), 3), 'mix', [smem...  7.96 us
    pallas_call x1, Pallas kernels, per_device(): call(functools.partial(mix_kernel, plan, len(low), 2), 'mix', [smem, smem...  5.14 us
    pallas_call x1, Pallas kernels, per_device(): call(functools.partial(end_kernel, plan), 'end', [vmem] * 8, array(slab,...  4.83 us
  transfers between devices with their start and end apart: 4, of which 4 were waited for; matrix products, arithmetic and copies ran while one was open for 0% of the time, Pallas kernels for 7%

profile of v5, /device:TPU:0, one launch (start us, length us, event | category | flops | bytes accessed | tf_op | source)
XLA Modules:
  0.0 143.9 jit_solution(1662283988162417631)
XLA Ops:
  0.6 0.7 copy-done.14
  1.3 0.1 pad_add_fusion.place_ref
  1.4 1.0 copy-done.1
  2.4 1.0 copy-done.3
  3.4 0.8 copy-done.11
  4.2 2.6 %start.1 = f32[32,48,128]{2,1,0:T(8,128)} custom-call(s32[2]{0:T(128)S(1)} %pad_add_fusion.place_ref, f32[3,36,768]{2,1,0:T(8,128)S(1)} %bitcast.10, f32[1,768]{1,0:T(1,128)S(1)} %reshape.13.mean_ref, f32[10,768]{1,0:T(8,128)S(1)} %copy-done.11, bf16[384,512]{1,0:T(8,128)(2,1)S(1)} %copy-done.1), custom_call_target="tpu_custom_call" | custom-call | tf_op jit(solution)/shard_map/start/pallas_call | solution.py:619
  6.8 7.3 %all-to-all-start = ((f32[32,48,128]{2,1,0:T(8,128)}), f32[32,48,128]{2,1,0:T(8,128)S(1)}, u32[]{:S(2)}, u32[]{:S(2)}) async-start(f32[32,48,128]{2,1,0:T(8,128)} %start.1), calls=%async_computation | async-start | bytes 1572864 | tf_op jit(solution)/shard_map/all_to_all | solution.py:590
  14.1 0.0 copy-start.15
  14.2 0.8 split.1
  15.0 0.2 fusion.nodes_ref
  15.2 0.0 copy-start.6
  15.2 0.0 copy-start.10
  15.2 18.5 %all-to-all-done = f32[32,48,128]{2,1,0:T(8,128)S(1)} async-done(((f32[32,48,128]{2,1,0:T(8,128)}), f32[32,48,128]{2,1,0:T(8,128)S(1)}, u32[]{:S(2)}, u32[]{:S(2)}) %all-to-all-start) | async-done | bytes 786464 | tf_op jit(solution)/shard_map/all_to_all | solution.py:590
  33.7 4.5 %all-to-all-start.2 = ((f32[4,32,768]{2,1,0:T(8,128)}), f32[4,32,768]{2,1,0:T(8,128)S(1)}, u32[]{:S(2)}, u32[]{:S(2)}) async-start(f32[4,32,768]{2,1,0:T(8,128)} %split.1), calls=%async_computation.2 | async-start | bytes 786432 | tf_op jit(solution)/shard_map/all_to_all | solution.py:593
  38.3 8.0 %mix.2 = (f32[32,24,128]{2,1,0:T(8,128)}, f32[11,8,128]{2,1,0:T(8,128)S(1)}) custom-call(s32[2]{0:T(128)S(1)} %pad_add_fusion.place_ref, s32[726]{0:T(1024)S(1)} %fusion.nodes_ref, s32[660]{0:T(1024)S(1)} %copy-done.12, f32[1536,128]{1,0:T(8,128)S(1)} %bitcast.9, bf16[4,128,128]{2,1,0:T(8,128)(2,1)S(1)} %copy-done.10, bf16[256,384]{1,0:T(8,128)(2,1)S(1)} %copy-done.5, ...), custom_call_target="tpu_custom_call" | custom-call | tf_op jit(solution)/shard_map/mix/pallas_call | solution.py:643
  46.2 4.7 %all-to-all-done.2.in_ref = f32[4,32,768]{2,1,0:T(8,128)S(1)} async-done(((f32[4,32,768]{2,1,0:T(8,128)}), f32[4,32,768]{2,1,0:T(8,128)S(1)}, u32[]{:S(2)}, u32[]{:S(2)}) %all-to-all-start.2) | async-done | bytes 393248 | tf_op jit(solution)/shard_map/all_to_all | solution.py:593
  50.9 2.8 %all-to-all-start.1 = ((f32[32,24,128]{2,1,0:T(8,128)}), f32[32,24,128]{2,1,0:T(8,128)S(1)}, u32[]{:S(2)}, u32[]{:S(2)}) async-start(f32[32,24,128]{2,1,0:T(8,128)} %get-tuple-element.20), calls=%async_computation.1 | async-start | bytes 786432 | tf_op jit(solution)/shard_map/all_to_all | solution.py:590
  53.7 0.1 dynamic-slice_convert_fusion
  53.8 0.1 dynamic_slice.7
  53.9 0.6 load.1
  54.5 11.0 %all-to-all-done.1.image_ref = f32[32,24,128]{2,1,0:T(8,128)S(1)} async-done(((f32[32,24,128]{2,1,0:T(8,128)}), f32[32,24,128]{2,1,0:T(8,128)S(1)}, u32[]{:S(2)}, u32[]{:S(2)}) %all-to-all-start.1) | async-done | bytes 393248 | tf_op jit(solution)/shard_map/all_to_all | solution.py:590
  65.5 0.1 broadcast_in_dim.25.live_ref
  65.6 4.8 %middle.1 = (f32[32,48,128]{2,1,0:T(8,128)S(1)}, f32[24,3,16,128]{3,2,1,0:T(8,128)S(1)}, f32[25,3,16,128]{3,2,1,0:T(8,128)S(1)}) custom-call(f32[32,24,128]{2,1,0:T(8,128)S(1)} %all-to-all-done.1.image_ref, f32[24,3,16,128]{3,2,1,0:T(8,128)S(1)} %get-tuple-element.22.base_ref, f32[16,128]{1,0:T(8,128)S(1)} %broadcast_in_dim.25.live_ref, ...), custom_call_target="tpu_custom_call" | custom-call | tf_op jit(solution)/shard_map/middle/pallas_call | solution.py:650
  70.4 23.3 %all_to_all.30.msg_ref = f32[32,48,128]{2,1,0:T(8,128)S(1)} all-to-all(f32[32,48,128]{2,1,0:T(8,128)S(1)} %get-tuple-element.24), channel_id=1, replica_groups=mesh['chaos'=8,'slab'=4] {'chaos','slab'}, dimensions={0} | all-to-all | bytes 1572864 | tf_op jit(solution)/shard_map/all_to_all | solution.py:590
  93.7 5.1 %mix.3 = f32[32,24,128]{2,1,0:T(8,128)S(1)} custom-call(s32[726]{0:T(1024)S(1)} %fusion.nodes_ref, s32[660]{0:T(1024)S(1)} %copy-done.12, f32[32,48,128]{2,1,0:T(8,128)S(1)} %all_to_all.30.msg_ref, f32[11,8,128]{2,1,0:T(8,128)S(1)} %get-tuple-element.25.mods_ref, bf16[256,384]{1,0:T(8,128)(2,1)S(1)} %copy-done.5, bf16[384,128]{1,0:T(8,128)(2,1)S(1)} %copy-done.6), custom_call_target="tpu_custom_call" | custom-call | tf_op jit(solution)/shard_map/mix/pallas_call | solution.py:658
  98.8 16.0 %all_to_all.31.image_ref = f32[32,24,128]{2,1,0:T(8,128)S(1)} all-to-all(f32[32,24,128]{2,1,0:T(8,128)S(1)} %mix.3), channel_id=1, replica_groups=mesh['chaos'=8,'slab'=4] {'chaos','slab'}, dimensions={0} | all-to-all | bytes 786432 | tf_op jit(solution)/shard_map/all_to_all | solution.py:590
  114.8 4.8 %end.1 = f32[4,56,768]{2,1,0:T(8,128)} custom-call(f32[32,24,128]{2,1,0:T(8,128)S(1)} %all_to_all.31.image_ref, f32[24,3,16,128]{3,2,1,0:T(8,128)S(1)} %get-tuple-element.26.base_ref, f32[16,128]{1,0:T(8,128)S(1)} %broadcast_in_dim.25.live_ref, f32[24,16,128]{2,1,0:T(8,128)S(1)} %get-tuple-element.23.mean_ref, bf16[128,256]{1,0:T(8,128)(2,1)S(1)} %copy-done.8, ...), custom_call_target="tpu_custom_call" | custom-call | tf_op jit(solution)/shard_map/end/pallas_call | solution.py:661
  119.6 4.0 %all-to-all-start.5 = ((f32[4,56,768]{2,1,0:T(8,128)}), f32[4,56,768]{2,1,0:T(8,128)S(1)}, u32[]{:S(2)}, u32[]{:S(2)}) async-start(f32[4,56,768]{2,1,0:T(8,128)} %end.1), calls=%async_computation.5 | async-start | bytes 1376256 | tf_op jit(solution)/shard_map/all_to_all | solution.py:593
  123.6 0.1 fusion.1
  123.7 0.1 copy.18.live_ref
  123.8 19.0 %all-to-all-done.5.in_ref = f32[4,56,768]{2,1,0:T(8,128)S(1)} async-done(((f32[4,56,768]{2,1,0:T(8,128)}), f32[4,56,768]{2,1,0:T(8,128)S(1)}, u32[]{:S(2)}, u32[]{:S(2)}) %all-to-all-start.5) | async-done | bytes 688160 | tf_op jit(solution)/shard_map/all_to_all | solution.py:593
  142.8 1.1 finish.1
  (28 shorter events, 0.1 us)
Async XLA Ops:
  0.6 0.7 copy-start.14
  1.4 1.0 copy-start.1
  2.4 1.0 copy-start.3
  3.4 0.8 copy-start.11
  6.8 7.3 %copy-start.7 = (f32[36,3,768]{2,0,1:T(8,128)S(1)}, f32[36,3,768]{2,0,1:T(8,128)}, u32[]{:S(2)}) copy-start(f32[36,3,768]{2,0,1:T(8,128)} %param.16) | copy-start | bytes 995332
  6.8 26.9 %all-to-all-start = ((f32[32,48,128]{2,1,0:T(8,128)}), f32[32,48,128]{2,1,0:T(8,128)S(1)}, u32[]{:S(2)}, u32[]{:S(2)}) async-start(f32[32,48,128]{2,1,0:T(8,128)} %start.1), calls=%async_computation | async-start | bytes 1572864 | tf_op jit(solution)/shard_map/all_to_all | solution.py:590
  14.1 0.9 copy-start.13
  14.1 0.8 copy-start.15
  15.2 23.1 %copy-start.5 = (bf16[256,384]{1,0:T(8,128)(2,1)S(1)}, bf16[256,384]{1,0:T(8,128)(2,1)}, u32[]{:S(2)}) copy-start(bf16[256,384]{1,0:T(8,128)(2,1)} %constant.47.clone.grad_ref) | copy-start | bytes 589828
  15.2 23.1 %copy-start.6 = (bf16[384,128]{1,0:T(8,128)(2,1)S(1)}, bf16[384,128]{1,0:T(8,128)(2,1)}, u32[]{:S(2)}) copy-start(bf16[384,128]{1,0:T(8,128)(2,1)} %constant.48.clone.div_ref) | copy-start | bytes 294916
  15.2 23.1 %copy-start.10 = (bf16[4,128,128]{2,1,0:T(8,128)(2,1)S(1)}, bf16[4,128,128]{2,1,0:T(8,128)(2,1)}, u32[]{:S(2)}) copy-start(bf16[4,128,128]{2,1,0:T(8,128)(2,1)} %constant.44.clone.mtab_ref) | copy-start | bytes 393220
  33.7 4.5 %copy-start.12 = (s32[660]{0:T(1024)S(1)}, s32[660]{0:T(1024)}, u32[]{:S(2)}) copy-start(s32[660]{0:T(1024)} %constant.49.clone.level_ref) | copy-start | bytes 7924
  33.7 17.1 %all-to-all-start.2 = ((f32[4,32,768]{2,1,0:T(8,128)}), f32[4,32,768]{2,1,0:T(8,128)S(1)}, u32[]{:S(2)}, u32[]{:S(2)}) async-start(f32[4,32,768]{2,1,0:T(8,128)} %split.1), calls=%async_computation.2 | async-start | bytes 786432 | tf_op jit(solution)/shard_map/all_to_all | solution.py:593
  50.9 14.7 %copy-start = (bf16[512,512]{1,0:T(8,128)(2,1)S(1)}, bf16[512,512]{1,0:T(8,128)(2,1)}, u32[]{:S(2)}) copy-start(bf16[512,512]{1,0:T(8,128)(2,1)} %constant.43.clone.unpack_ref) | copy-start | bytes 1572868
  50.9 14.7 %copy-start.8 = (bf16[128,256]{1,0:T(8,128)(2,1)S(1)}, bf16[128,256]{1,0:T(8,128)(2,1)}, u32[]{:S(2)}) copy-start(bf16[128,256]{1,0:T(8,128)(2,1)} %constant.45.clone.slope_ref) | copy-start | bytes 196612
  50.9 14.7 %copy-start.9 = (bf16[256,128]{1,0:T(8,128)(2,1)S(1)}, bf16[256,128]{1,0:T(8,128)(2,1)}, u32[]{:S(2)}) copy-start(bf16[256,128]{1,0:T(8,128)(2,1)} %constant.46.clone.back_ref) | copy-start | bytes 196612
  50.9 14.6 %all-to-all-start.1 = ((f32[32,24,128]{2,1,0:T(8,128)}), f32[32,24,128]{2,1,0:T(8,128)S(1)}, u32[]{:S(2)}, u32[]{:S(2)}) async-start(f32[32,24,128]{2,1,0:T(8,128)} %get-tuple-element.20), calls=%async_computation.1 | async-start | bytes 786432 | tf_op jit(solution)/shard_map/all_to_all | solution.py:590
  53.7 11.9 %copy-start.2 = (bf16[384,512]{1,0:T(8,128)(2,1)S(1)}, bf16[384,512]{1,0:T(8,128)(2,1)}, u32[]{:S(2)}) copy-start(bf16[384,512]{1,0:T(8,128)(2,1)} %constant.42.clone.pack_ref) | copy-start | bytes 1179652
  119.6 23.2 %copy-start.4 = (f32[36,3,768]{2,0,1:T(8,128)S(1)}, f32[36,3,768]{2,0,1:T(8,128)}, u32[]{:S(2)}) copy-start(f32[36,3,768]{2,0,1:T(8,128)} %param.15) | copy-start | bytes 995332
  119.6 23.2 %all-to-all-start.5 = ((f32[4,56,768]{2,1,0:T(8,128)}), f32[4,56,768]{2,1,0:T(8,128)S(1)}, u32[]{:S(2)}, u32[]{:S(2)}) async-start(f32[4,56,768]{2,1,0:T(8,128)} %end.1), calls=%async_computation.5 | async-start | bytes 1376256 | tf_op jit(solution)/shard_map/all_to_all | solution.py:593

commit v6 on v5

--- a/solution.py
+++ b/solution.py
@@ -288,10 +288,12 @@
     return [jnp.concatenate(pieces, axis=1) if len(pieces) > 1 else pieces[0] for pieces in zip(*piece_of)]
 
 
-def start_kernel(plan, place_ref, in_ref, mean_ref, modes_ref, pack_ref, msg_ref, lhs, rows, moduli):
-    moduli[...] = jnp.zeros(moduli.shape, F32)
-    moduli[0:1] = mean_ref[...]
-    moduli[1:FIELDS] = modes_ref[...]
+def start_kernel(plan, place_ref, in_hbm, mean_hbm, modes_hbm, pack_hbm, msg_ref, lhs, rows, moduli, in_ref, mean_ref, modes_ref, pack_ref, arrived):
+    pairs = ((in_hbm, in_ref), (pack_hbm, pack_ref), (mean_hbm, mean_ref), (modes_hbm, modes_ref))
+    copies = [pltpu.make_async_copy(source, target, arrived.at[i]) for i, (source, target) in enumerate(pairs)]
+    for copy in copies:
+        copy.start()
+    copies[0].wait()
     for a in range(PLANE // 128):
         for c in range(3):
             pieces = rows_at(
@@ -306,35 +308,44 @@
             for b, piece in enumerate(pieces):
                 x = 4 * a + b
                 lhs[x * plan.hs : x * plan.hs + plan.sp, c * plan.ls : (c + 1) * plan.ls] = piece
+    copies[1].wait()
     pick_into(rows, lhs, pack_ref)
     store_message(plan, rows, msg_ref)
+    copies[2].wait()
+    copies[3].wait()
+    moduli[...] = jnp.zeros(moduli.shape, F32)
+    for a in range(PLANE // 128):
+        moduli[0:1, a * 128 : (a + 1) * 128] = mean_ref[a : a + 1, :]
+    moduli[1:FIELDS] = modes_ref[...]
     store_moduli(plan, jnp.minimum(place_ref[0], plan.per_share - 1), moduli, msg_ref)
 
 
-def split_kernel(plan, in_ref, mean_ref, out_ref):
+def split_kernel(plan, place_ref, in_ref, mean_ref, *refs):
+    out_refs, groups = refs[: plan.slab], refs[plan.slab]
     for group in range(plan.slab):
-        out_ref[group, 3 * plan.sp : 3 * plan.sp + 1, :] = mean_ref[...]
-        for c in range(3):
-            out_ref[group, c * plan.sp : (c + 1) * plan.sp, :] = in_ref[
-                c, group * plan.sp : (group + 1) * plan.sp, :
-            ]
-
-
-def load_kernel(plan, in_ref, out_ref, mean_ref):
+        step = lax.rem(group + plan.slab - place_ref[1], plan.slab)
+        for c in range(3):
+            groups[step, c * plan.sp : (c + 1) * plan.sp, :] = in_ref[c, group * plan.sp : (group + 1) * plan.sp, :]
+        groups[step, 3 * plan.sp : 3 * plan.sp + 1, :] = mean_ref[...]
+    for step, out_ref in enumerate(out_refs):
+        out_ref[...] = groups[step]
+
+
+def load_kernel(plan, place_ref, *refs):
+    in_refs, (out_ref, mean_ref, planes) = refs[: plan.slab], refs[plan.slab :]
+    for step, in_ref in enumerate(in_refs):
+        planes[lax.rem(place_ref[1] + (plan.slab - step), plan.slab)] = in_ref[...]
     for a in range(PLANE // 128):
+        lanes = slice(a * 128, (a + 1) * 128)
         pieces = rows_at(
-            swap_quarters(
-                [in_ref[4 * t + i, 3 * plan.sp : 3 * plan.sp + 1, a * 128 : (a + 1) * 128] for i in range(4)]
-            )
+            swap_quarters([planes[4 * t + i, 3 * plan.sp : 3 * plan.sp + 1, lanes] for i in range(4)])
             for t in range(plan.nz // 4)
         )
         for b, piece in enumerate(pieces):
             mean_ref[4 * a + b] = jnp.broadcast_to(piece, (plan.hs, plan.ls))
         for c in range(3):
             pieces = rows_at(
-                swap_quarters(
-                    [in_ref[4 * t + i, c * plan.sp : (c + 1) * plan.sp, a * 128 : (a + 1) * 128] for i in range(4)]
-                )
+                swap_quarters([planes[4 * t + i, c * plan.sp : (c + 1) * plan.sp, lanes] for i in range(4)])
                 for t in range(plan.nz // 4)
             )
             for b, piece in enumerate(pieces):
@@ -594,15 +605,16 @@
 
     smem = pl.BlockSpec(memory_space=pltpu.SMEM)
     vmem = pl.BlockSpec(memory_space=pltpu.VMEM)
-
-    def call(kernel, name, in_specs, out_shape, scratch_shapes):
+    hbm = pl.BlockSpec(memory_space=pltpu.HBM)
+
+    def call(kernel, name, in_specs, out_shape, scratch_shapes, grant=16 if n <= 64 else 60):
         return pl.pallas_call(
             kernel,
             out_shape=out_shape,
             in_specs=in_specs,
             out_specs=jax.tree.map(lambda _: vmem, out_shape),
             scratch_shapes=scratch_shapes,
-            compiler_params=pltpu.CompilerParams(vmem_limit_bytes=(16 if plan.positions <= 512 and n <= 64 else 60) * MIB),
+            compiler_params=pltpu.CompilerParams(vmem_limit_bytes=grant * MIB),
             name=name,
         )
 
@@ -619,10 +631,20 @@
     msg = call(
         functools.partial(start_kernel, plan),
         "start",
-        [smem, vmem, vmem, vmem, vmem],
+        [smem, hbm, hbm, hbm, hbm],
         message,
-        [narrow, wide, pltpu.VMEM((16, PLANE), F32)],
-    )(place, by_component(displacement), mean_row, modes, pack)
+        [
+            narrow,
+            wide,
+            pltpu.VMEM((16, PLANE), F32),
+            pltpu.VMEM((3, slots_pad, PLANE), F32),
+            pltpu.VMEM((PLANE // 128, 128), F32),
+            pltpu.VMEM((KL, PLANE), F32),
+            pltpu.VMEM(pack.shape, BF16),
+            pltpu.SemaphoreType.DMA((4,)),
+        ],
+        60,
+    )(place, by_component(displacement), mean_modulus.reshape(PLANE // 128, 128), modes, pack)
     levels = jnp.asarray(level, jnp.int32)
     mix_scratch = [
         pltpu.VMEM((plan.positions, 3, 8, lanes), F32),
@@ -631,15 +653,15 @@
     ]
 
     arrived = everyone(msg)
-    flat, parts = array(slab, plan.rows_flat, PLANE), array(3, slots_pad, PLANE)
-    load_flat = call(functools.partial(split_kernel, plan), "split", [vmem, vmem], flat, [])(
-        by_component(load), mean_row
-    )
-    load_flat, nodes, place = lax.optimization_barrier((load_flat, nodes, place))
-    load_flat, arrived = lax.optimization_barrier((load_flat, arrived))
-    load_s, mean_s = call(functools.partial(load_kernel, plan), "load", [vmem], (grid_field, array(NX, hs, ls)), [])(
-        column(load_flat)
-    )
+    flat, parts = array(plan.rows_flat, PLANE), array(3, slots_pad, PLANE)
+    load_flat = call(
+        functools.partial(split_kernel, plan), "split", [smem, vmem, vmem], (flat,) * slab, [pltpu.VMEM((slab, plan.rows_flat, PLANE), F32)]
+    )(place, by_component(load), mean_row)
+    load_flat = [load_flat[0]] + [
+        lax.ppermute(load_flat[step], "slab", [(z, (z + step) % slab) for z in range(slab)])
+        for step in range(1, slab)
+    ]
+    arrived, nodes = lax.optimization_barrier((arrived, nodes))
     first_image, mods = call(
         functools.partial(first_mix_kernel, plan, len(low), 3),
         "mix",
@@ -647,6 +669,14 @@
         (image, array(FIELDS, 8, lanes)),
         mix_scratch + [pltpu.VMEM((n, plan.rows_in, lanes), F32)],
     )(place, nodes, levels, arrived.reshape(n * plan.rows_in, lanes), mtab, grads, divs)
+    load_flat, first_image = lax.optimization_barrier((load_flat, first_image))
+    load_s, mean_s = call(
+        functools.partial(load_kernel, plan),
+        "load",
+        [smem] + [vmem] * slab,
+        (grid_field, array(NX, hs, ls)),
+        [pltpu.VMEM((slab, plan.rows_flat, PLANE), F32)],
+    )(place, *load_flat)
     msg, residual_s, update_s = call(
         functools.partial(middle_kernel, plan),
         "middle",

time: 144 us -> 140 us (0.972)
  waiting for transfers between devices: 53.3 us -> 46.8 us
  local copies, waits for them, and re-layouts: 3.78 us -> 0.35 us
  starting transfers between devices: 18.5 us -> 21.3 us
  Pallas kernels: 27.8 us -> 29.9 us
    ppermute x0 -> x3, starting transfers between devices: none -> 5.65 us  [per_device(): lax.ppermute(load_flat[step], 'slab', [(z, (z + step) % slab) for z in ra...]
    all_to_all x2 -> x1, waiting for transfers between devices: 23.7 us -> 19 us  [column(): return lax.all_to_all(values, 'slab', 0, 0, tiled=True)]
    all_to_all x2 -> x1, starting transfers between devices: 8.49 us -> 3.99 us  [column(): return lax.all_to_all(values, 'slab', 0, 0, tiled=True)]
    unnamed x32 -> x28, local copies, waits for them, and re-layouts: 3.52 us -> 0.09 us
    all_to_all x2, waiting for transfers between devices: 29.6 us -> 27.7 us  [everyone(): return lax.all_to_all(values, ('chaos', 'slab'), 0, 0, tiled=True)]
    pallas_call x3, Pallas kernels: 4.05 us -> 5.82 us  [the longest x1 4.03 us: per_device(): call(functools.partial(start_kernel, plan), 'start', [smem, hbm, hbm, hbm...]
    all_to_all x2, starting transfers between devices: 10.1 us -> 11.7 us  [everyone(): return lax.all_to_all(values, ('chaos', 'slab'), 0, 0, tiled=True)]
  transfers between devices with their start and end apart: 4 -> 6, of which waited for: 4 -> 3; matrix products, arithmetic and copies ran while one was open for 0% -> 0% of each run, Pallas kernels for 7% -> 7%
where the time goes in v6:
time: 140 us; the launch traced here: 139 us
  waiting for transfers between devices  46.8 us (33%)
  blocking collectives  39.3 us (28%)
  Pallas kernels  29.9 us (21%)
  starting transfers between devices  21.3 us (15%)
    all_to_all x2, blocking collectives, everyone(): return lax.all_to_all(values, ('chaos', 'slab'), 0, 0, tiled=True)  39.3 us
    all_to_all x2, waiting for transfers between devices, everyone(): return lax.all_to_all(values, ('chaos', 'slab'), 0, 0, tiled=True)  27.7 us
    all_to_all x1, waiting for transfers between devices, column(): return lax.all_to_all(values, 'slab', 0, 0, tiled=True)  19 us
    all_to_all x2, starting transfers between devices, everyone(): return lax.all_to_all(values, ('chaos', 'slab'), 0, 0, tiled=True)  11.7 us
    pallas_call x1, Pallas kernels, per_device(): call(functools.partial(first_mix_kernel, plan, len(low), 3), 'mix', [smem...  7.96 us
    ppermute x3, starting transfers between devices, per_device(): lax.ppermute(load_flat[step], 'slab', [(z, (z + step) % slab) for z in ra...  5.65 us
    pallas_call x1, Pallas kernels, per_device(): call(functools.partial(mix_kernel, plan, len(low), 2), 'mix', [smem, smem...  5.16 us
    pallas_call x1, Pallas kernels, per_device(): call(functools.partial(end_kernel, plan), 'end', [vmem] * 8, array(slab,...  5.02 us
  transfers between devices with their start and end apart: 6, of which 3 were waited for; matrix products, arithmetic and copies ran while one was open for 0% of the time, Pallas kernels for 7%

profile of v6, /device:TPU:0, one launch (start us, length us, event | category | flops | bytes accessed | tf_op | source)
XLA Modules:
  0.0 139.4 jit_solution(2566837702939016308)
XLA Ops:
  0.6 0.6 pad_add_fusion.place_ref
  1.2 4.0 %start.1 = f32[32,48,128]{2,1,0:T(8,128)} custom-call(s32[2]{0:T(128)} %pad_add_fusion.place_ref, f32[3,36,768]{2,1,0:T(8,128)} %bitcast.11, f32[6,128]{1,0:T(8,128)} %bitcast.14, f32[10,768]{1,0:T(8,128)} %modes_hbm.1, bf16[384,512]{1,0:T(8,128)(2,1)} %constant.42.clone.pack_hbm.pack_ref), custom_call_target="tpu_custom_call" | custom-call | tf_op jit(solution)/shard_map/start/pallas_call | solution.py:631
  5.3 0.0 copy-start.8
  5.3 7.3 %all-to-all-start = ((f32[32,48,128]{2,1,0:T(8,128)}), f32[32,48,128]{2,1,0:T(8,128)S(1)}, u32[]{:S(2)}, u32[]{:S(2)}) async-start(f32[32,48,128]{2,1,0:T(8,128)} %start.1), calls=%async_computation | async-start | bytes 1572864 | tf_op jit(solution)/shard_map/all_to_all | solution.py:601
  12.7 0.0 copy-start.3
  12.7 0.0 copy-start.13
  12.7 0.0 copy-start.4
  12.7 0.6 split.1
  13.4 1.8 %collective-permute-start = (f32[32,768]{1,0:T(8,128)S(1)}, f32[32,768]{1,0:T(8,128)S(1)}, u32[]{:S(2)}, u32[]{:S(2)}) collective-permute-start(f32[32,768]{1,0:T(8,128)S(1)} %get-tuple-element.24), channel_id=1, source_target_pairs={{0,1},{1,2},{2,3},{3,0},{4,5},{5,6},{6,7},{7,4},{8,9},{9,10},{10,1... | collective-permute-start | bytes 294920 | tf_op jit(solution)/shard_map/ppermute | solution.py:661
  15.2 2.4 %collective-permute-start.1 = (f32[32,768]{1,0:T(8,128)S(1)}, f32[32,768]{1,0:T(8,128)S(1)}, u32[]{:S(2)}, u32[]{:S(2)}) collective-permute-start(f32[32,768]{1,0:T(8,128)S(1)} %get-tuple-element.25), channel_id=1, source_target_pairs={{0,2},{1,3},{2,0},{3,1},{4,6},{5,7},{6,4},{7,5},{8,10},{9,11},{10,... | collective-permute-start | bytes 294920 | tf_op jit(solution)/shard_map/ppermute | solution.py:661
  17.6 1.4 %collective-permute-start.2 = (f32[32,768]{1,0:T(8,128)S(1)}, f32[32,768]{1,0:T(8,128)S(1)}, u32[]{:S(2)}, u32[]{:S(2)}) collective-permute-start(f32[32,768]{1,0:T(8,128)S(1)} %get-tuple-element.26), channel_id=1, source_target_pairs={{0,3},{1,0},{2,1},{3,2},{4,7},{5,4},{6,5},{7,6},{8,11},{9,8},{10,9... | collective-permute-start | bytes 294920 | tf_op jit(solution)/shard_map/ppermute | solution.py:661
  19.0 0.2 fusion.nodes_ref
  19.2 17.3 %all-to-all-done = f32[32,48,128]{2,1,0:T(8,128)S(1)} async-done(((f32[32,48,128]{2,1,0:T(8,128)}), f32[32,48,128]{2,1,0:T(8,128)S(1)}, u32[]{:S(2)}, u32[]{:S(2)}) %all-to-all-start) | async-done | bytes 786464 | tf_op jit(solution)/shard_map/all_to_all | solution.py:601
  36.5 8.0 %mix.2 = (f32[32,24,128]{2,1,0:T(8,128)}, f32[11,8,128]{2,1,0:T(8,128)S(1)}) custom-call(s32[2]{0:T(128)S(1)} %copy-done.10, s32[726]{0:T(1024)S(1)} %fusion.nodes_ref, s32[660]{0:T(1024)S(1)} %copy-done.9, f32[1536,128]{1,0:T(8,128)S(1)} %bitcast.10, bf16[4,128,128]{2,1,0:T(8,128)(2,1)S(1)} %copy-done.8, bf16[256,384]{1,0:T(8,128)(2,1)S(1)} %copy-done.3, ...), custom_call_target="tpu_custom_call" | custom-call | tf_op jit(solution)/shard_map/mix/pallas_call | solution.py:665
  44.5 0.0 copy-start
  44.5 0.0 copy-start.6
  44.5 4.4 %all-to-all-start.1 = ((f32[32,24,128]{2,1,0:T(8,128)}), f32[32,24,128]{2,1,0:T(8,128)S(1)}, u32[]{:S(2)}, u32[]{:S(2)}) async-start(f32[32,24,128]{2,1,0:T(8,128)} %get-tuple-element.29), calls=%async_computation.1 | async-start | bytes 786432 | tf_op jit(solution)/shard_map/all_to_all | solution.py:601
  48.9 0.1 dynamic-slice_convert_fusion
  49.0 0.1 dynamic_slice.7
  49.1 1.2 load.1
  50.3 10.5 %all-to-all-done.1.image_ref = f32[32,24,128]{2,1,0:T(8,128)S(1)} async-done(((f32[32,24,128]{2,1,0:T(8,128)}), f32[32,24,128]{2,1,0:T(8,128)S(1)}, u32[]{:S(2)}, u32[]{:S(2)}) %all-to-all-start.1) | async-done | bytes 393248 | tf_op jit(solution)/shard_map/all_to_all | solution.py:601
  60.7 0.1 broadcast_in_dim.25.live_ref
  60.8 4.8 %middle.1 = (f32[32,48,128]{2,1,0:T(8,128)S(1)}, f32[24,3,16,128]{3,2,1,0:T(8,128)S(1)}, f32[25,3,16,128]{3,2,1,0:T(8,128)S(1)}) custom-call(f32[32,24,128]{2,1,0:T(8,128)S(1)} %all-to-all-done.1.image_ref, f32[24,3,16,128]{3,2,1,0:T(8,128)S(1)} %get-tuple-element.34.base_ref, f32[16,128]{1,0:T(8,128)S(1)} %broadcast_in_dim.25.live_ref, ...), custom_call_target="tpu_custom_call" | custom-call | tf_op jit(solution)/shard_map/middle/pallas_call | solution.py:680
  65.7 23.3 %all_to_all.25.msg_ref = f32[32,48,128]{2,1,0:T(8,128)S(1)} all-to-all(f32[32,48,128]{2,1,0:T(8,128)S(1)} %get-tuple-element.36), channel_id=1, replica_groups=mesh['chaos'=8,'slab'=4] {'chaos','slab'}, dimensions={0} | all-to-all | bytes 1572864 | tf_op jit(solution)/shard_map/all_to_all | solution.py:601
  89.0 5.2 %mix.3 = f32[32,24,128]{2,1,0:T(8,128)S(1)} custom-call(s32[726]{0:T(1024)S(1)} %fusion.nodes_ref, s32[660]{0:T(1024)S(1)} %copy-done.9, f32[32,48,128]{2,1,0:T(8,128)S(1)} %all_to_all.25.msg_ref, f32[11,8,128]{2,1,0:T(8,128)S(1)} %get-tuple-element.37.mods_ref, bf16[256,384]{1,0:T(8,128)(2,1)S(1)} %copy-done.3, bf16[384,128]{1,0:T(8,128)(2,1)S(1)} %copy-done.4), custom_call_target="tpu_custom_call" | custom-call | tf_op jit(solution)/shard_map/mix/pallas_call | solution.py:688
  94.1 16.0 %all_to_all.26.image_ref = f32[32,24,128]{2,1,0:T(8,128)S(1)} all-to-all(f32[32,24,128]{2,1,0:T(8,128)S(1)} %mix.3), channel_id=1, replica_groups=mesh['chaos'=8,'slab'=4] {'chaos','slab'}, dimensions={0} | all-to-all | bytes 786432 | tf_op jit(solution)/shard_map/all_to_all | solution.py:601
  110.1 5.0 %end.1 = f32[4,56,768]{2,1,0:T(8,128)} custom-call(f32[32,24,128]{2,1,0:T(8,128)S(1)} %all_to_all.26.image_ref, f32[24,3,16,128]{3,2,1,0:T(8,128)S(1)} %get-tuple-element.38.base_ref, f32[16,128]{1,0:T(8,128)S(1)} %broadcast_in_dim.25.live_ref, f32[24,16,128]{2,1,0:T(8,128)S(1)} %get-tuple-element.35.mean_ref, bf16[128,256]{1,0:T(8,128)(2,1)S(1)} %copy-done.6, ...), custom_call_target="tpu_custom_call" | custom-call | tf_op jit(solution)/shard_map/end/pallas_call | solution.py:691
  115.1 4.0 %all-to-all-start.4 = ((f32[4,56,768]{2,1,0:T(8,128)}), f32[4,56,768]{2,1,0:T(8,128)S(1)}, u32[]{:S(2)}, u32[]{:S(2)}) async-start(f32[4,56,768]{2,1,0:T(8,128)} %end.1), calls=%async_computation.4 | async-start | bytes 1376256 | tf_op jit(solution)/shard_map/all_to_all | solution.py:604
  119.1 0.1 fusion.1
  119.2 0.1 copy.18.live_ref
  119.3 19.0 %all-to-all-done.4.in_ref = f32[4,56,768]{2,1,0:T(8,128)S(1)} async-done(((f32[4,56,768]{2,1,0:T(8,128)}), f32[4,56,768]{2,1,0:T(8,128)S(1)}, u32[]{:S(2)}, u32[]{:S(2)}) %all-to-all-start.4) | async-done | bytes 688160 | tf_op jit(solution)/shard_map/all_to_all | solution.py:604
  138.3 1.1 finish.1
  (28 shorter events, 0.1 us)
Async XLA Ops:
  5.3 7.4 %copy-start.11 = (f32[768]{0:T(1024)S(1)}, f32[768]{0:T(1024)}, u32[]{:S(2)}) copy-start(f32[768]{0:T(1024)} %param.17) | copy-start | bytes 9220
  5.3 7.4 %copy-start.5 = (f32[36,3,768]{2,0,1:T(8,128)S(1)}, f32[36,3,768]{2,0,1:T(8,128)}, u32[]{:S(2)}) copy-start(f32[36,3,768]{2,0,1:T(8,128)} %param.16) | copy-start | bytes 995332
  5.3 7.4 %copy-start.10 = (s32[2]{0:T(128)S(1)}, s32[2]{0:T(128)}, u32[]{:S(2)}) copy-start(s32[2]{0:T(128)} %pad_add_fusion.place_ref) | copy-start | bytes 28
  5.3 31.2 %copy-start.8 = (bf16[4,128,128]{2,1,0:T(8,128)(2,1)S(1)}, bf16[4,128,128]{2,1,0:T(8,128)(2,1)}, u32[]{:S(2)}) copy-start(bf16[4,128,128]{2,1,0:T(8,128)(2,1)} %constant.44.clone.mtab_ref) | copy-start | bytes 393220
  5.3 31.1 %all-to-all-start = ((f32[32,48,128]{2,1,0:T(8,128)}), f32[32,48,128]{2,1,0:T(8,128)S(1)}, u32[]{:S(2)}, u32[]{:S(2)}) async-start(f32[32,48,128]{2,1,0:T(8,128)} %start.1), calls=%async_computation | async-start | bytes 1572864 | tf_op jit(solution)/shard_map/all_to_all | solution.py:601
  12.7 23.8 %copy-start.3 = (bf16[256,384]{1,0:T(8,128)(2,1)S(1)}, bf16[256,384]{1,0:T(8,128)(2,1)}, u32[]{:S(2)}) copy-start(bf16[256,384]{1,0:T(8,128)(2,1)} %constant.47.clone.grad_ref) | copy-start | bytes 589828
  12.7 6.3 %copy-start.13 = (s32[726]{0:T(1024)S(1)}, s32[726]{0:T(1024)}, u32[]{:S(2)}) copy-start(s32[726]{0:T(1024)} %constant.54) | copy-start | bytes 8716
  12.7 23.8 %copy-start.4 = (bf16[384,128]{1,0:T(8,128)(2,1)S(1)}, bf16[384,128]{1,0:T(8,128)(2,1)}, u32[]{:S(2)}) copy-start(bf16[384,128]{1,0:T(8,128)(2,1)} %constant.48.clone.div_ref) | copy-start | bytes 294916
  13.4 5.7 %copy-start.12 = (s32[288]{0:T(512)S(1)}, s32[288]{0:T(512)}, u32[]{:S(2)}) copy-start(s32[288]{0:T(512)} %param.19) | copy-start | bytes 3460
  13.4 31.1 %collective-permute-start = (f32[32,768]{1,0:T(8,128)S(1)}, f32[32,768]{1,0:T(8,128)S(1)}, u32[]{:S(2)}, u32[]{:S(2)}) collective-permute-start(f32[32,768]{1,0:T(8,128)S(1)} %get-tuple-element.24), channel_id=1, source_target_pairs={{0,1},{1,2},{2,3},{3,0},{4,5},{5,6},{6,7},{7,4},{8,9},{9,10},{10,1... | collective-permute-start | bytes 294920 | tf_op jit(solution)/shard_map/ppermute | solution.py:661
  15.2 29.3 %collective-permute-start.1 = (f32[32,768]{1,0:T(8,128)S(1)}, f32[32,768]{1,0:T(8,128)S(1)}, u32[]{:S(2)}, u32[]{:S(2)}) collective-permute-start(f32[32,768]{1,0:T(8,128)S(1)} %get-tuple-element.25), channel_id=1, source_target_pairs={{0,2},{1,3},{2,0},{3,1},{4,6},{5,7},{6,4},{7,5},{8,10},{9,11},{10,... | collective-permute-start | bytes 294920 | tf_op jit(solution)/shard_map/ppermute | solution.py:661
  17.6 18.9 %copy-start.9 = (s32[660]{0:T(1024)S(1)}, s32[660]{0:T(1024)}, u32[]{:S(2)}) copy-start(s32[660]{0:T(1024)} %constant.49.clone.level_ref) | copy-start | bytes 7924
  17.6 26.8 %collective-permute-start.2 = (f32[32,768]{1,0:T(8,128)S(1)}, f32[32,768]{1,0:T(8,128)S(1)}, u32[]{:S(2)}, u32[]{:S(2)}) collective-permute-start(f32[32,768]{1,0:T(8,128)S(1)} %get-tuple-element.26), channel_id=1, source_target_pairs={{0,3},{1,0},{2,1},{3,2},{4,7},{5,4},{6,5},{7,6},{8,11},{9,8},{10,9... | collective-permute-start | bytes 294920 | tf_op jit(solution)/shard_map/ppermute | solution.py:661
  44.5 16.3 %copy-start = (bf16[512,512]{1,0:T(8,128)(2,1)S(1)}, bf16[512,512]{1,0:T(8,128)(2,1)}, u32[]{:S(2)}) copy-start(bf16[512,512]{1,0:T(8,128)(2,1)} %constant.43.clone.unpack_ref) | copy-start | bytes 1572868
  44.5 16.3 %copy-start.6 = (bf16[128,256]{1,0:T(8,128)(2,1)S(1)}, bf16[128,256]{1,0:T(8,128)(2,1)}, u32[]{:S(2)}) copy-start(bf16[128,256]{1,0:T(8,128)(2,1)} %constant.45.clone.slope_ref) | copy-start | bytes 196612
  44.5 16.3 %copy-start.7 = (bf16[256,128]{1,0:T(8,128)(2,1)S(1)}, bf16[256,128]{1,0:T(8,128)(2,1)}, u32[]{:S(2)}) copy-start(bf16[256,128]{1,0:T(8,128)(2,1)} %constant.46.clone.back_ref) | copy-start | bytes 196612
  44.5 16.2 %all-to-all-start.1 = ((f32[32,24,128]{2,1,0:T(8,128)}), f32[32,24,128]{2,1,0:T(8,128)S(1)}, u32[]{:S(2)}, u32[]{:S(2)}) async-start(f32[32,24,128]{2,1,0:T(8,128)} %get-tuple-element.29), calls=%async_computation.1 | async-start | bytes 786432 | tf_op jit(solution)/shard_map/all_to_all | solution.py:601
  48.9 11.9 %copy-start.1 = (bf16[384,512]{1,0:T(8,128)(2,1)S(1)}, bf16[384,512]{1,0:T(8,128)(2,1)}, u32[]{:S(2)}) copy-start(bf16[384,512]{1,0:T(8,128)(2,1)} %constant.42.clone.pack_hbm.pack_ref) | copy-start | bytes 1179652
  115.1 23.2 %copy-start.2 = (f32[36,3,768]{2,0,1:T(8,128)S(1)}, f32[36,3,768]{2,0,1:T(8,128)}, u32[]{:S(2)}) copy-start(f32[36,3,768]{2,0,1:T(8,128)} %param.15) | copy-start | bytes 995332
  115.1 23.2 %all-to-all-start.4 = ((f32[4,56,768]{2,1,0:T(8,128)}), f32[4,56,768]{2,1,0:T(8,128)S(1)}, u32[]{:S(2)}, u32[]{:S(2)}) async-start(f32[4,56,768]{2,1,0:T(8,128)} %end.1), calls=%async_computation.4 | async-start | bytes 1376256 | tf_op jit(solution)/shard_map/all_to_all | solution.py:604

commit v7 on v6

--- a/solution.py
+++ b/solution.py
@@ -288,7 +288,7 @@
     return [jnp.concatenate(pieces, axis=1) if len(pieces) > 1 else pieces[0] for pieces in zip(*piece_of)]
 
 
-def start_kernel(plan, place_ref, in_hbm, mean_hbm, modes_hbm, pack_hbm, msg_ref, lhs, rows, moduli, in_ref, mean_ref, modes_ref, pack_ref, arrived):
+def start_kernel(plan, in_hbm, mean_hbm, modes_hbm, pack_hbm, msg_ref, lhs, rows, moduli, in_ref, mean_ref, modes_ref, pack_ref, arrived):
     pairs = ((in_hbm, in_ref), (pack_hbm, pack_ref), (mean_hbm, mean_ref), (modes_hbm, modes_ref))
     copies = [pltpu.make_async_copy(source, target, arrived.at[i]) for i, (source, target) in enumerate(pairs)]
     for copy in copies:
@@ -317,13 +317,13 @@
     for a in range(PLANE // 128):
         moduli[0:1, a * 128 : (a + 1) * 128] = mean_ref[a : a + 1, :]
     moduli[1:FIELDS] = modes_ref[...]
-    store_moduli(plan, jnp.minimum(place_ref[0], plan.per_share - 1), moduli, msg_ref)
-
-
-def split_kernel(plan, place_ref, in_ref, mean_ref, *refs):
+    store_moduli(plan, jnp.minimum(lax.axis_index("chaos"), plan.per_share - 1), moduli, msg_ref)
+
+
+def split_kernel(plan, in_ref, mean_ref, *refs):
     out_refs, groups = refs[: plan.slab], refs[plan.slab]
     for group in range(plan.slab):
-        step = lax.rem(group + plan.slab - place_ref[1], plan.slab)
+        step = lax.rem(group + plan.slab - lax.axis_index("slab"), plan.slab)
         for c in range(3):
             groups[step, c * plan.sp : (c + 1) * plan.sp, :] = in_ref[c, group * plan.sp : (group + 1) * plan.sp, :]
         groups[step, 3 * plan.sp : 3 * plan.sp + 1, :] = mean_ref[...]
@@ -331,10 +331,10 @@
         out_ref[...] = groups[step]
 
 
-def load_kernel(plan, place_ref, *refs):
+def load_kernel(plan, *refs):
     in_refs, (out_ref, mean_ref, planes) = refs[: plan.slab], refs[plan.slab :]
     for step, in_ref in enumerate(in_refs):
-        planes[lax.rem(place_ref[1] + (plan.slab - step), plan.slab)] = in_ref[...]
+        planes[lax.rem(lax.axis_index("slab") + (plan.slab - step), plan.slab)] = in_ref[...]
     for a in range(PLANE // 128):
         lanes = slice(a * 128, (a + 1) * 128)
         pieces = rows_at(
@@ -352,15 +352,18 @@
                 out_ref[4 * a + b, c, 0 : plan.sp, :] = piece
 
 
-def finish_kernel(plan, in_ref, live_ref, start_ref, total_ref, residual_ref):
+def finish_kernel(plan, live_ref, start_ref, *refs):
+    piece_refs, (total_ref, residual_ref, groups) = refs[: plan.slab], refs[plan.slab :]
+    for step, piece_ref in enumerate(piece_refs):
+        groups[lax.rem(lax.axis_index("slab") + (plan.slab - step), plan.slab)] = piece_ref[...]
     for group in range(plan.slab):
         here = slice(group * plan.sp, (group + 1) * plan.sp)
         live = jnp.broadcast_to(live_ref[here, :], (plan.sp, PLANE)) != 0.0
         for c in range(3):
-            total_ref[c, here, :] = jnp.where(live, start_ref[c, here, :], 0.0) + in_ref[
+            total_ref[c, here, :] = jnp.where(live, start_ref[c, here, :], 0.0) + groups[
                 group, c * plan.sp : (c + 1) * plan.sp, :
             ]
-            residual_ref[c, here, :] = in_ref[group, (3 + c) * plan.sp : (4 + c) * plan.sp, :]
+            residual_ref[c, here, :] = groups[group, (3 + c) * plan.sp : (4 + c) * plan.sp, :]
 
 
 def regrouped(plan, msg_ref, out_ref):
@@ -383,8 +386,8 @@
     lax.fori_loop(0, plan.chaos, one, 0, unroll=4)
 
 
-def first_mix_kernel(plan, low_count, parts, place_ref, nodes_ref, level_ref, msg_ref, mtab_ref, grad_ref, div_ref, out_ref, mods_ref, grad, flux, scaled, regroup):
-    gather_moduli(plan, place_ref[0] * plan.slab + place_ref[1], msg_ref, mtab_ref, mods_ref)
+def first_mix_kernel(plan, low_count, parts, nodes_ref, level_ref, msg_ref, mtab_ref, grad_ref, div_ref, out_ref, mods_ref, grad, flux, scaled, regroup):
+    gather_moduli(plan, lax.axis_index("chaos") * plan.slab + lax.axis_index("slab"), msg_ref, mtab_ref, mods_ref)
     regrouped(plan, msg_ref, regroup)
     mix_kernel(plan, low_count, parts, nodes_ref, level_ref, regroup, mods_ref, grad_ref, div_ref, out_ref, grad, flux, scaled)
 
@@ -555,14 +558,17 @@
             out_ref[4 * t + i, first : first + plan.sp, a * 128 : (a + 1) * 128] = piece[: plan.sp]
 
 
-def end_kernel(plan, image_ref, base_ref, live_ref, mean_ref, slope_ref, back_ref, unpack_ref, before_ref, out_ref, wide, narrow, residual, update, step):
+def end_kernel(plan, image_ref, base_ref, live_ref, mean_ref, slope_ref, back_ref, unpack_ref, before_ref, *refs):
+    out_refs, (wide, narrow, residual, update, step, planes) = refs[: plan.slab], refs[plan.slab :]
     unpack_image(plan, image_ref, unpack_ref, wide, narrow)
     add_image(plan, base_ref, live_ref, narrow, residual)
     smooth(plan, mean_ref, slope_ref, back_ref, residual, update, step)
     for a in range(PLANE // 128):
         for c in range(3):
-            flat_rows(plan, [update[4 * a + b, c] + before_ref[4 * a + b, c] for b in range(4)], out_ref, c * plan.sp, a)
-            flat_rows(plan, [residual[4 * a + b, c] for b in range(4)], out_ref, (3 + c) * plan.sp, a)
+            flat_rows(plan, [update[4 * a + b, c] + before_ref[4 * a + b, c] for b in range(4)], planes, c * plan.sp, a)
+            flat_rows(plan, [residual[4 * a + b, c] for b in range(4)], planes, (3 + c) * plan.sp, a)
+    for number, out_ref in enumerate(out_refs):
+        out_ref[...] = planes[lax.rem(lax.axis_index("slab") + number, plan.slab)]
 
 
 def per_device(displacement, load, mean_modulus, modes, owner):
@@ -590,7 +596,6 @@
     mtab = jnp.asarray(plan.modulus_table(), BF16)
     slopes, backs = (jnp.asarray(values, BF16) for values in (plan.slope_table(), plan.slope_table().T))
     grads, divs = (jnp.asarray(values, BF16) for values in (plan.gradient_table(), plan.divergence_table()))
-    place = jnp.stack([at_chaos, at_slab]).astype(jnp.int32)
 
     slots_pad = slab * sp
 
@@ -600,8 +605,11 @@
     def everyone(values):
         return lax.all_to_all(values, ("chaos", "slab"), 0, 0, tiled=True)
 
-    def column(values):
-        return lax.all_to_all(values, "slab", 0, 0, tiled=True)
+    def column(pieces):
+        return [pieces[0]] + [
+            lax.ppermute(pieces[step], "slab", [(z, (z + step) % slab) for z in range(slab)])
+            for step in range(1, slab)
+        ]
 
     smem = pl.BlockSpec(memory_space=pltpu.SMEM)
     vmem = pl.BlockSpec(memory_space=pltpu.VMEM)
@@ -631,7 +639,7 @@
     msg = call(
         functools.partial(start_kernel, plan),
         "start",
-        [smem, hbm, hbm, hbm, hbm],
+        [hbm, hbm, hbm, hbm],
         message,
         [
             narrow,
@@ -644,7 +652,7 @@
             pltpu.SemaphoreType.DMA((4,)),
         ],
         60,
-    )(place, by_component(displacement), mean_modulus.reshape(PLANE // 128, 128), modes, pack)
+    )(by_component(displacement), mean_modulus.reshape(PLANE // 128, 128), modes, pack)
     levels = jnp.asarray(level, jnp.int32)
     mix_scratch = [
         pltpu.VMEM((plan.positions, 3, 8, lanes), F32),
@@ -655,28 +663,25 @@
     arrived = everyone(msg)
     flat, parts = array(plan.rows_flat, PLANE), array(3, slots_pad, PLANE)
     load_flat = call(
-        functools.partial(split_kernel, plan), "split", [smem, vmem, vmem], (flat,) * slab, [pltpu.VMEM((slab, plan.rows_flat, PLANE), F32)]
-    )(place, by_component(load), mean_row)
-    load_flat = [load_flat[0]] + [
-        lax.ppermute(load_flat[step], "slab", [(z, (z + step) % slab) for z in range(slab)])
-        for step in range(1, slab)
-    ]
+        functools.partial(split_kernel, plan), "split", [vmem, vmem], (flat,) * slab, [pltpu.VMEM((slab, plan.rows_flat, PLANE), F32)]
+    )(by_component(load), mean_row)
+    load_flat = column(load_flat)
     arrived, nodes = lax.optimization_barrier((arrived, nodes))
     first_image, mods = call(
         functools.partial(first_mix_kernel, plan, len(low), 3),
         "mix",
-        [smem, smem, smem, vmem, vmem, vmem, vmem],
+        [smem, smem, vmem, vmem, vmem, vmem],
         (image, array(FIELDS, 8, lanes)),
         mix_scratch + [pltpu.VMEM((n, plan.rows_in, lanes), F32)],
-    )(place, nodes, levels, arrived.reshape(n * plan.rows_in, lanes), mtab, grads, divs)
+    )(nodes, levels, arrived.reshape(n * plan.rows_in, lanes), mtab, grads, divs)
     load_flat, first_image = lax.optimization_barrier((load_flat, first_image))
     load_s, mean_s = call(
         functools.partial(load_kernel, plan),
         "load",
-        [smem] + [vmem] * slab,
+        [vmem] * slab,
         (grid_field, array(NX, hs, ls)),
         [pltpu.VMEM((slab, plan.rows_flat, PLANE), F32)],
-    )(place, *load_flat)
+    )(*load_flat)
     msg, residual_s, update_s = call(
         functools.partial(middle_kernel, plan),
         "middle",
@@ -688,16 +693,17 @@
     second_image = call(
         functools.partial(mix_kernel, plan, len(low), 2), "mix", [smem, smem, vmem, vmem, vmem, vmem], image, mix_scratch
     )(nodes, levels, everyone(msg), mods, grads, divs)
+    around = pltpu.VMEM((slab, plan.rows_end, PLANE), F32)
     ending = call(
         functools.partial(end_kernel, plan),
         "end",
         [vmem] * 8,
-        array(slab, plan.rows_end, PLANE),
-        [wide, narrow, field_scratch, more_scratch, field_scratch],
+        (array(plan.rows_end, PLANE),) * slab,
+        [wide, narrow, field_scratch, more_scratch, field_scratch, around],
     )(everyone(second_image), residual_s, live_here, mean_s, slopes, backs, unpack, update_s)
     live_pad = jnp.pad(live_own.astype(F32), (0, slots_pad - slots_dev))
-    outs = call(functools.partial(finish_kernel, plan), "finish", [vmem] * 3, (parts, parts), [])(
-        column(ending), live_pad[:, None], by_component(displacement)
+    outs = call(functools.partial(finish_kernel, plan), "finish", [vmem] * (2 + slab), (parts, parts), [around])(
+        live_pad[:, None], by_component(displacement), *column(ending)
     )
     return tuple(jnp.transpose(values, (1, 0, 2))[:slots_dev] for values in outs)
 

time: 140 us -> 132 us (0.943)
  waiting for transfers between devices: 46.8 us -> 40.5 us
  Pallas kernels: 29.9 us -> 27.4 us
    all_to_all x1 -> x0, waiting for transfers between devices: 19 us -> none  [column(): return lax.all_to_all(values, 'slab', 0, 0, tiled=True)]
    ppermute x3 -> x6, waiting for transfers between devices: 0.01 us -> 11.7 us  [column(): lax.ppermute(pieces[step], 'slab', [(z, (z + step) % slab) for z in range...]
    ppermute x3 -> x6, starting transfers between devices: 5.65 us -> 10.4 us  [column(): lax.ppermute(pieces[step], 'slab', [(z, (z + step) % slab) for z in range...]
    all_to_all x1 -> x0, starting transfers between devices: 3.99 us -> none  [column(): return lax.all_to_all(values, 'slab', 0, 0, tiled=True)]
    pallas_call x5, Pallas kernels: 11.9 us -> 9.4 us  [the longest x1 4.2 us: per_device(): call(functools.partial(end_kernel, plan), 'end', [vmem] * 8, (array(plan....]
  transfers between devices with their start and end apart: 6 -> 8, of which waited for: 3 -> 4; matrix products, arithmetic and copies ran while one was open for 0% -> 0% of each run, Pallas kernels for 7% -> 7%
where the time goes in v7:
time: 132 us; the launch traced here: 131 us
  waiting for transfers between devices  40.5 us (31%)
  blocking collectives  39.3 us (30%)
  Pallas kernels  27.4 us (21%)
  starting transfers between devices  22.1 us (17%)
    all_to_all x2, blocking collectives, everyone(): return lax.all_to_all(values, ('chaos', 'slab'), 0, 0, tiled=True)  39.3 us
    all_to_all x2, waiting for transfers between devices, everyone(): return lax.all_to_all(values, ('chaos', 'slab'), 0, 0, tiled=True)  28.8 us
    ppermute x6, waiting for transfers between devices, column(): lax.ppermute(pieces[step], 'slab', [(z, (z + step) % slab) for z in range...  11.7 us
    all_to_all x2, starting transfers between devices, everyone(): return lax.all_to_all(values, ('chaos', 'slab'), 0, 0, tiled=True)  11.7 us
    ppermute x6, starting transfers between devices, column(): lax.ppermute(pieces[step], 'slab', [(z, (z + step) % slab) for z in range...  10.4 us
    pallas_call x1, Pallas kernels, per_device(): call(functools.partial(first_mix_kernel, plan, len(low), 3), 'mix', [smem...  7.96 us
    pallas_call x1, Pallas kernels, per_device(): call(functools.partial(mix_kernel, plan, len(low), 2), 'mix', [smem, smem...  5.15 us
    pallas_call x1, Pallas kernels, per_device(): call(functools.partial(middle_kernel, plan), 'middle', [vmem] * 8, (messa...  4.9 us
  transfers between devices with their start and end apart: 8, of which 4 were waited for; matrix products, arithmetic and copies ran while one was open for 0% of the time, Pallas kernels for 7%

profile of v7, /device:TPU:0, one launch (start us, length us, event | category | flops | bytes accessed | tf_op | source)
XLA Modules:
  0.0 130.9 jit_solution(11272691313485307486)
XLA Ops:
  0.6 3.4 %start.1 = f32[32,48,128]{2,1,0:T(8,128)} custom-call(f32[3,36,768]{2,1,0:T(8,128)} %bitcast.9, f32[6,128]{1,0:T(8,128)} %bitcast.12, f32[10,768]{1,0:T(8,128)} %modes_hbm.1, bf16[384,512]{1,0:T(8,128)(2,1)} %constant.42.clone.pack_hbm.pack_ref), custom_call_target="tpu_custom_call" | custom-call | tf_op jit(solution)/shard_map/start/pallas_call | solution.py:639
  4.0 0.0 copy-start.8
  4.1 7.3 %all-to-all-start = ((f32[32,48,128]{2,1,0:T(8,128)}), f32[32,48,128]{2,1,0:T(8,128)S(1)}, u32[]{:S(2)}, u32[]{:S(2)}) async-start(f32[32,48,128]{2,1,0:T(8,128)} %start.1), calls=%async_computation | async-start | bytes 1572864 | tf_op jit(solution)/shard_map/all_to_all | solution.py:606
  11.4 0.0 copy-start.3
  11.4 0.0 copy-start.12
  11.4 0.1 split.1
  11.6 1.8 %collective-permute-start = (f32[32,768]{1,0:T(8,128)S(1)}, f32[32,768]{1,0:T(8,128)S(1)}, u32[]{:S(2)}, u32[]{:S(2)}) collective-permute-start(f32[32,768]{1,0:T(8,128)S(1)} %get-tuple-element.28), channel_id=1, source_target_pairs={{0,1},{1,2},{2,3},{3,0},{4,5},{5,6},{6,7},{7,4},{8,9},{9,10},{10,1... | collective-permute-start | bytes 294920 | tf_op jit(solution)/shard_map/ppermute | solution.py:610
  13.4 2.4 %collective-permute-start.1 = (f32[32,768]{1,0:T(8,128)S(1)}, f32[32,768]{1,0:T(8,128)S(1)}, u32[]{:S(2)}, u32[]{:S(2)}) collective-permute-start(f32[32,768]{1,0:T(8,128)S(1)} %get-tuple-element.29), channel_id=1, source_target_pairs={{0,2},{1,3},{2,0},{3,1},{4,6},{5,7},{6,4},{7,5},{8,10},{9,11},{10,... | collective-permute-start | bytes 294920 | tf_op jit(solution)/shard_map/ppermute | solution.py:610
  15.8 1.4 %collective-permute-start.2 = (f32[32,768]{1,0:T(8,128)S(1)}, f32[32,768]{1,0:T(8,128)S(1)}, u32[]{:S(2)}, u32[]{:S(2)}) collective-permute-start(f32[32,768]{1,0:T(8,128)S(1)} %get-tuple-element.30), channel_id=1, source_target_pairs={{0,3},{1,0},{2,1},{3,2},{4,7},{5,4},{6,5},{7,6},{8,11},{9,8},{10,9... | collective-permute-start | bytes 294920 | tf_op jit(solution)/shard_map/ppermute | solution.py:610
  17.2 0.2 fusion.nodes_ref
  17.4 17.8 %all-to-all-done = f32[32,48,128]{2,1,0:T(8,128)S(1)} async-done(((f32[32,48,128]{2,1,0:T(8,128)}), f32[32,48,128]{2,1,0:T(8,128)S(1)}, u32[]{:S(2)}, u32[]{:S(2)}) %all-to-all-start) | async-done | bytes 786464 | tf_op jit(solution)/shard_map/all_to_all | solution.py:606
  35.2 8.0 %mix.2 = (f32[32,24,128]{2,1,0:T(8,128)}, f32[11,8,128]{2,1,0:T(8,128)S(1)}) custom-call(s32[726]{0:T(1024)S(1)} %fusion.nodes_ref, s32[660]{0:T(1024)S(1)} %copy-done.9, f32[1536,128]{1,0:T(8,128)S(1)} %bitcast.8, bf16[4,128,128]{2,1,0:T(8,128)(2,1)S(1)} %copy-done.8, bf16[256,384]{1,0:T(8,128)(2,1)S(1)} %copy-done.3, bf16[384,128]{1,0:T(8,128)(2,1)S(1)} %copy-done.4), custom_call_target="tpu_custom_call" | custom-call | tf_op jit(solution)/shard_map/mix/pallas_call | solution.py:670
  43.2 0.0 copy-start.6
  43.2 4.4 %all-to-all-start.1 = ((f32[32,24,128]{2,1,0:T(8,128)}), f32[32,24,128]{2,1,0:T(8,128)S(1)}, u32[]{:S(2)}, u32[]{:S(2)}) async-start(f32[32,24,128]{2,1,0:T(8,128)} %get-tuple-element.33), calls=%async_computation.1 | async-start | bytes 786432 | tf_op jit(solution)/shard_map/all_to_all | solution.py:606
  47.7 0.1 dynamic-slice_convert_fusion
  47.8 0.1 dynamic_slice.7
  47.8 0.6 load.1
  48.5 11.0 %all-to-all-done.1.image_ref = f32[32,24,128]{2,1,0:T(8,128)S(1)} async-done(((f32[32,24,128]{2,1,0:T(8,128)}), f32[32,24,128]{2,1,0:T(8,128)S(1)}, u32[]{:S(2)}, u32[]{:S(2)}) %all-to-all-start.1) | async-done | bytes 393248 | tf_op jit(solution)/shard_map/all_to_all | solution.py:606
  59.5 0.1 broadcast_in_dim.26.live_ref
  59.6 4.9 %middle.1 = (f32[32,48,128]{2,1,0:T(8,128)S(1)}, f32[24,3,16,128]{3,2,1,0:T(8,128)S(1)}, f32[25,3,16,128]{3,2,1,0:T(8,128)S(1)}) custom-call(f32[32,24,128]{2,1,0:T(8,128)S(1)} %all-to-all-done.1.image_ref, f32[24,3,16,128]{3,2,1,0:T(8,128)S(1)} %get-tuple-element.38.base_ref, f32[16,128]{1,0:T(8,128)S(1)} %broadcast_in_dim.26.live_ref, ...), custom_call_target="tpu_custom_call" | custom-call | tf_op jit(solution)/shard_map/middle/pallas_call | solution.py:685
  64.5 23.3 %all_to_all.20.msg_ref = f32[32,48,128]{2,1,0:T(8,128)S(1)} all-to-all(f32[32,48,128]{2,1,0:T(8,128)S(1)} %get-tuple-element.40), channel_id=1, replica_groups=mesh['chaos'=8,'slab'=4] {'chaos','slab'}, dimensions={0} | all-to-all | bytes 1572864 | tf_op jit(solution)/shard_map/all_to_all | solution.py:606
  87.7 5.2 %mix.3 = f32[32,24,128]{2,1,0:T(8,128)S(1)} custom-call(s32[726]{0:T(1024)S(1)} %fusion.nodes_ref, s32[660]{0:T(1024)S(1)} %copy-done.9, f32[32,48,128]{2,1,0:T(8,128)S(1)} %all_to_all.20.msg_ref, f32[11,8,128]{2,1,0:T(8,128)S(1)} %get-tuple-element.41.mods_ref, bf16[256,384]{1,0:T(8,128)(2,1)S(1)} %copy-done.3, bf16[384,128]{1,0:T(8,128)(2,1)S(1)} %copy-done.4), custom_call_target="tpu_custom_call" | custom-call | tf_op jit(solution)/shard_map/mix/pallas_call | solution.py:693
  92.9 16.0 %all_to_all.21.image_ref = f32[32,24,128]{2,1,0:T(8,128)S(1)} all-to-all(f32[32,24,128]{2,1,0:T(8,128)S(1)} %mix.3), channel_id=1, replica_groups=mesh['chaos'=8,'slab'=4] {'chaos','slab'}, dimensions={0} | all-to-all | bytes 786432 | tf_op jit(solution)/shard_map/all_to_all | solution.py:606
  108.9 4.2 %end.1 = (f32[56,768]{1,0:T(8,128)S(1)}, f32[56,768]{1,0:T(8,128)S(1)}, f32[56,768]{1,0:T(8,128)S(1)}, f32[56,768]{1,0:T(8,128)S(1)}) custom-call(f32[32,24,128]{2,1,0:T(8,128)S(1)} %all_to_all.21.image_ref, f32[24,3,16,128]{3,2,1,0:T(8,128)S(1)} %get-tuple-element.42.base_ref, f32[16,128]{1,0:T(8,128)S(1)} %broadcast_in_dim.26.live_ref, ...), custom_call_target="tpu_custom_call" | custom-call | tf_op jit(solution)/shard_map/end/pallas_call | solution.py:697
  113.1 2.3 %collective-permute-start.3 = (f32[56,768]{1,0:T(8,128)S(1)}, f32[56,768]{1,0:T(8,128)S(1)}, u32[]{:S(2)}, u32[]{:S(2)}) collective-permute-start(f32[56,768]{1,0:T(8,128)S(1)} %get-tuple-element.45), channel_id=1, source_target_pairs={{0,1},{1,2},{2,3},{3,0},{4,5},{5,6},{6,7},{7,4},{8,9},{9,10},{10,1... | collective-permute-start | bytes 516104 | tf_op jit(solution)/shard_map/ppermute | solution.py:610
  115.4 0.9 collective-permute-start.4
  116.3 1.6 %collective-permute-start.5 = (f32[56,768]{1,0:T(8,128)S(1)}, f32[56,768]{1,0:T(8,128)S(1)}, u32[]{:S(2)}, u32[]{:S(2)}) collective-permute-start(f32[56,768]{1,0:T(8,128)S(1)} %get-tuple-element.47), channel_id=1, source_target_pairs={{0,3},{1,0},{2,1},{3,2},{4,7},{5,4},{6,5},{7,6},{8,11},{9,8},{10,9... | collective-permute-start | bytes 516104 | tf_op jit(solution)/shard_map/ppermute | solution.py:610
  117.9 0.1 fusion.1
  118.0 0.1 copy.18.live_ref
  118.1 4.1 %collective-permute-done.3.refs_1_ = f32[56,768]{1,0:T(8,128)S(1)} collective-permute-done((f32[56,768]{1,0:T(8,128)S(1)}, f32[56,768]{1,0:T(8,128)S(1)}, u32[]{:S(2)}, u32[]{:S(2)}) %collective-permute-start.3) | collective-permute-done | bytes 172064 | tf_op jit(solution)/shard_map/ppermute | solution.py:610
  122.2 7.6 %collective-permute-done.4.refs_2_ = f32[56,768]{1,0:T(8,128)S(1)} collective-permute-done((f32[56,768]{1,0:T(8,128)S(1)}, f32[56,768]{1,0:T(8,128)S(1)}, u32[]{:S(2)}, u32[]{:S(2)}) %collective-permute-start.4) | collective-permute-done | bytes 172064 | tf_op jit(solution)/shard_map/ppermute | solution.py:610
  129.8 1.1 finish.1
  (29 shorter events, 0.1 us)
Async XLA Ops:
  4.0 7.4 %copy-start.10 = (f32[768]{0:T(1024)S(1)}, f32[768]{0:T(1024)}, u32[]{:S(2)}) copy-start(f32[768]{0:T(1024)} %param.17) | copy-start | bytes 9220
  4.0 7.4 %copy-start.5 = (f32[36,3,768]{2,0,1:T(8,128)S(1)}, f32[36,3,768]{2,0,1:T(8,128)}, u32[]{:S(2)}) copy-start(f32[36,3,768]{2,0,1:T(8,128)} %param.16) | copy-start | bytes 995332
  4.0 31.2 %copy-start.8 = (bf16[4,128,128]{2,1,0:T(8,128)(2,1)S(1)}, bf16[4,128,128]{2,1,0:T(8,128)(2,1)}, u32[]{:S(2)}) copy-start(bf16[4,128,128]{2,1,0:T(8,128)(2,1)} %constant.44.clone.mtab_ref) | copy-start | bytes 393220
  4.1 31.1 %all-to-all-start = ((f32[32,48,128]{2,1,0:T(8,128)}), f32[32,48,128]{2,1,0:T(8,128)S(1)}, u32[]{:S(2)}, u32[]{:S(2)}) async-start(f32[32,48,128]{2,1,0:T(8,128)} %start.1), calls=%async_computation | async-start | bytes 1572864 | tf_op jit(solution)/shard_map/all_to_all | solution.py:606
  11.4 23.8 %copy-start.3 = (bf16[256,384]{1,0:T(8,128)(2,1)S(1)}, bf16[256,384]{1,0:T(8,128)(2,1)}, u32[]{:S(2)}) copy-start(bf16[256,384]{1,0:T(8,128)(2,1)} %constant.47.clone.grad_ref) | copy-start | bytes 589828
  11.4 5.8 %copy-start.12 = (s32[726]{0:T(1024)S(1)}, s32[726]{0:T(1024)}, u32[]{:S(2)}) copy-start(s32[726]{0:T(1024)} %constant.54) | copy-start | bytes 8716
  11.4 23.8 %copy-start.4 = (bf16[384,128]{1,0:T(8,128)(2,1)S(1)}, bf16[384,128]{1,0:T(8,128)(2,1)}, u32[]{:S(2)}) copy-start(bf16[384,128]{1,0:T(8,128)(2,1)} %constant.48.clone.div_ref) | copy-start | bytes 294916
  11.5 5.7 %copy-start.11 = (s32[288]{0:T(512)S(1)}, s32[288]{0:T(512)}, u32[]{:S(2)}) copy-start(s32[288]{0:T(512)} %param.19) | copy-start | bytes 3460
  11.6 31.6 %collective-permute-start = (f32[32,768]{1,0:T(8,128)S(1)}, f32[32,768]{1,0:T(8,128)S(1)}, u32[]{:S(2)}, u32[]{:S(2)}) collective-permute-start(f32[32,768]{1,0:T(8,128)S(1)} %get-tuple-element.28), channel_id=1, source_target_pairs={{0,1},{1,2},{2,3},{3,0},{4,5},{5,6},{6,7},{7,4},{8,9},{9,10},{10,1... | collective-permute-start | bytes 294920 | tf_op jit(solution)/shard_map/ppermute | solution.py:610
  13.4 29.8 %collective-permute-start.1 = (f32[32,768]{1,0:T(8,128)S(1)}, f32[32,768]{1,0:T(8,128)S(1)}, u32[]{:S(2)}, u32[]{:S(2)}) collective-permute-start(f32[32,768]{1,0:T(8,128)S(1)} %get-tuple-element.29), channel_id=1, source_target_pairs={{0,2},{1,3},{2,0},{3,1},{4,6},{5,7},{6,4},{7,5},{8,10},{9,11},{10,... | collective-permute-start | bytes 294920 | tf_op jit(solution)/shard_map/ppermute | solution.py:610
  15.8 19.4 %copy-start.9 = (s32[660]{0:T(1024)S(1)}, s32[660]{0:T(1024)}, u32[]{:S(2)}) copy-start(s32[660]{0:T(1024)} %constant.49.clone.level_ref) | copy-start | bytes 7924
  15.8 27.4 %collective-permute-start.2 = (f32[32,768]{1,0:T(8,128)S(1)}, f32[32,768]{1,0:T(8,128)S(1)}, u32[]{:S(2)}, u32[]{:S(2)}) collective-permute-start(f32[32,768]{1,0:T(8,128)S(1)} %get-tuple-element.30), channel_id=1, source_target_pairs={{0,3},{1,0},{2,1},{3,2},{4,7},{5,4},{6,5},{7,6},{8,11},{9,8},{10,9... | collective-permute-start | bytes 294920 | tf_op jit(solution)/shard_map/ppermute | solution.py:610
  43.2 16.3 %copy-start = (bf16[512,512]{1,0:T(8,128)(2,1)S(1)}, bf16[512,512]{1,0:T(8,128)(2,1)}, u32[]{:S(2)}) copy-start(bf16[512,512]{1,0:T(8,128)(2,1)} %constant.43.clone.unpack_ref) | copy-start | bytes 1572868
  43.2 16.3 %copy-start.6 = (bf16[128,256]{1,0:T(8,128)(2,1)S(1)}, bf16[128,256]{1,0:T(8,128)(2,1)}, u32[]{:S(2)}) copy-start(bf16[128,256]{1,0:T(8,128)(2,1)} %constant.45.clone.slope_ref) | copy-start | bytes 196612
  43.2 16.3 %copy-start.7 = (bf16[256,128]{1,0:T(8,128)(2,1)S(1)}, bf16[256,128]{1,0:T(8,128)(2,1)}, u32[]{:S(2)}) copy-start(bf16[256,128]{1,0:T(8,128)(2,1)} %constant.46.clone.back_ref) | copy-start | bytes 196612
  43.2 16.2 %all-to-all-start.1 = ((f32[32,24,128]{2,1,0:T(8,128)}), f32[32,24,128]{2,1,0:T(8,128)S(1)}, u32[]{:S(2)}, u32[]{:S(2)}) async-start(f32[32,24,128]{2,1,0:T(8,128)} %get-tuple-element.33), calls=%async_computation.1 | async-start | bytes 786432 | tf_op jit(solution)/shard_map/all_to_all | solution.py:606
  47.6 11.9 %copy-start.1 = (bf16[384,512]{1,0:T(8,128)(2,1)S(1)}, bf16[384,512]{1,0:T(8,128)(2,1)}, u32[]{:S(2)}) copy-start(bf16[384,512]{1,0:T(8,128)(2,1)} %constant.42.clone.pack_hbm.pack_ref) | copy-start | bytes 1179652
  108.9 20.9 %copy-start.2 = (f32[36,3,768]{2,0,1:T(8,128)S(1)}, f32[36,3,768]{2,0,1:T(8,128)}, u32[]{:S(2)}) copy-start(f32[36,3,768]{2,0,1:T(8,128)} %param.15) | copy-start | bytes 995332
  113.1 9.1 %collective-permute-start.3 = (f32[56,768]{1,0:T(8,128)S(1)}, f32[56,768]{1,0:T(8,128)S(1)}, u32[]{:S(2)}, u32[]{:S(2)}) collective-permute-start(f32[56,768]{1,0:T(8,128)S(1)} %get-tuple-element.45), channel_id=1, source_target_pairs={{0,1},{1,2},{2,3},{3,0},{4,5},{5,6},{6,7},{7,4},{8,9},{9,10},{10,1... | collective-permute-start | bytes 516104 | tf_op jit(solution)/shard_map/ppermute | solution.py:610
  115.4 14.3 %collective-permute-start.4 = (f32[56,768]{1,0:T(8,128)S(1)}, f32[56,768]{1,0:T(8,128)S(1)}, u32[]{:S(2)}, u32[]{:S(2)}) collective-permute-start(f32[56,768]{1,0:T(8,128)S(1)} %get-tuple-element.46), channel_id=1, source_target_pairs={{0,2},{1,3},{2,0},{3,1},{4,6},{5,7},{6,4},{7,5},{8,10},{9,11},{10,... | collective-permute-start | bytes 516104 | tf_op jit(solution)/shard_map/ppermute | solution.py:610
  116.3 13.5 %collective-permute-start.5 = (f32[56,768]{1,0:T(8,128)S(1)}, f32[56,768]{1,0:T(8,128)S(1)}, u32[]{:S(2)}, u32[]{:S(2)}) collective-permute-start(f32[56,768]{1,0:T(8,128)S(1)} %get-tuple-element.47), channel_id=1, source_target_pairs={{0,3},{1,0},{2,1},{3,2},{4,7},{5,4},{6,5},{7,6},{8,11},{9,8},{10,9... | collective-permute-start | bytes 516104 | tf_op jit(solution)/shard_map/ppermute | solution.py:610

commit v8 on v7

--- a/solution.py
+++ b/solution.py
@@ -189,12 +189,12 @@
     return total
 
 
-def pick_into(out_ref, values_ref, table_ref):
+def pick_into(out_ref, values_ref, table_ref, parts=3):
     width = table_ref.shape[1]
     chunk = width if width <= 1024 else 512
     for first in range(0, width, chunk):
         out_ref[:, first : first + chunk] = picked(
-            values_ref[:, : table_ref.shape[0]], table_ref[:, first : first + chunk]
+            values_ref[:, : table_ref.shape[0]], table_ref[:, first : first + chunk], parts
         )
 
 
@@ -440,7 +440,7 @@
             flux[base, d] = total[d]
         return carry
 
-    lax.fori_loop(0, low_count, edges, 0, unroll=2)
+    lax.fori_loop(0, low_count, edges, 0, unroll=6)
 
     def divergences(chunk, carry):
         here = pl.ds(chunk * 4 * sp, 4 * sp)
@@ -462,7 +462,7 @@
     lax.fori_loop(0, plan.n // 4, divergences, 0, unroll=8)
 
 
-def unpack_image(plan, image_ref, unpack_ref, lhs, rows):
+def unpack_image(plan, image_ref, unpack_ref, lhs, rows, parts):
     for xb in range(plan.nxb):
         for k in range(plan.tx):
             x = xb * plan.tx + k
@@ -470,7 +470,7 @@
                 lhs[x * plan.hs : x * plan.hs + plan.kept, yb * plan.lanes_out : (yb + 1) * plan.lanes_out] = image_ref[
                     xb * plan.nyb + yb, strided(k, plan.kept, plan.tx), :
                 ]
-    pick_into(rows, lhs, unpack_ref)
+    pick_into(rows, lhs, unpack_ref, parts)
 
 
 def add_image(plan, base_ref, live_ref, rows, residual_ref):
@@ -541,13 +541,13 @@
 
 
 def middle_kernel(plan, image_ref, base_ref, live_ref, mean_ref, slope_ref, back_ref, unpack_ref, pack_ref, msg_ref, residual_ref, update_ref, wide, narrow, step):
-    unpack_image(plan, image_ref, unpack_ref, wide, narrow)
+    unpack_image(plan, image_ref, unpack_ref, wide, narrow, 3)
     add_image(plan, base_ref, live_ref, narrow, residual_ref)
     smooth(plan, mean_ref, slope_ref, back_ref, residual_ref, update_ref, step)
     for x in range(NX):
         for c in range(3):
             narrow[x * plan.hs : (x + 1) * plan.hs, c * plan.ls : (c + 1) * plan.ls] = update_ref[x, c]
-    pick_into(wide, narrow, pack_ref)
+    pick_into(wide, narrow, pack_ref, 2)
     store_message(plan, wide, msg_ref)
 
 
@@ -560,7 +560,7 @@
 
 def end_kernel(plan, image_ref, base_ref, live_ref, mean_ref, slope_ref, back_ref, unpack_ref, before_ref, *refs):
     out_refs, (wide, narrow, residual, update, step, planes) = refs[: plan.slab], refs[plan.slab :]
-    unpack_image(plan, image_ref, unpack_ref, wide, narrow)
+    unpack_image(plan, image_ref, unpack_ref, wide, narrow, 2)
     add_image(plan, base_ref, live_ref, narrow, residual)
     smooth(plan, mean_ref, slope_ref, back_ref, residual, update, step)
     for a in range(PLANE // 128):

time: 132 us -> 131 us (level)
  no operation moved by 1% of the time
where the time goes in v8:
time: 131 us; the launch traced here: 130 us
  waiting for transfers between devices  40.6 us (31%)
  blocking collectives  39.3 us (30%)
  Pallas kernels  26.8 us (20%)
  starting transfers between devices  22.1 us (17%)
    all_to_all x2, blocking collectives, everyone(): return lax.all_to_all(values, ('chaos', 'slab'), 0, 0, tiled=True)  39.3 us
    all_to_all x2, waiting for transfers between devices, everyone(): return lax.all_to_all(values, ('chaos', 'slab'), 0, 0, tiled=True)  28.8 us
    ppermute x6, waiting for transfers between devices, column(): lax.ppermute(pieces[step], 'slab', [(z, (z + step) % slab) for z in range...  11.7 us
    all_to_all x2, starting transfers between devices, everyone(): return lax.all_to_all(values, ('chaos', 'slab'), 0, 0, tiled=True)  11.7 us
    ppermute x6, starting transfers between devices, column(): lax.ppermute(pieces[step], 'slab', [(z, (z + step) % slab) for z in range...  10.4 us
    pallas_call x1, Pallas kernels, per_device(): call(functools.partial(first_mix_kernel, plan, len(low), 3), 'mix', [smem...  7.88 us
    pallas_call x1, Pallas kernels, per_device(): call(functools.partial(mix_kernel, plan, len(low), 2), 'mix', [smem, smem...  5.01 us
    pallas_call x1, Pallas kernels, per_device(): call(functools.partial(middle_kernel, plan), 'middle', [vmem] * 8, (messa...  4.65 us
  transfers between devices with their start and end apart: 8, of which 4 were waited for; matrix products, arithmetic and copies ran while one was open for 0% of the time, Pallas kernels for 7%

profile of v8, /device:TPU:0, one launch (start us, length us, event | category | flops | bytes accessed | tf_op | source)
XLA Modules:
  0.0 130.2 jit_solution(15896875866786255072)
XLA Ops:
  0.6 3.4 %start.1 = f32[32,48,128]{2,1,0:T(8,128)} custom-call(f32[3,36,768]{2,1,0:T(8,128)} %bitcast.9, f32[6,128]{1,0:T(8,128)} %bitcast.12, f32[10,768]{1,0:T(8,128)} %modes_hbm.1, bf16[384,512]{1,0:T(8,128)(2,1)} %constant.42.clone.pack_hbm.pack_ref), custom_call_target="tpu_custom_call" | custom-call | tf_op jit(solution)/shard_map/start/pallas_call | solution.py:639
  4.0 0.0 copy-start.8
  4.1 7.3 %all-to-all-start = ((f32[32,48,128]{2,1,0:T(8,128)}), f32[32,48,128]{2,1,0:T(8,128)S(1)}, u32[]{:S(2)}, u32[]{:S(2)}) async-start(f32[32,48,128]{2,1,0:T(8,128)} %start.1), calls=%async_computation | async-start | bytes 1572864 | tf_op jit(solution)/shard_map/all_to_all | solution.py:606
  11.4 0.0 copy-start.3
  11.4 0.0 copy-start.12
  11.4 0.0 copy-start.4
  11.4 0.1 split.1
  11.6 1.8 %collective-permute-start = (f32[32,768]{1,0:T(8,128)S(1)}, f32[32,768]{1,0:T(8,128)S(1)}, u32[]{:S(2)}, u32[]{:S(2)}) collective-permute-start(f32[32,768]{1,0:T(8,128)S(1)} %get-tuple-element.28), channel_id=1, source_target_pairs={{0,1},{1,2},{2,3},{3,0},{4,5},{5,6},{6,7},{7,4},{8,9},{9,10},{10,1... | collective-permute-start | bytes 294920 | tf_op jit(solution)/shard_map/ppermute | solution.py:610
  13.4 2.4 %collective-permute-start.1 = (f32[32,768]{1,0:T(8,128)S(1)}, f32[32,768]{1,0:T(8,128)S(1)}, u32[]{:S(2)}, u32[]{:S(2)}) collective-permute-start(f32[32,768]{1,0:T(8,128)S(1)} %get-tuple-element.29), channel_id=1, source_target_pairs={{0,2},{1,3},{2,0},{3,1},{4,6},{5,7},{6,4},{7,5},{8,10},{9,11},{10,... | collective-permute-start | bytes 294920 | tf_op jit(solution)/shard_map/ppermute | solution.py:610
  15.8 1.4 %collective-permute-start.2 = (f32[32,768]{1,0:T(8,128)S(1)}, f32[32,768]{1,0:T(8,128)S(1)}, u32[]{:S(2)}, u32[]{:S(2)}) collective-permute-start(f32[32,768]{1,0:T(8,128)S(1)} %get-tuple-element.30), channel_id=1, source_target_pairs={{0,3},{1,0},{2,1},{3,2},{4,7},{5,4},{6,5},{7,6},{8,11},{9,8},{10,9... | collective-permute-start | bytes 294920 | tf_op jit(solution)/shard_map/ppermute | solution.py:610
  17.2 0.2 fusion.nodes_ref
  17.4 17.8 %all-to-all-done = f32[32,48,128]{2,1,0:T(8,128)S(1)} async-done(((f32[32,48,128]{2,1,0:T(8,128)}), f32[32,48,128]{2,1,0:T(8,128)S(1)}, u32[]{:S(2)}, u32[]{:S(2)}) %all-to-all-start) | async-done | bytes 786464 | tf_op jit(solution)/shard_map/all_to_all | solution.py:606
  35.2 7.9 %mix.2 = (f32[32,24,128]{2,1,0:T(8,128)}, f32[11,8,128]{2,1,0:T(8,128)S(1)}) custom-call(s32[726]{0:T(1024)S(1)} %fusion.nodes_ref, s32[660]{0:T(1024)S(1)} %copy-done.9, f32[1536,128]{1,0:T(8,128)S(1)} %bitcast.8, bf16[4,128,128]{2,1,0:T(8,128)(2,1)S(1)} %copy-done.8, bf16[256,384]{1,0:T(8,128)(2,1)S(1)} %copy-done.3, bf16[384,128]{1,0:T(8,128)(2,1)S(1)} %copy-done.4), custom_call_target="tpu_custom_call" | custom-call | tf_op jit(solution)/shard_map/mix/pallas_call | solution.py:670
  43.2 4.4 %all-to-all-start.1 = ((f32[32,24,128]{2,1,0:T(8,128)}), f32[32,24,128]{2,1,0:T(8,128)S(1)}, u32[]{:S(2)}, u32[]{:S(2)}) async-start(f32[32,24,128]{2,1,0:T(8,128)} %get-tuple-element.33), calls=%async_computation.1 | async-start | bytes 786432 | tf_op jit(solution)/shard_map/all_to_all | solution.py:606
  47.6 0.1 dynamic-slice_convert_fusion
  47.7 0.1 dynamic_slice.7
  47.8 0.6 load.1
  48.4 11.0 %all-to-all-done.1.image_ref = f32[32,24,128]{2,1,0:T(8,128)S(1)} async-done(((f32[32,24,128]{2,1,0:T(8,128)}), f32[32,24,128]{2,1,0:T(8,128)S(1)}, u32[]{:S(2)}, u32[]{:S(2)}) %all-to-all-start.1) | async-done | bytes 393248 | tf_op jit(solution)/shard_map/all_to_all | solution.py:606
  59.4 0.1 broadcast_in_dim.26.live_ref
  59.5 4.6 %middle.1 = (f32[32,48,128]{2,1,0:T(8,128)S(1)}, f32[24,3,16,128]{3,2,1,0:T(8,128)S(1)}, f32[25,3,16,128]{3,2,1,0:T(8,128)S(1)}) custom-call(f32[32,24,128]{2,1,0:T(8,128)S(1)} %all-to-all-done.1.image_ref, f32[24,3,16,128]{3,2,1,0:T(8,128)S(1)} %get-tuple-element.38.base_ref, f32[16,128]{1,0:T(8,128)S(1)} %broadcast_in_dim.26.live_ref, ...), custom_call_target="tpu_custom_call" | custom-call | tf_op jit(solution)/shard_map/middle/pallas_call | solution.py:685
  64.1 23.3 %all_to_all.20.msg_ref = f32[32,48,128]{2,1,0:T(8,128)S(1)} all-to-all(f32[32,48,128]{2,1,0:T(8,128)S(1)} %get-tuple-element.40), channel_id=1, replica_groups=mesh['chaos'=8,'slab'=4] {'chaos','slab'}, dimensions={0} | all-to-all | bytes 1572864 | tf_op jit(solution)/shard_map/all_to_all | solution.py:606
  87.4 5.0 %mix.3 = f32[32,24,128]{2,1,0:T(8,128)S(1)} custom-call(s32[726]{0:T(1024)S(1)} %fusion.nodes_ref, s32[660]{0:T(1024)S(1)} %copy-done.9, f32[32,48,128]{2,1,0:T(8,128)S(1)} %all_to_all.20.msg_ref, f32[11,8,128]{2,1,0:T(8,128)S(1)} %get-tuple-element.41.mods_ref, bf16[256,384]{1,0:T(8,128)(2,1)S(1)} %copy-done.3, bf16[384,128]{1,0:T(8,128)(2,1)S(1)} %copy-done.4), custom_call_target="tpu_custom_call" | custom-call | tf_op jit(solution)/shard_map/mix/pallas_call | solution.py:693
  92.4 16.0 %all_to_all.21.image_ref = f32[32,24,128]{2,1,0:T(8,128)S(1)} all-to-all(f32[32,24,128]{2,1,0:T(8,128)S(1)} %mix.3), channel_id=1, replica_groups=mesh['chaos'=8,'slab'=4] {'chaos','slab'}, dimensions={0} | all-to-all | bytes 786432 | tf_op jit(solution)/shard_map/all_to_all | solution.py:606
  108.4 4.0 %end.1 = (f32[56,768]{1,0:T(8,128)S(1)}, f32[56,768]{1,0:T(8,128)S(1)}, f32[56,768]{1,0:T(8,128)S(1)}, f32[56,768]{1,0:T(8,128)S(1)}) custom-call(f32[32,24,128]{2,1,0:T(8,128)S(1)} %all_to_all.21.image_ref, f32[24,3,16,128]{3,2,1,0:T(8,128)S(1)} %get-tuple-element.42.base_ref, f32[16,128]{1,0:T(8,128)S(1)} %broadcast_in_dim.26.live_ref, ...), custom_call_target="tpu_custom_call" | custom-call | tf_op jit(solution)/shard_map/end/pallas_call | solution.py:697
  112.4 2.3 %collective-permute-start.3 = (f32[56,768]{1,0:T(8,128)S(1)}, f32[56,768]{1,0:T(8,128)S(1)}, u32[]{:S(2)}, u32[]{:S(2)}) collective-permute-start(f32[56,768]{1,0:T(8,128)S(1)} %get-tuple-element.45), channel_id=1, source_target_pairs={{0,1},{1,2},{2,3},{3,0},{4,5},{5,6},{6,7},{7,4},{8,9},{9,10},{10,1... | collective-permute-start | bytes 516104 | tf_op jit(solution)/shard_map/ppermute | solution.py:610
  114.8 0.9 collective-permute-start.4
  115.6 1.6 %collective-permute-start.5 = (f32[56,768]{1,0:T(8,128)S(1)}, f32[56,768]{1,0:T(8,128)S(1)}, u32[]{:S(2)}, u32[]{:S(2)}) collective-permute-start(f32[56,768]{1,0:T(8,128)S(1)} %get-tuple-element.47), channel_id=1, source_target_pairs={{0,3},{1,0},{2,1},{3,2},{4,7},{5,4},{6,5},{7,6},{8,11},{9,8},{10,9... | collective-permute-start | bytes 516104 | tf_op jit(solution)/shard_map/ppermute | solution.py:610
  117.2 0.1 fusion.1
  117.3 0.1 copy.18.live_ref
  117.4 4.1 %collective-permute-done.3.refs_1_ = f32[56,768]{1,0:T(8,128)S(1)} collective-permute-done((f32[56,768]{1,0:T(8,128)S(1)}, f32[56,768]{1,0:T(8,128)S(1)}, u32[]{:S(2)}, u32[]{:S(2)}) %collective-permute-start.3) | collective-permute-done | bytes 172064 | tf_op jit(solution)/shard_map/ppermute | solution.py:610
  121.5 7.6 %collective-permute-done.4.refs_2_ = f32[56,768]{1,0:T(8,128)S(1)} collective-permute-done((f32[56,768]{1,0:T(8,128)S(1)}, f32[56,768]{1,0:T(8,128)S(1)}, u32[]{:S(2)}, u32[]{:S(2)}) %collective-permute-start.4) | collective-permute-done | bytes 172064 | tf_op jit(solution)/shard_map/ppermute | solution.py:610
  129.1 1.1 finish.1
  (29 shorter events, 0.1 us)
Async XLA Ops:
  4.0 7.4 %copy-start.10 = (f32[768]{0:T(1024)S(1)}, f32[768]{0:T(1024)}, u32[]{:S(2)}) copy-start(f32[768]{0:T(1024)} %param.17) | copy-start | bytes 9220
  4.0 7.4 %copy-start.5 = (f32[36,3,768]{2,0,1:T(8,128)S(1)}, f32[36,3,768]{2,0,1:T(8,128)}, u32[]{:S(2)}) copy-start(f32[36,3,768]{2,0,1:T(8,128)} %param.16) | copy-start | bytes 995332
  4.0 31.2 %copy-start.8 = (bf16[4,128,128]{2,1,0:T(8,128)(2,1)S(1)}, bf16[4,128,128]{2,1,0:T(8,128)(2,1)}, u32[]{:S(2)}) copy-start(bf16[4,128,128]{2,1,0:T(8,128)(2,1)} %constant.44.clone.mtab_ref) | copy-start | bytes 393220
  4.1 31.1 %all-to-all-start = ((f32[32,48,128]{2,1,0:T(8,128)}), f32[32,48,128]{2,1,0:T(8,128)S(1)}, u32[]{:S(2)}, u32[]{:S(2)}) async-start(f32[32,48,128]{2,1,0:T(8,128)} %start.1), calls=%async_computation | async-start | bytes 1572864 | tf_op jit(solution)/shard_map/all_to_all | solution.py:606
  11.4 23.8 %copy-start.3 = (bf16[256,384]{1,0:T(8,128)(2,1)S(1)}, bf16[256,384]{1,0:T(8,128)(2,1)}, u32[]{:S(2)}) copy-start(bf16[256,384]{1,0:T(8,128)(2,1)} %constant.47.clone.grad_ref) | copy-start | bytes 589828
  11.4 5.8 %copy-start.12 = (s32[726]{0:T(1024)S(1)}, s32[726]{0:T(1024)}, u32[]{:S(2)}) copy-start(s32[726]{0:T(1024)} %constant.54) | copy-start | bytes 8716
  11.4 23.8 %copy-start.4 = (bf16[384,128]{1,0:T(8,128)(2,1)S(1)}, bf16[384,128]{1,0:T(8,128)(2,1)}, u32[]{:S(2)}) copy-start(bf16[384,128]{1,0:T(8,128)(2,1)} %constant.48.clone.div_ref) | copy-start | bytes 294916
  11.5 5.7 %copy-start.11 = (s32[288]{0:T(512)S(1)}, s32[288]{0:T(512)}, u32[]{:S(2)}) copy-start(s32[288]{0:T(512)} %param.19) | copy-start | bytes 3460
  11.6 31.6 %collective-permute-start = (f32[32,768]{1,0:T(8,128)S(1)}, f32[32,768]{1,0:T(8,128)S(1)}, u32[]{:S(2)}, u32[]{:S(2)}) collective-permute-start(f32[32,768]{1,0:T(8,128)S(1)} %get-tuple-element.28), channel_id=1, source_target_pairs={{0,1},{1,2},{2,3},{3,0},{4,5},{5,6},{6,7},{7,4},{8,9},{9,10},{10,1... | collective-permute-start | bytes 294920 | tf_op jit(solution)/shard_map/ppermute | solution.py:610
  13.4 29.7 %collective-permute-start.1 = (f32[32,768]{1,0:T(8,128)S(1)}, f32[32,768]{1,0:T(8,128)S(1)}, u32[]{:S(2)}, u32[]{:S(2)}) collective-permute-start(f32[32,768]{1,0:T(8,128)S(1)} %get-tuple-element.29), channel_id=1, source_target_pairs={{0,2},{1,3},{2,0},{3,1},{4,6},{5,7},{6,4},{7,5},{8,10},{9,11},{10,... | collective-permute-start | bytes 294920 | tf_op jit(solution)/shard_map/ppermute | solution.py:610
  15.8 19.4 %copy-start.9 = (s32[660]{0:T(1024)S(1)}, s32[660]{0:T(1024)}, u32[]{:S(2)}) copy-start(s32[660]{0:T(1024)} %constant.49.clone.level_ref) | copy-start | bytes 7924
  15.8 27.3 %collective-permute-start.2 = (f32[32,768]{1,0:T(8,128)S(1)}, f32[32,768]{1,0:T(8,128)S(1)}, u32[]{:S(2)}, u32[]{:S(2)}) collective-permute-start(f32[32,768]{1,0:T(8,128)S(1)} %get-tuple-element.30), channel_id=1, source_target_pairs={{0,3},{1,0},{2,1},{3,2},{4,7},{5,4},{6,5},{7,6},{8,11},{9,8},{10,9... | collective-permute-start | bytes 294920 | tf_op jit(solution)/shard_map/ppermute | solution.py:610
  43.1 16.3 %copy-start = (bf16[512,512]{1,0:T(8,128)(2,1)S(1)}, bf16[512,512]{1,0:T(8,128)(2,1)}, u32[]{:S(2)}) copy-start(bf16[512,512]{1,0:T(8,128)(2,1)} %constant.43.clone.unpack_ref) | copy-start | bytes 1572868
  43.1 16.3 %copy-start.6 = (bf16[128,256]{1,0:T(8,128)(2,1)S(1)}, bf16[128,256]{1,0:T(8,128)(2,1)}, u32[]{:S(2)}) copy-start(bf16[128,256]{1,0:T(8,128)(2,1)} %constant.45.clone.slope_ref) | copy-start | bytes 196612
  43.1 16.3 %copy-start.7 = (bf16[256,128]{1,0:T(8,128)(2,1)S(1)}, bf16[256,128]{1,0:T(8,128)(2,1)}, u32[]{:S(2)}) copy-start(bf16[256,128]{1,0:T(8,128)(2,1)} %constant.46.clone.back_ref) | copy-start | bytes 196612
  43.2 16.2 %all-to-all-start.1 = ((f32[32,24,128]{2,1,0:T(8,128)}), f32[32,24,128]{2,1,0:T(8,128)S(1)}, u32[]{:S(2)}, u32[]{:S(2)}) async-start(f32[32,24,128]{2,1,0:T(8,128)} %get-tuple-element.33), calls=%async_computation.1 | async-start | bytes 786432 | tf_op jit(solution)/shard_map/all_to_all | solution.py:606
  47.6 11.9 %copy-start.1 = (bf16[384,512]{1,0:T(8,128)(2,1)S(1)}, bf16[384,512]{1,0:T(8,128)(2,1)}, u32[]{:S(2)}) copy-start(bf16[384,512]{1,0:T(8,128)(2,1)} %constant.42.clone.pack_hbm.pack_ref) | copy-start | bytes 1179652
  108.4 20.7 %copy-start.2 = (f32[36,3,768]{2,0,1:T(8,128)S(1)}, f32[36,3,768]{2,0,1:T(8,128)}, u32[]{:S(2)}) copy-start(f32[36,3,768]{2,0,1:T(8,128)} %param.15) | copy-start | bytes 995332
  112.4 9.1 %collective-permute-start.3 = (f32[56,768]{1,0:T(8,128)S(1)}, f32[56,768]{1,0:T(8,128)S(1)}, u32[]{:S(2)}, u32[]{:S(2)}) collective-permute-start(f32[56,768]{1,0:T(8,128)S(1)} %get-tuple-element.45), channel_id=1, source_target_pairs={{0,1},{1,2},{2,3},{3,0},{4,5},{5,6},{6,7},{7,4},{8,9},{9,10},{10,1... | collective-permute-start | bytes 516104 | tf_op jit(solution)/shard_map/ppermute | solution.py:610
  114.8 14.3 %collective-permute-start.4 = (f32[56,768]{1,0:T(8,128)S(1)}, f32[56,768]{1,0:T(8,128)S(1)}, u32[]{:S(2)}, u32[]{:S(2)}) collective-permute-start(f32[56,768]{1,0:T(8,128)S(1)} %get-tuple-element.46), channel_id=1, source_target_pairs={{0,2},{1,3},{2,0},{3,1},{4,6},{5,7},{6,4},{7,5},{8,10},{9,11},{10,... | collective-permute-start | bytes 516104 | tf_op jit(solution)/shard_map/ppermute | solution.py:610
  115.6 13.5 %collective-permute-start.5 = (f32[56,768]{1,0:T(8,128)S(1)}, f32[56,768]{1,0:T(8,128)S(1)}, u32[]{:S(2)}, u32[]{:S(2)}) collective-permute-start(f32[56,768]{1,0:T(8,128)S(1)} %get-tuple-element.47), channel_id=1, source_target_pairs={{0,3},{1,0},{2,1},{3,2},{4,7},{5,4},{6,5},{7,6},{8,11},{9,8},{10,9... | collective-permute-start | bytes 516104 | tf_op jit(solution)/shard_map/ppermute | solution.py:610

commit v9 on v7

--- a/solution.py
+++ b/solution.py
@@ -440,7 +440,7 @@
             flux[base, d] = total[d]
         return carry
 
-    lax.fori_loop(0, low_count, edges, 0, unroll=2)
+    lax.fori_loop(0, low_count, edges, 0, unroll=6)
 
     def divergences(chunk, carry):
         here = pl.ds(chunk * 4 * sp, 4 * sp)
@@ -665,6 +665,7 @@
     load_flat = call(
         functools.partial(split_kernel, plan), "split", [vmem, vmem], (flat,) * slab, [pltpu.VMEM((slab, plan.rows_flat, PLANE), F32)]
     )(by_component(load), mean_row)
+    load_flat, arrived = lax.optimization_barrier((load_flat, arrived))
     load_flat = column(load_flat)
     arrived, nodes = lax.optimization_barrier((arrived, nodes))
     first_image, mods = call(

time: 132 us -> 131 us (level)
  starting transfers between devices: 22.1 us -> 20.2 us
  waiting for transfers between devices: 40.5 us -> 42.2 us
    all_to_all x2, starting transfers between devices: 11.7 us -> 10 us  [everyone(): return lax.all_to_all(values, ('chaos', 'slab'), 0, 0, tiled=True)]
    all_to_all x2, waiting for transfers between devices: 28.8 us -> 30.4 us  [everyone(): return lax.all_to_all(values, ('chaos', 'slab'), 0, 0, tiled=True)]
where the time goes in v9:
time: 131 us; the launch traced here: 130 us
  waiting for transfers between devices  42.2 us (32%)
  blocking collectives  39.2 us (30%)
  Pallas kernels  27.1 us (21%)
  starting transfers between devices  20.2 us (15%)
    all_to_all x2, blocking collectives, everyone(): return lax.all_to_all(values, ('chaos', 'slab'), 0, 0, tiled=True)  39.2 us
    all_to_all x2, waiting for transfers between devices, everyone(): return lax.all_to_all(values, ('chaos', 'slab'), 0, 0, tiled=True)  30.4 us
    ppermute x6, waiting for transfers between devices, column(): lax.ppermute(pieces[step], 'slab', [(z, (z + step) % slab) for z in range...  11.7 us
    ppermute x6, starting transfers between devices, column(): lax.ppermute(pieces[step], 'slab', [(z, (z + step) % slab) for z in range...  10.1 us
    all_to_all x2, starting transfers between devices, everyone(): return lax.all_to_all(values, ('chaos', 'slab'), 0, 0, tiled=True)  10 us
    pallas_call x1, Pallas kernels, per_device(): call(functools.partial(first_mix_kernel, plan, len(low), 3), 'mix', [smem...  7.89 us
    pallas_call x1, Pallas kernels, per_device(): call(functools.partial(mix_kernel, plan, len(low), 2), 'mix', [smem, smem...  5.01 us
    pallas_call x1, Pallas kernels, per_device(): call(functools.partial(middle_kernel, plan), 'middle', [vmem] * 8, (messa...  4.85 us
  transfers between devices with their start and end apart: 8, of which 4 were waited for; matrix products, arithmetic and copies ran while one was open for 0% of the time, Pallas kernels for 7%

profile of v9, /device:TPU:0, one launch (start us, length us, event | category | flops | bytes accessed | tf_op | source)
XLA Modules:
  0.0 130.3 jit_solution(10078138397462314313)
XLA Ops:
  0.6 3.4 %start.1 = f32[32,48,128]{2,1,0:T(8,128)} custom-call(f32[3,36,768]{2,1,0:T(8,128)} %bitcast.9, f32[6,128]{1,0:T(8,128)} %bitcast.12, f32[10,768]{1,0:T(8,128)} %modes_hbm.1, bf16[384,512]{1,0:T(8,128)(2,1)} %constant.42.clone.pack_hbm.pack_ref), custom_call_target="tpu_custom_call" | custom-call | tf_op jit(solution)/shard_map/start/pallas_call | solution.py:639
  4.0 0.0 copy-start.8
  4.1 7.3 %all-to-all-start = ((f32[32,48,128]{2,1,0:T(8,128)}), f32[32,48,128]{2,1,0:T(8,128)S(1)}, u32[]{:S(2)}, u32[]{:S(2)}) async-start(f32[32,48,128]{2,1,0:T(8,128)} %start.1), calls=%async_computation | async-start | bytes 1572864 | tf_op jit(solution)/shard_map/all_to_all | solution.py:606
  11.4 0.0 copy-start.3
  11.4 0.0 copy-start.4
  11.4 0.1 split.1
  11.5 0.0 copy-start.12
  11.5 19.4 %all-to-all-done = f32[32,48,128]{2,1,0:T(8,128)S(1)} async-done(((f32[32,48,128]{2,1,0:T(8,128)}), f32[32,48,128]{2,1,0:T(8,128)S(1)}, u32[]{:S(2)}, u32[]{:S(2)}) %all-to-all-start) | async-done | bytes 786464 | tf_op jit(solution)/shard_map/all_to_all | solution.py:606
  31.0 2.9 %collective-permute-start = (f32[32,768]{1,0:T(8,128)S(1)}, f32[32,768]{1,0:T(8,128)S(1)}, u32[]{:S(2)}, u32[]{:S(2)}) collective-permute-start(f32[32,768]{1,0:T(8,128)S(1)} %get-tuple-element.38), channel_id=1, source_target_pairs={{0,1},{1,2},{2,3},{3,0},{4,5},{5,6},{6,7},{7,4},{8,9},{9,10},{10,1... | collective-permute-start | bytes 294920 | tf_op jit(solution)/shard_map/ppermute | solution.py:610
  33.9 0.7 collective-permute-start.1
  34.7 1.7 %collective-permute-start.2 = (f32[32,768]{1,0:T(8,128)S(1)}, f32[32,768]{1,0:T(8,128)S(1)}, u32[]{:S(2)}, u32[]{:S(2)}) collective-permute-start(f32[32,768]{1,0:T(8,128)S(1)} %get-tuple-element.40), channel_id=1, source_target_pairs={{0,3},{1,0},{2,1},{3,2},{4,7},{5,4},{6,5},{7,6},{8,11},{9,8},{10,9... | collective-permute-start | bytes 294920 | tf_op jit(solution)/shard_map/ppermute | solution.py:610
  36.3 0.2 fusion.nodes_ref
  36.6 7.9 %mix.2 = (f32[32,24,128]{2,1,0:T(8,128)}, f32[11,8,128]{2,1,0:T(8,128)S(1)}) custom-call(s32[726]{0:T(1024)S(1)} %fusion.nodes_ref, s32[660]{0:T(1024)S(1)} %copy-done.9, f32[1536,128]{1,0:T(8,128)S(1)} %bitcast.8, bf16[4,128,128]{2,1,0:T(8,128)(2,1)S(1)} %copy-done.8, bf16[256,384]{1,0:T(8,128)(2,1)S(1)} %copy-done.3, bf16[384,128]{1,0:T(8,128)(2,1)S(1)} %copy-done.4), custom_call_target="tpu_custom_call" | custom-call | tf_op jit(solution)/shard_map/mix/pallas_call | solution.py:671
  44.5 2.7 %all-to-all-start.1 = ((f32[32,24,128]{2,1,0:T(8,128)}), f32[32,24,128]{2,1,0:T(8,128)S(1)}, u32[]{:S(2)}, u32[]{:S(2)}) async-start(f32[32,24,128]{2,1,0:T(8,128)} %get-tuple-element.43), calls=%async_computation.1 | async-start | bytes 786432 | tf_op jit(solution)/shard_map/all_to_all | solution.py:606
  47.3 0.1 dynamic-slice_convert_fusion
  47.4 0.1 dynamic_slice.7
  47.4 0.6 load.1
  48.1 11.0 %all-to-all-done.1.image_ref = f32[32,24,128]{2,1,0:T(8,128)S(1)} async-done(((f32[32,24,128]{2,1,0:T(8,128)}), f32[32,24,128]{2,1,0:T(8,128)S(1)}, u32[]{:S(2)}, u32[]{:S(2)}) %all-to-all-start.1) | async-done | bytes 393248 | tf_op jit(solution)/shard_map/all_to_all | solution.py:606
  59.1 0.1 broadcast_in_dim.26.live_ref
  59.2 4.8 %middle.1 = (f32[32,48,128]{2,1,0:T(8,128)S(1)}, f32[24,3,16,128]{3,2,1,0:T(8,128)S(1)}, f32[25,3,16,128]{3,2,1,0:T(8,128)S(1)}) custom-call(f32[32,24,128]{2,1,0:T(8,128)S(1)} %all-to-all-done.1.image_ref, f32[24,3,16,128]{3,2,1,0:T(8,128)S(1)} %get-tuple-element.48.base_ref, f32[16,128]{1,0:T(8,128)S(1)} %broadcast_in_dim.26.live_ref, ...), custom_call_target="tpu_custom_call" | custom-call | tf_op jit(solution)/shard_map/middle/pallas_call | solution.py:686
  64.0 23.3 %all_to_all.20.msg_ref = f32[32,48,128]{2,1,0:T(8,128)S(1)} all-to-all(f32[32,48,128]{2,1,0:T(8,128)S(1)} %get-tuple-element.50), channel_id=1, replica_groups=mesh['chaos'=8,'slab'=4] {'chaos','slab'}, dimensions={0} | all-to-all | bytes 1572864 | tf_op jit(solution)/shard_map/all_to_all | solution.py:606
  87.3 5.0 %mix.3 = f32[32,24,128]{2,1,0:T(8,128)S(1)} custom-call(s32[726]{0:T(1024)S(1)} %fusion.nodes_ref, s32[660]{0:T(1024)S(1)} %copy-done.9, f32[32,48,128]{2,1,0:T(8,128)S(1)} %all_to_all.20.msg_ref, f32[11,8,128]{2,1,0:T(8,128)S(1)} %get-tuple-element.51.mods_ref, bf16[256,384]{1,0:T(8,128)(2,1)S(1)} %copy-done.3, bf16[384,128]{1,0:T(8,128)(2,1)S(1)} %copy-done.4), custom_call_target="tpu_custom_call" | custom-call | tf_op jit(solution)/shard_map/mix/pallas_call | solution.py:694
  92.3 16.0 %all_to_all.21.image_ref = f32[32,24,128]{2,1,0:T(8,128)S(1)} all-to-all(f32[32,24,128]{2,1,0:T(8,128)S(1)} %mix.3), channel_id=1, replica_groups=mesh['chaos'=8,'slab'=4] {'chaos','slab'}, dimensions={0} | all-to-all | bytes 786432 | tf_op jit(solution)/shard_map/all_to_all | solution.py:606
  108.3 4.2 %end.1 = (f32[56,768]{1,0:T(8,128)S(1)}, f32[56,768]{1,0:T(8,128)S(1)}, f32[56,768]{1,0:T(8,128)S(1)}, f32[56,768]{1,0:T(8,128)S(1)}) custom-call(f32[32,24,128]{2,1,0:T(8,128)S(1)} %all_to_all.21.image_ref, f32[24,3,16,128]{3,2,1,0:T(8,128)S(1)} %get-tuple-element.52.base_ref, f32[16,128]{1,0:T(8,128)S(1)} %broadcast_in_dim.26.live_ref, ...), custom_call_target="tpu_custom_call" | custom-call | tf_op jit(solution)/shard_map/end/pallas_call | solution.py:698
  112.5 2.3 %collective-permute-start.3 = (f32[56,768]{1,0:T(8,128)S(1)}, f32[56,768]{1,0:T(8,128)S(1)}, u32[]{:S(2)}, u32[]{:S(2)}) collective-permute-start(f32[56,768]{1,0:T(8,128)S(1)} %get-tuple-element.55), channel_id=1, source_target_pairs={{0,1},{1,2},{2,3},{3,0},{4,5},{5,6},{6,7},{7,4},{8,9},{9,10},{10,1... | collective-permute-start | bytes 516104 | tf_op jit(solution)/shard_map/ppermute | solution.py:610
  114.8 0.9 collective-permute-start.4
  115.7 1.6 %collective-permute-start.5 = (f32[56,768]{1,0:T(8,128)S(1)}, f32[56,768]{1,0:T(8,128)S(1)}, u32[]{:S(2)}, u32[]{:S(2)}) collective-permute-start(f32[56,768]{1,0:T(8,128)S(1)} %get-tuple-element.57), channel_id=1, source_target_pairs={{0,3},{1,0},{2,1},{3,2},{4,7},{5,4},{6,5},{7,6},{8,11},{9,8},{10,9... | collective-permute-start | bytes 516104 | tf_op jit(solution)/shard_map/ppermute | solution.py:610
  117.3 0.1 fusion.1
  117.3 0.1 copy.18.live_ref
  117.4 4.1 %collective-permute-done.3.refs_1_ = f32[56,768]{1,0:T(8,128)S(1)} collective-permute-done((f32[56,768]{1,0:T(8,128)S(1)}, f32[56,768]{1,0:T(8,128)S(1)}, u32[]{:S(2)}, u32[]{:S(2)}) %collective-permute-start.3) | collective-permute-done | bytes 172064 | tf_op jit(solution)/shard_map/ppermute | solution.py:610
  121.6 7.6 %collective-permute-done.4.refs_2_ = f32[56,768]{1,0:T(8,128)S(1)} collective-permute-done((f32[56,768]{1,0:T(8,128)S(1)}, f32[56,768]{1,0:T(8,128)S(1)}, u32[]{:S(2)}, u32[]{:S(2)}) %collective-permute-start.4) | collective-permute-done | bytes 172064 | tf_op jit(solution)/shard_map/ppermute | solution.py:610
  129.2 1.1 finish.1
  (29 shorter events, 0.1 us)
Async XLA Ops:
  4.0 7.4 %copy-start.10 = (f32[768]{0:T(1024)S(1)}, f32[768]{0:T(1024)}, u32[]{:S(2)}) copy-start(f32[768]{0:T(1024)} %param.17) | copy-start | bytes 9220
  4.0 7.4 %copy-start.5 = (f32[36,3,768]{2,0,1:T(8,128)S(1)}, f32[36,3,768]{2,0,1:T(8,128)}, u32[]{:S(2)}) copy-start(f32[36,3,768]{2,0,1:T(8,128)} %param.16) | copy-start | bytes 995332
  4.0 32.5 %copy-start.8 = (bf16[4,128,128]{2,1,0:T(8,128)(2,1)S(1)}, bf16[4,128,128]{2,1,0:T(8,128)(2,1)}, u32[]{:S(2)}) copy-start(bf16[4,128,128]{2,1,0:T(8,128)(2,1)} %constant.44.clone.mtab_ref) | copy-start | bytes 393220
  4.1 26.9 %all-to-all-start = ((f32[32,48,128]{2,1,0:T(8,128)}), f32[32,48,128]{2,1,0:T(8,128)S(1)}, u32[]{:S(2)}, u32[]{:S(2)}) async-start(f32[32,48,128]{2,1,0:T(8,128)} %start.1), calls=%async_computation | async-start | bytes 1572864 | tf_op jit(solution)/shard_map/all_to_all | solution.py:606
  11.4 25.1 %copy-start.3 = (bf16[256,384]{1,0:T(8,128)(2,1)S(1)}, bf16[256,384]{1,0:T(8,128)(2,1)}, u32[]{:S(2)}) copy-start(bf16[256,384]{1,0:T(8,128)(2,1)} %constant.47.clone.grad_ref) | copy-start | bytes 589828
  11.4 25.1 %copy-start.4 = (bf16[384,128]{1,0:T(8,128)(2,1)S(1)}, bf16[384,128]{1,0:T(8,128)(2,1)}, u32[]{:S(2)}) copy-start(bf16[384,128]{1,0:T(8,128)(2,1)} %constant.48.clone.div_ref) | copy-start | bytes 294916
  11.5 24.8 %copy-start.12 = (s32[726]{0:T(1024)S(1)}, s32[726]{0:T(1024)}, u32[]{:S(2)}) copy-start(s32[726]{0:T(1024)} %constant.54) | copy-start | bytes 8716
  31.0 5.4 %copy-start.11 = (s32[288]{0:T(512)S(1)}, s32[288]{0:T(512)}, u32[]{:S(2)}) copy-start(s32[288]{0:T(512)} %param.19) | copy-start | bytes 3460
  31.0 5.6 %copy-start.9 = (s32[660]{0:T(1024)S(1)}, s32[660]{0:T(1024)}, u32[]{:S(2)}) copy-start(s32[660]{0:T(1024)} %constant.49.clone.level_ref) | copy-start | bytes 7924
  31.0 13.5 %collective-permute-start = (f32[32,768]{1,0:T(8,128)S(1)}, f32[32,768]{1,0:T(8,128)S(1)}, u32[]{:S(2)}, u32[]{:S(2)}) collective-permute-start(f32[32,768]{1,0:T(8,128)S(1)} %get-tuple-element.38), channel_id=1, source_target_pairs={{0,1},{1,2},{2,3},{3,0},{4,5},{5,6},{6,7},{7,4},{8,9},{9,10},{10,1... | collective-permute-start | bytes 294920 | tf_op jit(solution)/shard_map/ppermute | solution.py:610
  33.9 10.5 %collective-permute-start.1 = (f32[32,768]{1,0:T(8,128)S(1)}, f32[32,768]{1,0:T(8,128)S(1)}, u32[]{:S(2)}, u32[]{:S(2)}) collective-permute-start(f32[32,768]{1,0:T(8,128)S(1)} %get-tuple-element.39), channel_id=1, source_target_pairs={{0,2},{1,3},{2,0},{3,1},{4,6},{5,7},{6,4},{7,5},{8,10},{9,11},{10,... | collective-permute-start | bytes 294920 | tf_op jit(solution)/shard_map/ppermute | solution.py:610
  34.7 9.8 %collective-permute-start.2 = (f32[32,768]{1,0:T(8,128)S(1)}, f32[32,768]{1,0:T(8,128)S(1)}, u32[]{:S(2)}, u32[]{:S(2)}) collective-permute-start(f32[32,768]{1,0:T(8,128)S(1)} %get-tuple-element.40), channel_id=1, source_target_pairs={{0,3},{1,0},{2,1},{3,2},{4,7},{5,4},{6,5},{7,6},{8,11},{9,8},{10,9... | collective-permute-start | bytes 294920 | tf_op jit(solution)/shard_map/ppermute | solution.py:610
  44.5 14.7 %copy-start = (bf16[512,512]{1,0:T(8,128)(2,1)S(1)}, bf16[512,512]{1,0:T(8,128)(2,1)}, u32[]{:S(2)}) copy-start(bf16[512,512]{1,0:T(8,128)(2,1)} %constant.43.clone.unpack_ref) | copy-start | bytes 1572868
  44.5 14.7 %copy-start.6 = (bf16[128,256]{1,0:T(8,128)(2,1)S(1)}, bf16[128,256]{1,0:T(8,128)(2,1)}, u32[]{:S(2)}) copy-start(bf16[128,256]{1,0:T(8,128)(2,1)} %constant.45.clone.slope_ref) | copy-start | bytes 196612
  44.5 14.7 %copy-start.7 = (bf16[256,128]{1,0:T(8,128)(2,1)S(1)}, bf16[256,128]{1,0:T(8,128)(2,1)}, u32[]{:S(2)}) copy-start(bf16[256,128]{1,0:T(8,128)(2,1)} %constant.46.clone.back_ref) | copy-start | bytes 196612
  44.5 14.6 %all-to-all-start.1 = ((f32[32,24,128]{2,1,0:T(8,128)}), f32[32,24,128]{2,1,0:T(8,128)S(1)}, u32[]{:S(2)}, u32[]{:S(2)}) async-start(f32[32,24,128]{2,1,0:T(8,128)} %get-tuple-element.43), calls=%async_computation.1 | async-start | bytes 786432 | tf_op jit(solution)/shard_map/all_to_all | solution.py:606
  47.2 11.9 %copy-start.1 = (bf16[384,512]{1,0:T(8,128)(2,1)S(1)}, bf16[384,512]{1,0:T(8,128)(2,1)}, u32[]{:S(2)}) copy-start(bf16[384,512]{1,0:T(8,128)(2,1)} %constant.42.clone.pack_hbm.pack_ref) | copy-start | bytes 1179652
  108.3 20.9 %copy-start.2 = (f32[36,3,768]{2,0,1:T(8,128)S(1)}, f32[36,3,768]{2,0,1:T(8,128)}, u32[]{:S(2)}) copy-start(f32[36,3,768]{2,0,1:T(8,128)} %param.15) | copy-start | bytes 995332
  112.5 9.1 %collective-permute-start.3 = (f32[56,768]{1,0:T(8,128)S(1)}, f32[56,768]{1,0:T(8,128)S(1)}, u32[]{:S(2)}, u32[]{:S(2)}) collective-permute-start(f32[56,768]{1,0:T(8,128)S(1)} %get-tuple-element.55), channel_id=1, source_target_pairs={{0,1},{1,2},{2,3},{3,0},{4,5},{5,6},{6,7},{7,4},{8,9},{9,10},{10,1... | collective-permute-start | bytes 516104 | tf_op jit(solution)/shard_map/ppermute | solution.py:610
  114.8 14.3 %collective-permute-start.4 = (f32[56,768]{1,0:T(8,128)S(1)}, f32[56,768]{1,0:T(8,128)S(1)}, u32[]{:S(2)}, u32[]{:S(2)}) collective-permute-start(f32[56,768]{1,0:T(8,128)S(1)} %get-tuple-element.56), channel_id=1, source_target_pairs={{0,2},{1,3},{2,0},{3,1},{4,6},{5,7},{6,4},{7,5},{8,10},{9,11},{10,... | collective-permute-start | bytes 516104 | tf_op jit(solution)/shard_map/ppermute | solution.py:610
  115.7 13.5 %collective-permute-start.5 = (f32[56,768]{1,0:T(8,128)S(1)}, f32[56,768]{1,0:T(8,128)S(1)}, u32[]{:S(2)}, u32[]{:S(2)}) collective-permute-start(f32[56,768]{1,0:T(8,128)S(1)} %get-tuple-element.57), channel_id=1, source_target_pairs={{0,3},{1,0},{2,1},{3,2},{4,7},{5,4},{6,5},{7,6},{8,11},{9,8},{10,9... | collective-permute-start | bytes 516104 | tf_op jit(solution)/shard_map/ppermute | solution.py:610

commit v10 on v9

--- a/solution.py
+++ b/solution.py
@@ -665,8 +665,8 @@
     load_flat = call(
         functools.partial(split_kernel, plan), "split", [vmem, vmem], (flat,) * slab, [pltpu.VMEM((slab, plan.rows_flat, PLANE), F32)]
     )(by_component(load), mean_row)
-    load_flat, arrived = lax.optimization_barrier((load_flat, arrived))
-    load_flat = column(load_flat)
+    later, arrived = lax.optimization_barrier((load_flat[2:], arrived))
+    load_flat = column([*load_flat[:2], *later])
     arrived, nodes = lax.optimization_barrier((arrived, nodes))
     first_image, mods = call(
         functools.partial(first_mix_kernel, plan, len(low), 3),

time: 131 us -> 133 us (1.015)
  starting transfers between devices: 20.2 us -> 21.9 us
    ppermute x6, starting transfers between devices: 10.1 us -> 11.9 us  [column(): lax.ppermute(pieces[step], 'slab', [(z, (z + step) % slab) for z in range...]
  transfers between devices with their start and end apart: 8 -> 8, of which waited for: 4 -> 4; matrix products, arithmetic and copies ran while one was open for 0% -> 0% of each run, Pallas kernels for 7% -> 6%
where the time goes in v10:
time: 133 us; the launch traced here: 132 us
  waiting for transfers between devices  42.4 us (32%)
  blocking collectives  39.2 us (29%)
  Pallas kernels  27.2 us (20%)
  starting transfers between devices  21.9 us (16%)
    all_to_all x2, blocking collectives, everyone(): return lax.all_to_all(values, ('chaos', 'slab'), 0, 0, tiled=True)  39.2 us
    all_to_all x2, waiting for transfers between devices, everyone(): return lax.all_to_all(values, ('chaos', 'slab'), 0, 0, tiled=True)  30.7 us
    ppermute x6, starting transfers between devices, column(): lax.ppermute(pieces[step], 'slab', [(z, (z + step) % slab) for z in range...  11.9 us
    ppermute x6, waiting for transfers between devices, column(): lax.ppermute(pieces[step], 'slab', [(z, (z + step) % slab) for z in range...  11.7 us
    all_to_all x2, starting transfers between devices, everyone(): return lax.all_to_all(values, ('chaos', 'slab'), 0, 0, tiled=True)  10 us
    pallas_call x1, Pallas kernels, per_device(): call(functools.partial(first_mix_kernel, plan, len(low), 3), 'mix', [smem...  7.87 us
    pallas_call x1, Pallas kernels, per_device(): call(functools.partial(mix_kernel, plan, len(low), 2), 'mix', [smem, smem...  5.02 us
    pallas_call x1, Pallas kernels, per_device(): call(functools.partial(middle_kernel, plan), 'middle', [vmem] * 8, (messa...  4.9 us
  transfers between devices with their start and end apart: 8, of which 4 were waited for; matrix products, arithmetic and copies ran while one was open for 0% of the time, Pallas kernels for 6%

profile of v10, /device:TPU:0, one launch (start us, length us, event | category | flops | bytes accessed | tf_op | source)
XLA Modules:
  0.0 132.3 jit_solution(84771831079465630)
XLA Ops:
  0.6 3.4 %start.1 = f32[32,48,128]{2,1,0:T(8,128)} custom-call(f32[3,36,768]{2,1,0:T(8,128)} %bitcast.9, f32[6,128]{1,0:T(8,128)} %bitcast.12, f32[10,768]{1,0:T(8,128)} %modes_hbm.1, bf16[384,512]{1,0:T(8,128)(2,1)} %constant.42.clone.pack_hbm.pack_ref), custom_call_target="tpu_custom_call" | custom-call | tf_op jit(solution)/shard_map/start/pallas_call | solution.py:639
  4.0 0.0 copy-start.8
  4.1 7.3 %all-to-all-start = ((f32[32,48,128]{2,1,0:T(8,128)}), f32[32,48,128]{2,1,0:T(8,128)S(1)}, u32[]{:S(2)}, u32[]{:S(2)}) async-start(f32[32,48,128]{2,1,0:T(8,128)} %start.1), calls=%async_computation | async-start | bytes 1572864 | tf_op jit(solution)/shard_map/all_to_all | solution.py:606
  11.4 0.0 copy-start.3
  11.4 0.0 copy-start.12
  11.4 0.0 copy-start.4
  11.4 0.1 split.1
  11.6 1.8 %collective-permute-start = (f32[32,768]{1,0:T(8,128)S(1)}, f32[32,768]{1,0:T(8,128)S(1)}, u32[]{:S(2)}, u32[]{:S(2)}) collective-permute-start(f32[32,768]{1,0:T(8,128)S(1)} %get-tuple-element.34), channel_id=1, source_target_pairs={{0,1},{1,2},{2,3},{3,0},{4,5},{5,6},{6,7},{7,4},{8,9},{9,10},{10,1... | collective-permute-start | bytes 294920 | tf_op jit(solution)/shard_map/ppermute | solution.py:610
  13.4 19.7 %all-to-all-done = f32[32,48,128]{2,1,0:T(8,128)S(1)} async-done(((f32[32,48,128]{2,1,0:T(8,128)}), f32[32,48,128]{2,1,0:T(8,128)S(1)}, u32[]{:S(2)}, u32[]{:S(2)}) %all-to-all-start) | async-done | bytes 786464 | tf_op jit(solution)/shard_map/all_to_all | solution.py:606
  33.1 0.5 collective-permute-start.1
  33.6 4.7 %collective-permute-start.2 = (f32[32,768]{1,0:T(8,128)S(1)}, f32[32,768]{1,0:T(8,128)S(1)}, u32[]{:S(2)}, u32[]{:S(2)}) collective-permute-start(f32[32,768]{1,0:T(8,128)S(1)} %get-tuple-element.36), channel_id=1, source_target_pairs={{0,3},{1,0},{2,1},{3,2},{4,7},{5,4},{6,5},{7,6},{8,11},{9,8},{10,9... | collective-permute-start | bytes 294920 | tf_op jit(solution)/shard_map/ppermute | solution.py:610
  38.4 0.2 fusion.nodes_ref
  38.6 7.9 %mix.2 = (f32[32,24,128]{2,1,0:T(8,128)}, f32[11,8,128]{2,1,0:T(8,128)S(1)}) custom-call(s32[726]{0:T(1024)S(1)} %fusion.nodes_ref, s32[660]{0:T(1024)S(1)} %copy-done.9, f32[1536,128]{1,0:T(8,128)S(1)} %bitcast.8, bf16[4,128,128]{2,1,0:T(8,128)(2,1)S(1)} %copy-done.8, bf16[256,384]{1,0:T(8,128)(2,1)S(1)} %copy-done.3, bf16[384,128]{1,0:T(8,128)(2,1)S(1)} %copy-done.4), custom_call_target="tpu_custom_call" | custom-call | tf_op jit(solution)/shard_map/mix/pallas_call | solution.py:671
  46.5 2.7 %all-to-all-start.1 = ((f32[32,24,128]{2,1,0:T(8,128)}), f32[32,24,128]{2,1,0:T(8,128)S(1)}, u32[]{:S(2)}, u32[]{:S(2)}) async-start(f32[32,24,128]{2,1,0:T(8,128)} %get-tuple-element.39), calls=%async_computation.1 | async-start | bytes 786432 | tf_op jit(solution)/shard_map/all_to_all | solution.py:606
  49.3 0.1 dynamic-slice_convert_fusion
  49.4 0.1 dynamic_slice.7
  49.5 0.6 load.1
  50.1 11.0 %all-to-all-done.1.image_ref = f32[32,24,128]{2,1,0:T(8,128)S(1)} async-done(((f32[32,24,128]{2,1,0:T(8,128)}), f32[32,24,128]{2,1,0:T(8,128)S(1)}, u32[]{:S(2)}, u32[]{:S(2)}) %all-to-all-start.1) | async-done | bytes 393248 | tf_op jit(solution)/shard_map/all_to_all | solution.py:606
  61.1 0.1 broadcast_in_dim.26.live_ref
  61.2 4.9 %middle.1 = (f32[32,48,128]{2,1,0:T(8,128)S(1)}, f32[24,3,16,128]{3,2,1,0:T(8,128)S(1)}, f32[25,3,16,128]{3,2,1,0:T(8,128)S(1)}) custom-call(f32[32,24,128]{2,1,0:T(8,128)S(1)} %all-to-all-done.1.image_ref, f32[24,3,16,128]{3,2,1,0:T(8,128)S(1)} %get-tuple-element.44.base_ref, f32[16,128]{1,0:T(8,128)S(1)} %broadcast_in_dim.26.live_ref, ...), custom_call_target="tpu_custom_call" | custom-call | tf_op jit(solution)/shard_map/middle/pallas_call | solution.py:686
  66.1 23.2 %all_to_all.20.msg_ref = f32[32,48,128]{2,1,0:T(8,128)S(1)} all-to-all(f32[32,48,128]{2,1,0:T(8,128)S(1)} %get-tuple-element.46), channel_id=1, replica_groups=mesh['chaos'=8,'slab'=4] {'chaos','slab'}, dimensions={0} | all-to-all | bytes 1572864 | tf_op jit(solution)/shard_map/all_to_all | solution.py:606
  89.3 5.0 %mix.3 = f32[32,24,128]{2,1,0:T(8,128)S(1)} custom-call(s32[726]{0:T(1024)S(1)} %fusion.nodes_ref, s32[660]{0:T(1024)S(1)} %copy-done.9, f32[32,48,128]{2,1,0:T(8,128)S(1)} %all_to_all.20.msg_ref, f32[11,8,128]{2,1,0:T(8,128)S(1)} %get-tuple-element.47.mods_ref, bf16[256,384]{1,0:T(8,128)(2,1)S(1)} %copy-done.3, bf16[384,128]{1,0:T(8,128)(2,1)S(1)} %copy-done.4), custom_call_target="tpu_custom_call" | custom-call | tf_op jit(solution)/shard_map/mix/pallas_call | solution.py:694
  94.3 16.0 %all_to_all.21.image_ref = f32[32,24,128]{2,1,0:T(8,128)S(1)} all-to-all(f32[32,24,128]{2,1,0:T(8,128)S(1)} %mix.3), channel_id=1, replica_groups=mesh['chaos'=8,'slab'=4] {'chaos','slab'}, dimensions={0} | all-to-all | bytes 786432 | tf_op jit(solution)/shard_map/all_to_all | solution.py:606
  110.3 4.2 %end.1 = (f32[56,768]{1,0:T(8,128)S(1)}, f32[56,768]{1,0:T(8,128)S(1)}, f32[56,768]{1,0:T(8,128)S(1)}, f32[56,768]{1,0:T(8,128)S(1)}) custom-call(f32[32,24,128]{2,1,0:T(8,128)S(1)} %all_to_all.21.image_ref, f32[24,3,16,128]{3,2,1,0:T(8,128)S(1)} %get-tuple-element.48.base_ref, f32[16,128]{1,0:T(8,128)S(1)} %broadcast_in_dim.26.live_ref, ...), custom_call_target="tpu_custom_call" | custom-call | tf_op jit(solution)/shard_map/end/pallas_call | solution.py:698
  114.5 2.3 %collective-permute-start.3 = (f32[56,768]{1,0:T(8,128)S(1)}, f32[56,768]{1,0:T(8,128)S(1)}, u32[]{:S(2)}, u32[]{:S(2)}) collective-permute-start(f32[56,768]{1,0:T(8,128)S(1)} %get-tuple-element.51), channel_id=1, source_target_pairs={{0,1},{1,2},{2,3},{3,0},{4,5},{5,6},{6,7},{7,4},{8,9},{9,10},{10,1... | collective-permute-start | bytes 516104 | tf_op jit(solution)/shard_map/ppermute | solution.py:610
  116.9 0.9 collective-permute-start.4
  117.8 1.6 %collective-permute-start.5 = (f32[56,768]{1,0:T(8,128)S(1)}, f32[56,768]{1,0:T(8,128)S(1)}, u32[]{:S(2)}, u32[]{:S(2)}) collective-permute-start(f32[56,768]{1,0:T(8,128)S(1)} %get-tuple-element.53), channel_id=1, source_target_pairs={{0,3},{1,0},{2,1},{3,2},{4,7},{5,4},{6,5},{7,6},{8,11},{9,8},{10,9... | collective-permute-start | bytes 516104 | tf_op jit(solution)/shard_map/ppermute | solution.py:610
  119.3 0.1 fusion.1
  119.4 0.1 copy.18.live_ref
  119.5 4.1 %collective-permute-done.3.refs_1_ = f32[56,768]{1,0:T(8,128)S(1)} collective-permute-done((f32[56,768]{1,0:T(8,128)S(1)}, f32[56,768]{1,0:T(8,128)S(1)}, u32[]{:S(2)}, u32[]{:S(2)}) %collective-permute-start.3) | collective-permute-done | bytes 172064 | tf_op jit(solution)/shard_map/ppermute | solution.py:610
  123.6 7.6 %collective-permute-done.4.refs_2_ = f32[56,768]{1,0:T(8,128)S(1)} collective-permute-done((f32[56,768]{1,0:T(8,128)S(1)}, f32[56,768]{1,0:T(8,128)S(1)}, u32[]{:S(2)}, u32[]{:S(2)}) %collective-permute-start.4) | collective-permute-done | bytes 172064 | tf_op jit(solution)/shard_map/ppermute | solution.py:610
  131.2 1.1 finish.1
  (29 shorter events, 0.1 us)
Async XLA Ops:
  4.0 7.4 %copy-start.10 = (f32[768]{0:T(1024)S(1)}, f32[768]{0:T(1024)}, u32[]{:S(2)}) copy-start(f32[768]{0:T(1024)} %param.17) | copy-start | bytes 9220
  4.0 7.4 %copy-start.5 = (f32[36,3,768]{2,0,1:T(8,128)S(1)}, f32[36,3,768]{2,0,1:T(8,128)}, u32[]{:S(2)}) copy-start(f32[36,3,768]{2,0,1:T(8,128)} %param.16) | copy-start | bytes 995332
  4.0 34.5 %copy-start.8 = (bf16[4,128,128]{2,1,0:T(8,128)(2,1)S(1)}, bf16[4,128,128]{2,1,0:T(8,128)(2,1)}, u32[]{:S(2)}) copy-start(bf16[4,128,128]{2,1,0:T(8,128)(2,1)} %constant.44.clone.mtab_ref) | copy-start | bytes 393220
  4.1 29.0 %all-to-all-start = ((f32[32,48,128]{2,1,0:T(8,128)}), f32[32,48,128]{2,1,0:T(8,128)S(1)}, u32[]{:S(2)}, u32[]{:S(2)}) async-start(f32[32,48,128]{2,1,0:T(8,128)} %start.1), calls=%async_computation | async-start | bytes 1572864 | tf_op jit(solution)/shard_map/all_to_all | solution.py:606
  11.4 27.2 %copy-start.3 = (bf16[256,384]{1,0:T(8,128)(2,1)S(1)}, bf16[256,384]{1,0:T(8,128)(2,1)}, u32[]{:S(2)}) copy-start(bf16[256,384]{1,0:T(8,128)(2,1)} %constant.47.clone.grad_ref) | copy-start | bytes 589828
  11.4 27.0 %copy-start.12 = (s32[726]{0:T(1024)S(1)}, s32[726]{0:T(1024)}, u32[]{:S(2)}) copy-start(s32[726]{0:T(1024)} %constant.54) | copy-start | bytes 8716
  11.4 27.1 %copy-start.4 = (bf16[384,128]{1,0:T(8,128)(2,1)S(1)}, bf16[384,128]{1,0:T(8,128)(2,1)}, u32[]{:S(2)}) copy-start(bf16[384,128]{1,0:T(8,128)(2,1)} %constant.48.clone.div_ref) | copy-start | bytes 294916
  11.5 26.8 %copy-start.11 = (s32[288]{0:T(512)S(1)}, s32[288]{0:T(512)}, u32[]{:S(2)}) copy-start(s32[288]{0:T(512)} %param.19) | copy-start | bytes 3460
  11.6 34.9 %collective-permute-start = (f32[32,768]{1,0:T(8,128)S(1)}, f32[32,768]{1,0:T(8,128)S(1)}, u32[]{:S(2)}, u32[]{:S(2)}) collective-permute-start(f32[32,768]{1,0:T(8,128)S(1)} %get-tuple-element.34), channel_id=1, source_target_pairs={{0,1},{1,2},{2,3},{3,0},{4,5},{5,6},{6,7},{7,4},{8,9},{9,10},{10,1... | collective-permute-start | bytes 294920 | tf_op jit(solution)/shard_map/ppermute | solution.py:610
  33.1 5.5 %copy-start.9 = (s32[660]{0:T(1024)S(1)}, s32[660]{0:T(1024)}, u32[]{:S(2)}) copy-start(s32[660]{0:T(1024)} %constant.49.clone.level_ref) | copy-start | bytes 7924
  33.1 13.4 %collective-permute-start.1 = (f32[32,768]{1,0:T(8,128)S(1)}, f32[32,768]{1,0:T(8,128)S(1)}, u32[]{:S(2)}, u32[]{:S(2)}) collective-permute-start(f32[32,768]{1,0:T(8,128)S(1)} %get-tuple-element.35), channel_id=1, source_target_pairs={{0,2},{1,3},{2,0},{3,1},{4,6},{5,7},{6,4},{7,5},{8,10},{9,11},{10,... | collective-permute-start | bytes 294920 | tf_op jit(solution)/shard_map/ppermute | solution.py:610
  33.6 12.8 %collective-permute-start.2 = (f32[32,768]{1,0:T(8,128)S(1)}, f32[32,768]{1,0:T(8,128)S(1)}, u32[]{:S(2)}, u32[]{:S(2)}) collective-permute-start(f32[32,768]{1,0:T(8,128)S(1)} %get-tuple-element.36), channel_id=1, source_target_pairs={{0,3},{1,0},{2,1},{3,2},{4,7},{5,4},{6,5},{7,6},{8,11},{9,8},{10,9... | collective-permute-start | bytes 294920 | tf_op jit(solution)/shard_map/ppermute | solution.py:610
  46.5 14.7 %copy-start = (bf16[512,512]{1,0:T(8,128)(2,1)S(1)}, bf16[512,512]{1,0:T(8,128)(2,1)}, u32[]{:S(2)}) copy-start(bf16[512,512]{1,0:T(8,128)(2,1)} %constant.43.clone.unpack_ref) | copy-start | bytes 1572868
  46.5 14.7 %copy-start.6 = (bf16[128,256]{1,0:T(8,128)(2,1)S(1)}, bf16[128,256]{1,0:T(8,128)(2,1)}, u32[]{:S(2)}) copy-start(bf16[128,256]{1,0:T(8,128)(2,1)} %constant.45.clone.slope_ref) | copy-start | bytes 196612
  46.5 14.7 %copy-start.7 = (bf16[256,128]{1,0:T(8,128)(2,1)S(1)}, bf16[256,128]{1,0:T(8,128)(2,1)}, u32[]{:S(2)}) copy-start(bf16[256,128]{1,0:T(8,128)(2,1)} %constant.46.clone.back_ref) | copy-start | bytes 196612
  46.5 14.6 %all-to-all-start.1 = ((f32[32,24,128]{2,1,0:T(8,128)}), f32[32,24,128]{2,1,0:T(8,128)S(1)}, u32[]{:S(2)}, u32[]{:S(2)}) async-start(f32[32,24,128]{2,1,0:T(8,128)} %get-tuple-element.39), calls=%async_computation.1 | async-start | bytes 786432 | tf_op jit(solution)/shard_map/all_to_all | solution.py:606
  49.3 11.9 %copy-start.1 = (bf16[384,512]{1,0:T(8,128)(2,1)S(1)}, bf16[384,512]{1,0:T(8,128)(2,1)}, u32[]{:S(2)}) copy-start(bf16[384,512]{1,0:T(8,128)(2,1)} %constant.42.clone.pack_hbm.pack_ref) | copy-start | bytes 1179652
  110.3 20.9 %copy-start.2 = (f32[36,3,768]{2,0,1:T(8,128)S(1)}, f32[36,3,768]{2,0,1:T(8,128)}, u32[]{:S(2)}) copy-start(f32[36,3,768]{2,0,1:T(8,128)} %param.15) | copy-start | bytes 995332
  114.5 9.1 %collective-permute-start.3 = (f32[56,768]{1,0:T(8,128)S(1)}, f32[56,768]{1,0:T(8,128)S(1)}, u32[]{:S(2)}, u32[]{:S(2)}) collective-permute-start(f32[56,768]{1,0:T(8,128)S(1)} %get-tuple-element.51), channel_id=1, source_target_pairs={{0,1},{1,2},{2,3},{3,0},{4,5},{5,6},{6,7},{7,4},{8,9},{9,10},{10,1... | collective-permute-start | bytes 516104 | tf_op jit(solution)/shard_map/ppermute | solution.py:610
  116.9 14.3 %collective-permute-start.4 = (f32[56,768]{1,0:T(8,128)S(1)}, f32[56,768]{1,0:T(8,128)S(1)}, u32[]{:S(2)}, u32[]{:S(2)}) collective-permute-start(f32[56,768]{1,0:T(8,128)S(1)} %get-tuple-element.52), channel_id=1, source_target_pairs={{0,2},{1,3},{2,0},{3,1},{4,6},{5,7},{6,4},{7,5},{8,10},{9,11},{10,... | collective-permute-start | bytes 516104 | tf_op jit(solution)/shard_map/ppermute | solution.py:610
  117.8 13.5 %collective-permute-start.5 = (f32[56,768]{1,0:T(8,128)S(1)}, f32[56,768]{1,0:T(8,128)S(1)}, u32[]{:S(2)}, u32[]{:S(2)}) collective-permute-start(f32[56,768]{1,0:T(8,128)S(1)} %get-tuple-element.53), channel_id=1, source_target_pairs={{0,3},{1,0},{2,1},{3,2},{4,7},{5,4},{6,5},{7,6},{8,11},{9,8},{10,9... | collective-permute-start | bytes 516104 | tf_op jit(solution)/shard_map/ppermute | solution.py:610

commit v11 on v8

--- a/solution.py
+++ b/solution.py
@@ -166,6 +166,20 @@
                     table[j + NY, self.ls + j] = 1
         return table
 
+    def regroup_table(self):
+        wide = self.slab * self.lanes
+        if wide > 1024:
+            return np.zeros((8, 128), np.float32)
+        table = np.zeros((wide, wide), np.float32)
+        for c in range(3):
+            for z in range(self.nz):
+                for group in range(self.slab):
+                    for y in range(self.ry):
+                        table[
+                            z * self.lanes + self.tile_lane(c, group, y), group * self.lanes + self.tile_lane(c, z, y)
+                        ] = 1
+        return table
+
     def modulus_table(self):
         table = np.zeros((self.nyb, self.ls, self.lanes), np.float32)
         for yb in range(self.nyb):
@@ -366,7 +380,27 @@
             residual_ref[c, here, :] = groups[group, (3 + c) * plan.sp : (4 + c) * plan.sp, :]
 
 
-def regrouped(plan, msg_ref, out_ref):
+def regrouped(plan, msg_ref, table_ref, out_ref):
+    if table_ref.shape[0] == plan.slab * plan.lanes:
+        many = 4 if plan.chaos % 4 == 0 else 1
+        for first in range(0, plan.chaos, many):
+            blocks = [
+                jnp.concatenate(
+                    [
+                        msg_ref[pl.ds((row * plan.slab + z) * plan.rows_in, plan.rows_in), :]
+                        for z in range(plan.nz)
+                    ],
+                    axis=1,
+                )
+                for row in range(first, first + many)
+            ]
+            moved = picked(jnp.concatenate(blocks, axis=0), table_ref[...])
+            for i in range(many):
+                for group in range(plan.slab):
+                    out_ref[(first + i) * plan.slab + group] = moved[
+                        i * plan.rows_in : (i + 1) * plan.rows_in, group * plan.lanes : (group + 1) * plan.lanes
+                    ]
+        return
     lane = lax.broadcasted_iota(jnp.int32, (plan.rows_in, plan.lanes), 1)
     height = lane % (plan.nz * plan.ry) // plan.ry
 
@@ -386,9 +420,9 @@
     lax.fori_loop(0, plan.chaos, one, 0, unroll=4)
 
 
-def first_mix_kernel(plan, low_count, parts, nodes_ref, level_ref, msg_ref, mtab_ref, grad_ref, div_ref, out_ref, mods_ref, grad, flux, scaled, regroup):
+def first_mix_kernel(plan, low_count, parts, nodes_ref, level_ref, msg_ref, mtab_ref, regroup_ref, grad_ref, div_ref, out_ref, mods_ref, grad, flux, scaled, regroup):
     gather_moduli(plan, lax.axis_index("chaos") * plan.slab + lax.axis_index("slab"), msg_ref, mtab_ref, mods_ref)
-    regrouped(plan, msg_ref, regroup)
+    regrouped(plan, msg_ref, regroup_ref, regroup)
     mix_kernel(plan, low_count, parts, nodes_ref, level_ref, regroup, mods_ref, grad_ref, div_ref, out_ref, grad, flux, scaled)
 
 
@@ -665,15 +699,16 @@
     load_flat = call(
         functools.partial(split_kernel, plan), "split", [vmem, vmem], (flat,) * slab, [pltpu.VMEM((slab, plan.rows_flat, PLANE), F32)]
     )(by_component(load), mean_row)
+    load_flat, arrived = lax.optimization_barrier((load_flat, arrived))
     load_flat = column(load_flat)
     arrived, nodes = lax.optimization_barrier((arrived, nodes))
     first_image, mods = call(
         functools.partial(first_mix_kernel, plan, len(low), 3),
         "mix",
-        [smem, smem, vmem, vmem, vmem, vmem],
+        [smem, smem, vmem, vmem, vmem, vmem, vmem],
         (image, array(FIELDS, 8, lanes)),
         mix_scratch + [pltpu.VMEM((n, plan.rows_in, lanes), F32)],
-    )(nodes, levels, arrived.reshape(n * plan.rows_in, lanes), mtab, grads, divs)
+    )(nodes, levels, arrived.reshape(n * plan.rows_in, lanes), mtab, jnp.asarray(plan.regroup_table(), BF16), grads, divs)
     load_flat, first_image = lax.optimization_barrier((load_flat, first_image))
     load_s, mean_s = call(
         functools.partial(load_kernel, plan),

time: 131 us -> 130 us (level)
  starting transfers between devices: 22.1 us -> 20.1 us
  waiting for transfers between devices: 40.6 us -> 42.2 us
    all_to_all x2, starting transfers between devices: 11.7 us -> 10 us  [everyone(): return lax.all_to_all(values, ('chaos', 'slab'), 0, 0, tiled=True)]
    all_to_all x2, waiting for transfers between devices: 28.8 us -> 30.4 us  [everyone(): return lax.all_to_all(values, ('chaos', 'slab'), 0, 0, tiled=True)]
where the time goes in v11:
time: 130 us
  waiting for transfers between devices  42.2 us (32%)
  blocking collectives  39.2 us (30%)
  Pallas kernels  26.6 us (20%)
  starting transfers between devices  20.1 us (15%)
    all_to_all x2, blocking collectives, everyone(): return lax.all_to_all(values, ('chaos', 'slab'), 0, 0, tiled=True)  39.2 us
    all_to_all x2, waiting for transfers between devices, everyone(): return lax.all_to_all(values, ('chaos', 'slab'), 0, 0, tiled=True)  30.4 us
    ppermute x6, waiting for transfers between devices, column(): lax.ppermute(pieces[step], 'slab', [(z, (z + step) % slab) for z in range...  11.8 us
    ppermute x6, starting transfers between devices, column(): lax.ppermute(pieces[step], 'slab', [(z, (z + step) % slab) for z in range...  10.1 us
    all_to_all x2, starting transfers between devices, everyone(): return lax.all_to_all(values, ('chaos', 'slab'), 0, 0, tiled=True)  10 us
    pallas_call x1, Pallas kernels, per_device(): call(functools.partial(first_mix_kernel, plan, len(low), 3), 'mix', [smem...  7.77 us
    pallas_call x1, Pallas kernels, per_device(): call(functools.partial(mix_kernel, plan, len(low), 2), 'mix', [smem, smem...  5.01 us
    pallas_call x1, Pallas kernels, per_device(): call(functools.partial(middle_kernel, plan), 'middle', [vmem] * 8, (messa...  4.59 us
  transfers between devices with their start and end apart: 8, of which 4 were waited for; matrix products, arithmetic and copies ran while one was open for 0% of the time, Pallas kernels for 7%

profile of v11, /device:TPU:0, one launch (start us, length us, event | category | flops | bytes accessed | tf_op | source)
XLA Modules:
  0.0 129.7 jit_solution(4297599555435834192)
XLA Ops:
  0.6 3.4 %start.1 = f32[32,48,128]{2,1,0:T(8,128)} custom-call(f32[3,36,768]{2,1,0:T(8,128)} %bitcast.9, f32[6,128]{1,0:T(8,128)} %bitcast.12, f32[10,768]{1,0:T(8,128)} %modes_hbm.1, bf16[384,512]{1,0:T(8,128)(2,1)} %constant.44.clone.pack_hbm.pack_ref), custom_call_target="tpu_custom_call" | custom-call | tf_op jit(solution)/shard_map/start/pallas_call | solution.py:673
  4.0 0.0 copy-start.4
  4.1 0.0 copy-start.9
  4.1 7.3 %all-to-all-start = ((f32[32,48,128]{2,1,0:T(8,128)}), f32[32,48,128]{2,1,0:T(8,128)S(1)}, u32[]{:S(2)}, u32[]{:S(2)}) async-start(f32[32,48,128]{2,1,0:T(8,128)} %start.1), calls=%async_computation | async-start | bytes 1572864 | tf_op jit(solution)/shard_map/all_to_all | solution.py:640
  11.4 0.0 copy-start.3
  11.4 0.0 copy-start.5
  11.4 0.1 split.1
  11.6 19.4 %all-to-all-done = f32[32,48,128]{2,1,0:T(8,128)S(1)} async-done(((f32[32,48,128]{2,1,0:T(8,128)}), f32[32,48,128]{2,1,0:T(8,128)S(1)}, u32[]{:S(2)}, u32[]{:S(2)}) %all-to-all-start) | async-done | bytes 786464 | tf_op jit(solution)/shard_map/all_to_all | solution.py:640
  31.0 2.9 %collective-permute-start = (f32[32,768]{1,0:T(8,128)S(1)}, f32[32,768]{1,0:T(8,128)S(1)}, u32[]{:S(2)}, u32[]{:S(2)}) collective-permute-start(f32[32,768]{1,0:T(8,128)S(1)} %get-tuple-element.38), channel_id=1, source_target_pairs={{0,1},{1,2},{2,3},{3,0},{4,5},{5,6},{6,7},{7,4},{8,9},{9,10},{10,1... | collective-permute-start | bytes 294920 | tf_op jit(solution)/shard_map/ppermute | solution.py:644
  33.9 0.7 collective-permute-start.1
  34.7 1.7 %collective-permute-start.2 = (f32[32,768]{1,0:T(8,128)S(1)}, f32[32,768]{1,0:T(8,128)S(1)}, u32[]{:S(2)}, u32[]{:S(2)}) collective-permute-start(f32[32,768]{1,0:T(8,128)S(1)} %get-tuple-element.40), channel_id=1, source_target_pairs={{0,3},{1,0},{2,1},{3,2},{4,7},{5,4},{6,5},{7,6},{8,11},{9,8},{10,9... | collective-permute-start | bytes 294920 | tf_op jit(solution)/shard_map/ppermute | solution.py:644
  36.3 0.2 fusion.nodes_ref
  36.6 7.8 %mix.2 = (f32[32,24,128]{2,1,0:T(8,128)}, f32[11,8,128]{2,1,0:T(8,128)S(1)}) custom-call(s32[726]{0:T(1024)S(1)} %fusion.nodes_ref, s32[660]{0:T(1024)S(1)} %copy-done.10, f32[1536,128]{1,0:T(8,128)S(1)} %bitcast.8, bf16[4,128,128]{2,1,0:T(8,128)(2,1)S(1)} %copy-done.9, bf16[512,512]{1,0:T(8,128)(2,1)S(1)} %copy-done.4, bf16[256,384]{1,0:T(8,128)(2,1)S(1)} %copy-done.3, ...), custom_call_target="tpu_custom_call" | custom-call | tf_op jit(solution)/shard_map/mix/pallas_call | solution.py:705
  44.4 2.7 %all-to-all-start.1 = ((f32[32,24,128]{2,1,0:T(8,128)}), f32[32,24,128]{2,1,0:T(8,128)S(1)}, u32[]{:S(2)}, u32[]{:S(2)}) async-start(f32[32,24,128]{2,1,0:T(8,128)} %get-tuple-element.43), calls=%async_computation.1 | async-start | bytes 786432 | tf_op jit(solution)/shard_map/all_to_all | solution.py:640
  47.2 0.1 dynamic-slice_convert_fusion
  47.3 0.1 dynamic_slice.7
  47.3 0.6 load.1
  48.0 11.0 %all-to-all-done.1.image_ref = f32[32,24,128]{2,1,0:T(8,128)S(1)} async-done(((f32[32,24,128]{2,1,0:T(8,128)}), f32[32,24,128]{2,1,0:T(8,128)S(1)}, u32[]{:S(2)}, u32[]{:S(2)}) %all-to-all-start.1) | async-done | bytes 393248 | tf_op jit(solution)/shard_map/all_to_all | solution.py:640
  59.0 0.1 broadcast_in_dim.26.live_ref
  59.1 4.6 %middle.1 = (f32[32,48,128]{2,1,0:T(8,128)S(1)}, f32[24,3,16,128]{3,2,1,0:T(8,128)S(1)}, f32[25,3,16,128]{3,2,1,0:T(8,128)S(1)}) custom-call(f32[32,24,128]{2,1,0:T(8,128)S(1)} %all-to-all-done.1.image_ref, f32[24,3,16,128]{3,2,1,0:T(8,128)S(1)} %get-tuple-element.48.base_ref, f32[16,128]{1,0:T(8,128)S(1)} %broadcast_in_dim.26.live_ref, ...), custom_call_target="tpu_custom_call" | custom-call | tf_op jit(solution)/shard_map/middle/pallas_call | solution.py:720
  63.6 23.3 %all_to_all.20.msg_ref = f32[32,48,128]{2,1,0:T(8,128)S(1)} all-to-all(f32[32,48,128]{2,1,0:T(8,128)S(1)} %get-tuple-element.50), channel_id=1, replica_groups=mesh['chaos'=8,'slab'=4] {'chaos','slab'}, dimensions={0} | all-to-all | bytes 1572864 | tf_op jit(solution)/shard_map/all_to_all | solution.py:640
  86.9 5.0 %mix.3 = f32[32,24,128]{2,1,0:T(8,128)S(1)} custom-call(s32[726]{0:T(1024)S(1)} %fusion.nodes_ref, s32[660]{0:T(1024)S(1)} %copy-done.10, f32[32,48,128]{2,1,0:T(8,128)S(1)} %all_to_all.20.msg_ref, f32[11,8,128]{2,1,0:T(8,128)S(1)} %get-tuple-element.51.mods_ref, bf16[256,384]{1,0:T(8,128)(2,1)S(1)} %copy-done.3, bf16[384,128]{1,0:T(8,128)(2,1)S(1)} %copy-done.5), custom_call_target="tpu_custom_call" | custom-call | tf_op jit(solution)/shard_map/mix/pallas_call | solution.py:728
  91.9 16.0 %all_to_all.21.image_ref = f32[32,24,128]{2,1,0:T(8,128)S(1)} all-to-all(f32[32,24,128]{2,1,0:T(8,128)S(1)} %mix.3), channel_id=1, replica_groups=mesh['chaos'=8,'slab'=4] {'chaos','slab'}, dimensions={0} | all-to-all | bytes 786432 | tf_op jit(solution)/shard_map/all_to_all | solution.py:640
  107.9 4.0 %end.1 = (f32[56,768]{1,0:T(8,128)S(1)}, f32[56,768]{1,0:T(8,128)S(1)}, f32[56,768]{1,0:T(8,128)S(1)}, f32[56,768]{1,0:T(8,128)S(1)}) custom-call(f32[32,24,128]{2,1,0:T(8,128)S(1)} %all_to_all.21.image_ref, f32[24,3,16,128]{3,2,1,0:T(8,128)S(1)} %get-tuple-element.52.base_ref, f32[16,128]{1,0:T(8,128)S(1)} %broadcast_in_dim.26.live_ref, ...), custom_call_target="tpu_custom_call" | custom-call | tf_op jit(solution)/shard_map/end/pallas_call | solution.py:732
  111.9 2.3 %collective-permute-start.3 = (f32[56,768]{1,0:T(8,128)S(1)}, f32[56,768]{1,0:T(8,128)S(1)}, u32[]{:S(2)}, u32[]{:S(2)}) collective-permute-start(f32[56,768]{1,0:T(8,128)S(1)} %get-tuple-element.55), channel_id=1, source_target_pairs={{0,1},{1,2},{2,3},{3,0},{4,5},{5,6},{6,7},{7,4},{8,9},{9,10},{10,1... | collective-permute-start | bytes 516104 | tf_op jit(solution)/shard_map/ppermute | solution.py:644
  114.2 0.9 collective-permute-start.4
  115.1 1.5 %collective-permute-start.5 = (f32[56,768]{1,0:T(8,128)S(1)}, f32[56,768]{1,0:T(8,128)S(1)}, u32[]{:S(2)}, u32[]{:S(2)}) collective-permute-start(f32[56,768]{1,0:T(8,128)S(1)} %get-tuple-element.57), channel_id=1, source_target_pairs={{0,3},{1,0},{2,1},{3,2},{4,7},{5,4},{6,5},{7,6},{8,11},{9,8},{10,9... | collective-permute-start | bytes 516104 | tf_op jit(solution)/shard_map/ppermute | solution.py:644
  116.7 0.1 fusion.1
  116.8 0.1 copy.19.live_ref
  116.9 4.2 %collective-permute-done.3.refs_1_ = f32[56,768]{1,0:T(8,128)S(1)} collective-permute-done((f32[56,768]{1,0:T(8,128)S(1)}, f32[56,768]{1,0:T(8,128)S(1)}, u32[]{:S(2)}, u32[]{:S(2)}) %collective-permute-start.3) | collective-permute-done | bytes 172064 | tf_op jit(solution)/shard_map/ppermute | solution.py:644
  121.0 7.6 %collective-permute-done.4.refs_2_ = f32[56,768]{1,0:T(8,128)S(1)} collective-permute-done((f32[56,768]{1,0:T(8,128)S(1)}, f32[56,768]{1,0:T(8,128)S(1)}, u32[]{:S(2)}, u32[]{:S(2)}) %collective-permute-start.4) | collective-permute-done | bytes 172064 | tf_op jit(solution)/shard_map/ppermute | solution.py:644
  128.6 1.1 finish.1
  (31 shorter events, 0.1 us)
Async XLA Ops:
  4.0 7.4 %copy-start.11 = (f32[768]{0:T(1024)S(1)}, f32[768]{0:T(1024)}, u32[]{:S(2)}) copy-start(f32[768]{0:T(1024)} %param.18) | copy-start | bytes 9220
  4.0 7.4 %copy-start.6 = (f32[36,3,768]{2,0,1:T(8,128)S(1)}, f32[36,3,768]{2,0,1:T(8,128)}, u32[]{:S(2)}) copy-start(f32[36,3,768]{2,0,1:T(8,128)} %param.17) | copy-start | bytes 995332
  4.0 32.5 %copy-start.4 = (bf16[512,512]{1,0:T(8,128)(2,1)S(1)}, bf16[512,512]{1,0:T(8,128)(2,1)}, u32[]{:S(2)}) copy-start(bf16[512,512]{1,0:T(8,128)(2,1)} %constant.52.clone.regroup_ref) | copy-start | bytes 1572868
  4.1 32.5 %copy-start.9 = (bf16[4,128,128]{2,1,0:T(8,128)(2,1)S(1)}, bf16[4,128,128]{2,1,0:T(8,128)(2,1)}, u32[]{:S(2)}) copy-start(bf16[4,128,128]{2,1,0:T(8,128)(2,1)} %constant.46.clone.mtab_ref) | copy-start | bytes 393220
  4.1 26.9 %all-to-all-start = ((f32[32,48,128]{2,1,0:T(8,128)}), f32[32,48,128]{2,1,0:T(8,128)S(1)}, u32[]{:S(2)}, u32[]{:S(2)}) async-start(f32[32,48,128]{2,1,0:T(8,128)} %start.1), calls=%async_computation | async-start | bytes 1572864 | tf_op jit(solution)/shard_map/all_to_all | solution.py:640
  11.4 25.1 %copy-start.3 = (bf16[256,384]{1,0:T(8,128)(2,1)S(1)}, bf16[256,384]{1,0:T(8,128)(2,1)}, u32[]{:S(2)}) copy-start(bf16[256,384]{1,0:T(8,128)(2,1)} %constant.49.clone.grad_ref) | copy-start | bytes 589828
  11.4 25.1 %copy-start.5 = (bf16[384,128]{1,0:T(8,128)(2,1)S(1)}, bf16[384,128]{1,0:T(8,128)(2,1)}, u32[]{:S(2)}) copy-start(bf16[384,128]{1,0:T(8,128)(2,1)} %constant.50.clone.div_ref) | copy-start | bytes 294916
  11.5 24.8 %copy-start.13 = (s32[726]{0:T(1024)S(1)}, s32[726]{0:T(1024)}, u32[]{:S(2)}) copy-start(s32[726]{0:T(1024)} %constant.57) | copy-start | bytes 8716
  31.0 5.4 %copy-start.12 = (s32[288]{0:T(512)S(1)}, s32[288]{0:T(512)}, u32[]{:S(2)}) copy-start(s32[288]{0:T(512)} %param.20) | copy-start | bytes 3460
  31.0 5.6 %copy-start.10 = (s32[660]{0:T(1024)S(1)}, s32[660]{0:T(1024)}, u32[]{:S(2)}) copy-start(s32[660]{0:T(1024)} %constant.51.clone.level_ref) | copy-start | bytes 7924
  31.0 13.3 %collective-permute-start = (f32[32,768]{1,0:T(8,128)S(1)}, f32[32,768]{1,0:T(8,128)S(1)}, u32[]{:S(2)}, u32[]{:S(2)}) collective-permute-start(f32[32,768]{1,0:T(8,128)S(1)} %get-tuple-element.38), channel_id=1, source_target_pairs={{0,1},{1,2},{2,3},{3,0},{4,5},{5,6},{6,7},{7,4},{8,9},{9,10},{10,1... | collective-permute-start | bytes 294920 | tf_op jit(solution)/shard_map/ppermute | solution.py:644
  33.9 10.4 %collective-permute-start.1 = (f32[32,768]{1,0:T(8,128)S(1)}, f32[32,768]{1,0:T(8,128)S(1)}, u32[]{:S(2)}, u32[]{:S(2)}) collective-permute-start(f32[32,768]{1,0:T(8,128)S(1)} %get-tuple-element.39), channel_id=1, source_target_pairs={{0,2},{1,3},{2,0},{3,1},{4,6},{5,7},{6,4},{7,5},{8,10},{9,11},{10,... | collective-permute-start | bytes 294920 | tf_op jit(solution)/shard_map/ppermute | solution.py:644
  34.7 9.7 %collective-permute-start.2 = (f32[32,768]{1,0:T(8,128)S(1)}, f32[32,768]{1,0:T(8,128)S(1)}, u32[]{:S(2)}, u32[]{:S(2)}) collective-permute-start(f32[32,768]{1,0:T(8,128)S(1)} %get-tuple-element.40), channel_id=1, source_target_pairs={{0,3},{1,0},{2,1},{3,2},{4,7},{5,4},{6,5},{7,6},{8,11},{9,8},{10,9... | collective-permute-start | bytes 294920 | tf_op jit(solution)/shard_map/ppermute | solution.py:644
  44.3 14.7 %copy-start = (bf16[512,512]{1,0:T(8,128)(2,1)S(1)}, bf16[512,512]{1,0:T(8,128)(2,1)}, u32[]{:S(2)}) copy-start(bf16[512,512]{1,0:T(8,128)(2,1)} %constant.45.clone.unpack_ref) | copy-start | bytes 1572868
  44.4 14.7 %copy-start.7 = (bf16[128,256]{1,0:T(8,128)(2,1)S(1)}, bf16[128,256]{1,0:T(8,128)(2,1)}, u32[]{:S(2)}) copy-start(bf16[128,256]{1,0:T(8,128)(2,1)} %constant.47.clone.slope_ref) | copy-start | bytes 196612
  44.4 14.7 %copy-start.8 = (bf16[256,128]{1,0:T(8,128)(2,1)S(1)}, bf16[256,128]{1,0:T(8,128)(2,1)}, u32[]{:S(2)}) copy-start(bf16[256,128]{1,0:T(8,128)(2,1)} %constant.48.clone.back_ref) | copy-start | bytes 196612
  44.4 14.6 %all-to-all-start.1 = ((f32[32,24,128]{2,1,0:T(8,128)}), f32[32,24,128]{2,1,0:T(8,128)S(1)}, u32[]{:S(2)}, u32[]{:S(2)}) async-start(f32[32,24,128]{2,1,0:T(8,128)} %get-tuple-element.43), calls=%async_computation.1 | async-start | bytes 786432 | tf_op jit(solution)/shard_map/all_to_all | solution.py:640
  47.1 11.9 %copy-start.1 = (bf16[384,512]{1,0:T(8,128)(2,1)S(1)}, bf16[384,512]{1,0:T(8,128)(2,1)}, u32[]{:S(2)}) copy-start(bf16[384,512]{1,0:T(8,128)(2,1)} %constant.44.clone.pack_hbm.pack_ref) | copy-start | bytes 1179652
  107.9 20.7 %copy-start.2 = (f32[36,3,768]{2,0,1:T(8,128)S(1)}, f32[36,3,768]{2,0,1:T(8,128)}, u32[]{:S(2)}) copy-start(f32[36,3,768]{2,0,1:T(8,128)} %param.16) | copy-start | bytes 995332
  111.9 9.1 %collective-permute-start.3 = (f32[56,768]{1,0:T(8,128)S(1)}, f32[56,768]{1,0:T(8,128)S(1)}, u32[]{:S(2)}, u32[]{:S(2)}) collective-permute-start(f32[56,768]{1,0:T(8,128)S(1)} %get-tuple-element.55), channel_id=1, source_target_pairs={{0,1},{1,2},{2,3},{3,0},{4,5},{5,6},{6,7},{7,4},{8,9},{9,10},{10,1... | collective-permute-start | bytes 516104 | tf_op jit(solution)/shard_map/ppermute | solution.py:644
  114.2 14.4 %collective-permute-start.4 = (f32[56,768]{1,0:T(8,128)S(1)}, f32[56,768]{1,0:T(8,128)S(1)}, u32[]{:S(2)}, u32[]{:S(2)}) collective-permute-start(f32[56,768]{1,0:T(8,128)S(1)} %get-tuple-element.56), channel_id=1, source_target_pairs={{0,2},{1,3},{2,0},{3,1},{4,6},{5,7},{6,4},{7,5},{8,10},{9,11},{10,... | collective-permute-start | bytes 516104 | tf_op jit(solution)/shard_map/ppermute | solution.py:644
  115.1 13.5 %collective-permute-start.5 = (f32[56,768]{1,0:T(8,128)S(1)}, f32[56,768]{1,0:T(8,128)S(1)}, u32[]{:S(2)}, u32[]{:S(2)}) collective-permute-start(f32[56,768]{1,0:T(8,128)S(1)} %get-tuple-element.57), channel_id=1, source_target_pairs={{0,3},{1,0},{2,1},{3,2},{4,7},{5,4},{6,5},{7,6},{8,11},{9,8},{10,9... | collective-permute-start | bytes 516104 | tf_op jit(solution)/shard_map/ppermute | solution.py:644
